TPU v7x, 32 devices: a whole 2x2x4 slice. The times are simulated.
32 devices in a mesh: rows: 8 (over y, x, core), tp: 4 (over z).
Axes of the slice: x: 2, y: 2, z: 4, core: 2. Of those that a mesh axis runs over, the one named last changes fastest.
Arguments:
- tokens: bfloat16 [16, 1024, 1024], P('rows', 'tp'), may hold values from -6 to 6
- w_query: bfloat16 [1024, 1024], P('rows', 'tp'), may hold values from -0.1875 to 0.1875
- w_key: bfloat16 [1024, 1024], P('rows', 'tp'), may hold values from -0.1875 to 0.1875
- w_value: bfloat16 [1024, 1024], P('rows', 'tp'), may hold values from -0.1875 to 0.1875
- w_attn_out: bfloat16 [1024, 1024], P('tp', 'rows'), may hold values from -0.75 to 0.75
- w_up: bfloat16 [1024, 4096], P('rows', 'tp'), may hold values from -0.1875 to 0.1875
- w_down: bfloat16 [4096, 1024], P('tp', 'rows'), may hold values from -0.09375 to 0.09375
- first_gain: float32 [1024], replicated, may hold values from 0.5 to 1.5
- first_shift: float32 [1024], replicated, may hold values from -3 to 3
- second_gain: float32 [1024], replicated, may hold values from 0.5 to 1.5
- second_shift: float32 [1024], replicated, may hold values from -3 to 3
- prefix_keys: bfloat16 [4, 100, 1024], P(None, None, 'tp'), may hold values from -6 to 6
- prefix_values: bfloat16 [4, 100, 1024], P(None, None, 'tp'), may hold values from -6 to 6
- example_lengths: int32 [16, 8], P('rows'), may hold values from 1 to 512, 1024 in all within a row
- task_ids: int32 [16], P('rows'), may hold values from 0 to 3
- prefix_lens: int32 [4], replicated, may hold values from 20 to 100, as said below
- slot_masks: int32 [4, 100], replicated, may hold values 0 or 1
- out_grad: bfloat16 [16, 1024, 1024], P('rows', 'tp'), may hold values from -6 to 6
Outputs:
- output: bfloat16 [16, 1024, 1024], P('rows', 'tp')
- tokens_grad: float32 [16, 1024, 1024], P('rows', 'tp')
- prefix_keys_grad: float32 [4, 100, 1024], P(None, None, 'tp')
- prefix_values_grad: float32 [4, 100, 1024], P(None, None, 'tp')
Inputs may be any that keep to these rules, and one draw needn't show every extreme that they name: `prefix_lens`: each of 20, 64 and 100 is the prefix length of some task, and no other value occurs. `example_lengths`: the 8 lengths of a row sum to 1024.
All inputs are finite; a program needn't handle non-finite values.
Results may differ from a plain program's by a relative error of at most 0.014.
Values may be sent and summed in bfloat16 or wider, within the bound.
A program may use at most 192 MiB of HBM per device.

v0:
```python
import jax
import jax.numpy as jnp
from jax import lax
from jax.sharding import PartitionSpec as P

HD = 64
MICRO = 2


highest = lax.Precision.HIGHEST


def layer_norm(z, gain, shift):
    mean = jnp.mean(z, axis=-1, keepdims=True)
    centred = z - mean
    spread = jnp.mean(centred * centred, axis=-1, keepdims=True)
    return centred * lax.rsqrt(spread + 1e-05) * gain + shift


def gelu_exact(v):
    return jax.nn.gelu(v, approximate=False)


def split_heads(a):
    return a.reshape(a.shape[0], a.shape[1], a.shape[2] // HD, HD)


def row_tables(lengths, tasks, prefix_lens, slot_masks, length):
    ends = jnp.cumsum(lengths, axis=1)
    places = jnp.arange(length, dtype=jnp.int32)
    segment = jnp.sum((places[None, :, None] >= ends[:, None, :]).astype(jnp.int32), axis=-1)
    slots = jnp.arange(slot_masks.shape[1], dtype=jnp.int32)
    valid_table = ((slots[None, :] < prefix_lens[:, None]) & (slot_masks == 1)).astype(jnp.float32)
    onehot = (tasks[:, None] == jnp.arange(prefix_lens.shape[0], dtype=jnp.int32)[None, :]).astype(
        jnp.float32
    )
    valid_rows = jnp.dot(onehot, valid_table, precision=highest) > 0.5
    return (segment, onehot, valid_rows)


def rounded_product(matrix, piece):
    return jnp.einsum("rnd,de->rne", piece, matrix, preferred_element_type=jnp.float32).astype(
        jnp.bfloat16
    )


def plain_product(matrix, piece):
    return jnp.einsum("rnd,de->rne", piece, matrix, preferred_element_type=jnp.float32)


def block_scores(q_block, keys, pre_keys, seg_block, segment, valid_rows):
    seq = jnp.einsum("rqhd,rkhd->rhqk", q_block, keys, preferred_element_type=jnp.float32) * 0.125
    pre = (
        jnp.einsum("rqhd,rphd->rhqp", q_block, pre_keys, preferred_element_type=jnp.float32) * 0.125
    )
    same = seg_block[:, None, :, None] == segment[:, None, None, :]
    seq = jnp.where(same, seq, -1e30)
    pre = jnp.where(valid_rows[:, None, None, :], pre, -1e30)
    return (seq, pre)


def attend_forward(qkv, pre_keys, pre_values, segment, valid_rows):
    width = qkv.shape[2] // 3
    count = qkv.shape[0]
    length = qkv.shape[1]
    query = split_heads(qkv[:, :, :width])
    keys = split_heads(qkv[:, :, width : 2 * width])
    values = split_heads(qkv[:, :, 2 * width :])
    block = min(512, length)
    outputs = []
    totals = []
    for first in range(0, length, block):
        seq, pre = block_scores(
            query[:, first : first + block],
            keys,
            pre_keys,
            segment[:, first : first + block],
            segment,
            valid_rows,
        )
        top = jnp.maximum(jnp.max(seq, axis=-1), jnp.max(pre, axis=-1))
        summed = jnp.sum(jnp.exp(seq - top[..., None]), axis=-1) + jnp.sum(
            jnp.exp(pre - top[..., None]), axis=-1
        )
        log_total = top + jnp.log(summed)
        p_seq = jnp.exp(seq - log_total[..., None]).astype(jnp.bfloat16)
        p_pre = jnp.exp(pre - log_total[..., None]).astype(jnp.bfloat16)
        mixed = jnp.einsum("rhqk,rkhd->rqhd", p_seq, values, preferred_element_type=jnp.float32)
        mixed = mixed + jnp.einsum(
            "rhqp,rphd->rqhd", p_pre, pre_values, preferred_element_type=jnp.float32
        )
        outputs.append(mixed.astype(jnp.bfloat16))
        totals.append(log_total)
    attended = jnp.concatenate(outputs, axis=1).reshape(count, length, width)
    return (attended, jnp.concatenate(totals, axis=2))


def attend_backward(qkv, pre_keys, pre_values, segment, valid_rows, log_totals, d_attended):
    width = qkv.shape[2] // 3
    count = qkv.shape[0]
    length = qkv.shape[1]
    query = split_heads(qkv[:, :, :width])
    keys = split_heads(qkv[:, :, width : 2 * width])
    values = split_heads(qkv[:, :, 2 * width :])
    d_out = split_heads(d_attended)
    block = min(512, length)
    d_query_parts = []
    d_keys = jnp.zeros(keys.shape, jnp.float32)
    d_values = jnp.zeros(values.shape, jnp.float32)
    d_pre_keys = jnp.zeros(pre_keys.shape, jnp.float32)
    d_pre_values = jnp.zeros(pre_values.shape, jnp.float32)
    for first in range(0, length, block):
        q_block = query[:, first : first + block]
        d_block = d_out[:, first : first + block]
        seq, pre = block_scores(
            q_block, keys, pre_keys, segment[:, first : first + block], segment, valid_rows
        )
        log_total = log_totals[:, :, first : first + block][..., None]
        p_seq = jnp.exp(seq - log_total)
        p_pre = jnp.exp(pre - log_total)
        dp_seq = jnp.einsum("rqhd,rkhd->rhqk", d_block, values, preferred_element_type=jnp.float32)
        dp_pre = jnp.einsum(
            "rqhd,rphd->rhqp", d_block, pre_values, preferred_element_type=jnp.float32
        )
        inner = jnp.sum(p_seq * dp_seq, axis=-1) + jnp.sum(p_pre * dp_pre, axis=-1)
        ds_seq = (p_seq * (dp_seq - inner[..., None])).astype(jnp.bfloat16)
        ds_pre = (p_pre * (dp_pre - inner[..., None])).astype(jnp.bfloat16)
        d_query = jnp.einsum("rhqk,rkhd->rqhd", ds_seq, keys, preferred_element_type=jnp.float32)
        d_query = d_query + jnp.einsum(
            "rhqp,rphd->rqhd", ds_pre, pre_keys, preferred_element_type=jnp.float32
        )
        d_query_parts.append((0.125 * d_query).astype(jnp.bfloat16))
        d_keys = d_keys + 0.125 * jnp.einsum(
            "rhqk,rqhd->rkhd", ds_seq, q_block, preferred_element_type=jnp.float32
        )
        d_values = d_values + jnp.einsum(
            "rhqk,rqhd->rkhd",
            p_seq.astype(jnp.bfloat16),
            d_block,
            preferred_element_type=jnp.float32,
        )
        d_pre_keys = d_pre_keys + 0.125 * jnp.einsum(
            "rhqp,rqhd->rphd", ds_pre, q_block, preferred_element_type=jnp.float32
        )
        d_pre_values = d_pre_values + jnp.einsum(
            "rhqp,rqhd->rphd",
            p_pre.astype(jnp.bfloat16),
            d_block,
            preferred_element_type=jnp.float32,
        )
    grads_qkv = jnp.concatenate(
        [
            jnp.concatenate(d_query_parts, axis=1).reshape(count, length, width),
            d_keys.astype(jnp.bfloat16).reshape(count, length, width),
            d_values.astype(jnp.bfloat16).reshape(count, length, width),
        ],
        axis=2,
    )
    slots = pre_keys.shape[1]
    return (
        grads_qkv,
        d_pre_keys.reshape(count, slots, width),
        d_pre_values.reshape(count, slots, width),
    )


def shards(
    tokens,
    w_query,
    w_key,
    w_value,
    w_attn_out,
    w_up,
    w_down,
    first_gain,
    first_shift,
    second_gain,
    second_shift,
    prefix_keys,
    prefix_values,
    example_lengths,
    task_ids,
    prefix_lens,
    slot_masks,
    out_grad,
):
    per_batch = tokens.shape[0] // MICRO
    places_own = tokens.shape[1]
    length = places_own * lax.axis_size("tp")
    segment_all, onehot_all, valid_all = row_tables(
        example_lengths, task_ids, prefix_lens, slot_masks, length
    )

    def task_rows(onehot):
        picker = onehot.astype(jnp.bfloat16)
        pre_keys = jnp.einsum(
            "rt,tpe->rpe", picker, prefix_keys, preferred_element_type=jnp.float32
        ).astype(jnp.bfloat16)
        pre_values = jnp.einsum(
            "rt,tpe->rpe", picker, prefix_values, preferred_element_type=jnp.float32
        ).astype(jnp.bfloat16)
        return (split_heads(pre_keys), split_heads(pre_values))

    kept = []
    outputs = []
    for batch in range(MICRO):
        low_row = batch * per_batch
        token_part = tokens[low_row : low_row + per_batch]
        segment = segment_all[low_row : low_row + per_batch]
        valid_rows = valid_all[low_row : low_row + per_batch]
        pre_keys, pre_values = task_rows(onehot_all[low_row : low_row + per_batch])
        weights = (
            lax.all_gather(w_query, "rows", axis=0, tiled=True),
            lax.all_gather(w_key, "rows", axis=0, tiled=True),
            lax.all_gather(w_value, "rows", axis=0, tiled=True),
            lax.all_gather(w_up, "rows", axis=0, tiled=True),
            lax.all_gather(w_attn_out, "rows", axis=1, tiled=True),
            lax.all_gather(w_down, "rows", axis=1, tiled=True),
        )
        w_joint = jnp.concatenate(weights[:3], axis=1)
        qkv = rounded_product(w_joint, lax.all_gather(token_part, "tp", axis=1, tiled=True))
        attended, log_totals = attend_forward(qkv, pre_keys, pre_values, segment, valid_rows)
        attn_terms = jnp.einsum(
            "rne,ed->rnd", attended, weights[4], preferred_element_type=jnp.float32
        )
        first_sum = token_part.astype(jnp.float32) + lax.psum_scatter(
            attn_terms, "tp", scatter_dimension=1, tiled=True
        )
        normed = layer_norm(first_sum, first_gain, first_shift).astype(jnp.bfloat16)
        upper = plain_product(weights[3], lax.all_gather(normed, "tp", axis=1, tiled=True))
        acted = gelu_exact(upper).astype(jnp.bfloat16)
        down_terms = jnp.einsum(
            "rnf,fd->rnd", acted, weights[5], preferred_element_type=jnp.float32
        )
        second_sum = normed.astype(jnp.float32) + lax.psum_scatter(
            down_terms, "tp", scatter_dimension=1, tiled=True
        )
        outputs.append(layer_norm(second_sum, second_gain, second_shift).astype(jnp.bfloat16))
        stash = None
        kept.append((first_sum, second_sum, log_totals, stash))

    def norm_two(z):
        return layer_norm(z, second_gain, second_shift)

    def norm_one(z):
        return layer_norm(z, first_gain, first_shift)

    key_total = jnp.zeros(prefix_keys.shape, jnp.float32)
    value_total = jnp.zeros(prefix_values.shape, jnp.float32)
    grads = []
    for batch in range(MICRO):
        low_row = batch * per_batch
        first_sum, second_sum, log_totals, stash = kept[batch]
        segment = segment_all[low_row : low_row + per_batch]
        valid_rows = valid_all[low_row : low_row + per_batch]
        onehot = onehot_all[low_row : low_row + per_batch]
        pre_keys, pre_values = task_rows(onehot)
        weights = (
            lax.all_gather(w_query, "rows", axis=0, tiled=True),
            lax.all_gather(w_key, "rows", axis=0, tiled=True),
            lax.all_gather(w_value, "rows", axis=0, tiled=True),
            lax.all_gather(w_up, "rows", axis=0, tiled=True),
            lax.all_gather(w_attn_out, "rows", axis=1, tiled=True),
            lax.all_gather(w_down, "rows", axis=1, tiled=True),
        )
        cotangent = out_grad[low_row : low_row + per_batch].astype(jnp.float32)
        d_second = jax.vjp(norm_two, second_sum)[1](cotangent)[0]
        w_joint = jnp.concatenate(weights[:3], axis=1)
        token_part = tokens[low_row : low_row + per_batch]
        qkv = rounded_product(w_joint, lax.all_gather(token_part, "tp", axis=1, tiled=True))
        normed = layer_norm(first_sum, first_gain, first_shift).astype(jnp.bfloat16)
        upper = plain_product(weights[3], lax.all_gather(normed, "tp", axis=1, tiled=True))
        d_acted = plain_product(
            weights[5].T, lax.all_gather(d_second.astype(jnp.bfloat16), "tp", axis=1, tiled=True)
        )
        d_upper = jax.vjp(gelu_exact, upper)[1](d_acted)[0].astype(jnp.bfloat16)
        up_terms = jnp.einsum(
            "rnf,df->rnd", d_upper, weights[3], preferred_element_type=jnp.float32
        )
        d_normed = d_second + lax.psum_scatter(up_terms, "tp", scatter_dimension=1, tiled=True)
        d_first = jax.vjp(norm_one, first_sum)[1](d_normed)[0]
        d_attended = rounded_product(
            weights[4].T, lax.all_gather(d_first.astype(jnp.bfloat16), "tp", axis=1, tiled=True)
        )
        grads_qkv, d_pre_keys, d_pre_values = attend_backward(
            qkv, pre_keys, pre_values, segment, valid_rows, log_totals, d_attended
        )
        in_terms = jnp.einsum("rne,de->rnd", grads_qkv, w_joint, preferred_element_type=jnp.float32)
        grads.append(
            d_first
            + lax.psum_scatter(
                in_terms.astype(jnp.bfloat16), "tp", scatter_dimension=1, tiled=True
            ).astype(jnp.float32)
        )
        key_total = key_total + jnp.einsum("rt,rpe->tpe", onehot, d_pre_keys, precision=highest)
        value_total = value_total + jnp.einsum(
            "rt,rpe->tpe", onehot, d_pre_values, precision=highest
        )
    keys_grad, values_grad = (
        lax.psum(key_total.astype(jnp.bfloat16), "rows").astype(jnp.float32),
        lax.psum(value_total.astype(jnp.bfloat16), "rows").astype(jnp.float32),
    )
    return (
        jnp.concatenate(outputs, axis=0),
        jnp.concatenate(grads, axis=0),
        keys_grad,
        values_grad,
    )


def solution(mesh):
    placed = (
        P("rows", "tp", None),
        P("rows", "tp"),
        P("rows", "tp"),
        P("rows", "tp"),
        P("tp", "rows"),
        P("rows", "tp"),
        P("tp", "rows"),
        P(),
        P(),
        P(),
        P(),
        P(None, None, "tp"),
        P(None, None, "tp"),
        P("rows", None),
        P("rows"),
        P(),
        P(),
        P("rows", "tp", None),
    )
    return jax.shard_map(
        shards,
        mesh=mesh,
        in_specs=placed,
        out_specs=(
            P("rows", "tp", None),
            P("rows", "tp", None),
            P(None, None, "tp"),
            P(None, None, "tp"),
        ),
        check_vma=False,
    )
```

profile of v0, /device:TPU:0, one launch (start us, length us, event | category | flops | bytes accessed | tf_op | source)
XLA Modules:
  0.0 1118.7 jit_solution(16416638801324213368)
XLA Ops:
  15.4 11.3 %all_gather.28 = bf16[1024,256]{1,0:T(8,128)(2,1)S(1)} all-gather(bf16[128,256]{1,0:T(8,128)(2,1)S(1)} %copy-done.89), channel_id=1, replica_groups=mesh['rows'=8,'tp'=4] {'rows'}, dimensions={0}, use_global_device_ids=true | all-gather | bytes 589824 | tf_op jit(solution)/shard_map/all_gather | solution.py:213
  26.8 9.8 all_gather.29
  36.6 8.9 all_gather.30
  45.7 10.0 all_gather.32
  82.9 23.6 %all-gather.19.cloned.1.call-done = bf16[1,1024,1024]{2,1,0:T(8,128)(2,1)} async-done(((bf16[1,256,1024]{2,1,0:T(8,128)(2,1)}), bf16[1,1024,1024]{2,1,0:T(8,128)(2,1)}) %all-gather.19.cloned.1.call-update) | async-done | bytes 2097168 | tf_op jit(solution)/shard_map/all_gather | solution.py:221
  128.7 55.7 %reduce-scatter.9.cloned.1.call-done = f32[1,256,1024]{2,1,0:T(8,128)} async-done(((f32[1,1024,1024]{2,1,0:T(8,128)}), f32[1,256,1024]{2,1,0:T(8,128)}) %reduce-scatter.9.cloned.1.call-update) | async-done | bytes 1048592 | tf_op jit(solution)/shard_map/reduce_scatter | solution.py:226
  184.4 79.5 %reduce-scatter.13.cloned.1.call-done = f32[1,256,1024]{2,1,0:T(8,128)} async-done(((f32[1,1024,1024]{2,1,0:T(8,128)}), f32[1,256,1024]{2,1,0:T(8,128)}) %reduce-scatter.13.cloned.1.call-update) | async-done | bytes 1048592 | tf_op jit(solution)/shard_map/reduce_scatter | solution.py:226
  270.9 44.8 %all-gather.13.cloned.1.call-done = bf16[1,1024,1024]{2,1,0:T(8,128)(2,1)} async-done(((bf16[1,256,1024]{2,1,0:T(8,128)(2,1)}), bf16[1,1024,1024]{2,1,0:T(8,128)(2,1)}) %all-gather.13.cloned.1.call-update) | async-done | bytes 2097168 | tf_op jit(solution)/shard_map/all_gather | solution.py:230
  315.6 14.4 %fusion.8 = (f32[1024,1024]{1,0:T(8,128)}, f32[1024,1024]{1,0:T(8,128)}) fusion(bf16[1024,1024]{1,0:T(8,128)(2,1)} %all-gather.15.cloned.1.call-done, bf16[1,1024,1024]{2,1,0:T(8,128)(2,1)} %all-gather.13.cloned.1.call-done), kind=kOutput, calls=%fused_computation.30 | convolution fusion | flops 2212495360 | bytes 12582912 | tf_op jit(solution)/shard_map/rnd,de->rne/dot_general | solution.py:48
  330.0 14.2 %all-gather.17.cloned.1.call-done = bf16[1024,1024]{1,0:T(8,128)(2,1)} async-done(((bf16[1024,128]{1,0:T(8,128)(2,1)}), bf16[1024,1024]{1,0:T(8,128)(2,1)}) %all-gather.17.cloned.1.call-update) | async-done | bytes 2097168 | tf_op jit(solution)/shard_map/all_gather | solution.py:218
  344.2 8.5 convolution_bitcast_fusion.4
  352.8 39.2 %all-gather.21.cloned.1.call-done = bf16[1,1024,1024]{2,1,0:T(8,128)(2,1)} async-done(((bf16[1,256,1024]{2,1,0:T(8,128)(2,1)}), bf16[1,1024,1024]{2,1,0:T(8,128)(2,1)}) %all-gather.21.cloned.1.call-update) | async-done | bytes 2097168 | tf_op jit(solution)/shard_map/all_gather | solution.py:230
  392.0 12.8 %fusion.9 = (f32[1024,1024]{1,0:T(8,128)S(1)}, f32[1024,1024]{1,0:T(8,128)S(1)}) fusion(bf16[1024,1024]{1,0:T(8,128)(2,1)} %all-gather.15.cloned.1.call-done, bf16[1,1024,1024]{2,1,0:T(8,128)(2,1)} %all-gather.21.cloned.1.call-done), kind=kOutput, calls=%fused_computation.31 | convolution fusion | flops 2212495360 | bytes 12582912 | tf_op jit(solution)/shard_map/rnd,de->rne/dot_general | solution.py:48
  412.5 57.4 %reduce-scatter.11.cloned.1.call-done = f32[1,256,1024]{2,1,0:T(8,128)} async-done(((f32[1,1024,1024]{2,1,0:T(8,128)}), f32[1,256,1024]{2,1,0:T(8,128)}) %reduce-scatter.11.cloned.1.call-update) | async-done | bytes 1048592 | tf_op jit(solution)/shard_map/reduce_scatter | solution.py:235
  471.5 78.1 %reduce-scatter.15.cloned.1.call-done = f32[1,256,1024]{2,1,0:T(8,128)} async-done(((f32[1,1024,1024]{2,1,0:T(8,128)}), f32[1,256,1024]{2,1,0:T(8,128)}) %reduce-scatter.15.cloned.1.call-update) | async-done | bytes 1048592 | tf_op jit(solution)/shard_map/reduce_scatter | solution.py:235
  561.0 43.8 %all-gather.23.cloned.1.call-done = bf16[1,1024,1024]{2,1,0:T(8,128)(2,1)} async-done(((bf16[1,256,1024]{2,1,0:T(8,128)(2,1)}), bf16[1,1024,1024]{2,1,0:T(8,128)(2,1)}) %all-gather.23.cloned.1.call-update) | async-done | bytes 2097168 | tf_op jit(solution)/shard_map/all_gather | solution.py:274
  604.8 12.0 %convolution_bitcast_fusion.1 = f32[1,1024,1024]{2,1,0:T(8,128)} fusion(bf16[1024,1024]{1,0:T(8,128)(2,1)} %all-gather.15.cloned.1.call-done, f32[1024,1024]{1,0:T(8,128)} %get-tuple-element.81, f32[1024,1024]{1,0:T(8,128)} %get-tuple-element.82, bf16[1024,1024]{1,0:T(8,128)(2,1)} %all-gather.17.cloned.1.call-done, ...), kind=kOutput, calls=%fused_computation.63 | convolution fusion | flops 4309647360 | bytes 18874368 | tf_op jit(solution)/shard_map/rnf,df->rnd/dot_general | solution.py:277
  616.9 34.1 %all-gather.27.cloned.1.call-done = bf16[1,1024,1024]{2,1,0:T(8,128)(2,1)} async-done(((bf16[1,256,1024]{2,1,0:T(8,128)(2,1)}), bf16[1,1024,1024]{2,1,0:T(8,128)(2,1)}) %all-gather.27.cloned.1.call-update) | async-done | bytes 2097168 | tf_op jit(solution)/shard_map/all_gather | solution.py:274
  650.9 12.0 %convolution_bitcast_fusion = f32[1,1024,1024]{2,1,0:T(8,128)} fusion(bf16[1024,1024]{1,0:T(8,128)(2,1)} %all-gather.15.cloned.1.call-done, f32[1024,1024]{1,0:T(8,128)} %copy-done.110, f32[1024,1024]{1,0:T(8,128)} %copy-done.111, bf16[1024,1024]{1,0:T(8,128)(2,1)} %all-gather.17.cloned.1.call-done, bf16[1,1024,1024]{2,1,0:T(8,128)(2,1)} %all-gather.27.cloned.1.call-done), kind=kOutput, calls=%fused_computation.62 | convolution fusion | flops 4309647360 | bytes 18874368 | tf_op jit(solution)/shard_map/rnf,df->rnd/dot_general | solution.py:277
  663.1 65.7 %reduce-scatter.17.cloned.1.call-done = f32[1,256,1024]{2,1,0:T(8,128)} async-done(((f32[1,1024,1024]{2,1,0:T(8,128)}), f32[1,256,1024]{2,1,0:T(8,128)}) %reduce-scatter.17.cloned.1.call-update) | async-done | bytes 1048592 | tf_op jit(solution)/shard_map/reduce_scatter | solution.py:280
  728.7 79.7 %reduce-scatter.21.cloned.1.call-done = f32[1,256,1024]{2,1,0:T(8,128)} async-done(((f32[1,1024,1024]{2,1,0:T(8,128)}), f32[1,256,1024]{2,1,0:T(8,128)}) %reduce-scatter.21.cloned.1.call-update) | async-done | bytes 1048592 | tf_op jit(solution)/shard_map/reduce_scatter | solution.py:280
  818.6 43.3 %all-gather.29.cloned.1.call-done = bf16[1,1024,1024]{2,1,0:T(8,128)(2,1)} async-done(((bf16[1,256,1024]{2,1,0:T(8,128)(2,1)}), bf16[1,1024,1024]{2,1,0:T(8,128)(2,1)}) %all-gather.29.cloned.1.call-update) | async-done | bytes 2097168 | tf_op jit(solution)/shard_map/all_gather | solution.py:283
  867.0 6.4 fusion.123
  878.6 5.2 multiply_reduce_fusion.1
  883.8 23.9 %all-gather.25.cloned.1.call-done = bf16[1,1024,1024]{2,1,0:T(8,128)(2,1)} async-done(((bf16[1,256,1024]{2,1,0:T(8,128)(2,1)}), bf16[1,1024,1024]{2,1,0:T(8,128)(2,1)}) %all-gather.25.cloned.1.call-update) | async-done | bytes 2097168 | tf_op jit(solution)/shard_map/all_gather | solution.py:283
  910.3 7.6 multiply_reduce_fusion.2
  919.3 5.5 multiply_reduce_fusion.3
  933.5 8.6 multiply_convert_fusion
  969.5 12.6 %multiply_convert_fusion.2 = (bf16[4,512,1024]{2,1,0:T(8,128)(2,1)S(1)}, bf16[4,512,1024]{2,1,0:T(8,128)(2,1)S(1)}) fusion(f32[4,512,1024]{2,1,0:T(8,128)} %get-tuple-element.98, f32[4,512,1024]{2,1,0:T(8,128)} %copy-done.2, f32[4,512]{1,0:T(4,128)S(1)} %add.373, f32[4,512]{1,0:T(4,128)S(1)} %copy-done.84, pred[512,1024]{1,0:T(8,128)(4,1)S(1)} %copy-done.22, ...), kind=kLoop, calls=%fused_computation.4 | loop fusion | flops 25165824 | bytes 43024384 | tf_op jit(solution)/shard_map/convert_element_type | solution.py:126
  997.2 19.3 %all-reduce.3.cloned.1.call-done = (bf16[4,100,256]{2,0,1:T(4,128)(2,1)}, bf16[4,100,256]{2,0,1:T(4,128)(2,1)}) async-done(((bf16[4,100,256]{2,0,1:T(4,128)(2,1)}, bf16[4,100,256]{2,0,1:T(4,128)(2,1)}), (bf16[4,100,256]{2,0,1:T(4,128)(2,1)}, bf16[4,100,256]{2,0,1:T(4,128)(2,1)})) %all-reduce.3.cloned.1.call-update) | async-done | bytes 409616 | tf_op jit(solution)/shard_map/psum | solution.py:300
  1019.9 43.1 %reduce-scatter.23.cloned.1.call-done = bf16[1,256,1024]{2,1,0:T(8,128)(2,1)} async-done(((bf16[1,1024,1024]{2,1,0:T(8,128)(2,1)}), bf16[1,256,1024]{2,1,0:T(8,128)(2,1)}) %reduce-scatter.23.cloned.1.call-update) | async-done | bytes 524304 | tf_op jit(solution)/shard_map/reduce_scatter | solution.py:291
  1064.2 43.8 %reduce-scatter.19.cloned.1.call-done = bf16[1,256,1024]{2,1,0:T(8,128)(2,1)} async-done(((bf16[1,1024,1024]{2,1,0:T(8,128)(2,1)}), bf16[1,256,1024]{2,1,0:T(8,128)(2,1)}) %reduce-scatter.19.cloned.1.call-update) | async-done | bytes 524304 | tf_op jit(solution)/shard_map/reduce_scatter | solution.py:291
  (444 shorter events, 166.0 us)
Async XLA Ops:
  8.1 51.6 %all-gather.11.cloned.1.call-start = ((), (), s32[]{:S(2)}) async-start(), calls=%async_computation.8 | async-start | bytes 2621440 | tf_op jit(solution)/shard_map/all_gather | solution.py:221
  10.5 96.1 %all-gather.19.cloned.1.call-start = ((), (), s32[]{:S(2)}) async-start(), calls=%async_computation.14 | async-start | bytes 2621440 | tf_op jit(solution)/shard_map/all_gather | solution.py:221
  11.3 173.1 %reduce-scatter.9.cloned.1.call-start = ((), (), s32[]{:S(2)}) async-start(), calls=%async_computation.9 | async-start | bytes 5242880 | tf_op jit(solution)/shard_map/reduce_scatter | solution.py:226
  14.0 59.1 %copy-start.73 = (bf16[1,100,256]{1,2,0:T(8,128)(2,1)}, bf16[1,100,256]{1,2,0:T(8,128)(2,1)S(1)}, u32[]{:S(2)}) copy-start(bf16[1,100,256]{1,2,0:T(8,128)(2,1)S(1)} %copy.31) | copy-start | bytes 153604
  55.7 69.6 %copy-start.57 = (bf16[256,1024]{1,0:T(8,128)(2,1)}, bf16[256,1024]{1,0:T(8,128)(2,1)S(1)}, u32[]{:S(2)}) copy-start(bf16[256,1024]{1,0:T(8,128)(2,1)S(1)} %all_gather.32) | copy-start | bytes 1572868
  81.1 182.8 %reduce-scatter.13.cloned.1.call-start = ((), (), s32[]{:S(2)}) async-start(), calls=%async_computation.15 | async-start | bytes 5242880 | tf_op jit(solution)/shard_map/reduce_scatter | solution.py:226
  125.3 138.6 %copy-start.6 = (bf16[2,256,1024]{2,1,0:T(8,128)(2,1)S(1)}, bf16[2,256,1024]{2,1,0:T(8,128)(2,1)}, u32[]{:S(2)}) copy-start(bf16[2,256,1024]{2,1,0:T(8,128)(2,1)} %param.18) | copy-start | bytes 3145732
  128.0 139.9 %copy-start.93 = (f32[1024]{0:T(1024)S(1)}, f32[1024]{0:T(1024)}, u32[]{:S(2)}) copy-start(f32[1024]{0:T(1024)} %param.25) | copy-start | bytes 12292
  128.1 139.9 %copy-start.101 = (f32[1024]{0:T(1024)S(1)}, f32[1024]{0:T(1024)}, u32[]{:S(2)}) copy-start(f32[1024]{0:T(1024)} %param.26) | copy-start | bytes 12292
  128.1 142.8 %all-gather.15.cloned.1.call-start = ((), (), s32[]{:S(2)}) async-start(), calls=%async_computation.11 | async-start | bytes 2359296 | tf_op jit(solution)/shard_map/all_gather | solution.py:216
  128.7 187.0 %all-gather.13.cloned.1.call-start = ((), (), s32[]{:S(2)}) async-start(), calls=%async_computation.10 | async-start | bytes 2621440 | tf_op jit(solution)/shard_map/all_gather | solution.py:230
  184.4 83.6 %copy-start.7 = (f32[1,256,1024]{2,1,0:T(8,128)S(1)}, f32[1,256,1024]{2,1,0:T(8,128)}, u32[]{:S(2)}) copy-start(f32[1,256,1024]{2,1,0:T(8,128)} %reduce-scatter.9.cloned.1.call-done) | copy-start | bytes 3145732
  269.5 74.8 %all-gather.17.cloned.1.call-start = ((), (), s32[]{:S(2)}) async-start(), calls=%async_computation.12 | async-start | bytes 2359296 | tf_op jit(solution)/shard_map/all_gather | solution.py:218
  270.0 122.0 %all-gather.21.cloned.1.call-start = ((), (), s32[]{:S(2)}) async-start(), calls=%async_computation.16 | async-start | bytes 2621440 | tf_op jit(solution)/shard_map/all_gather | solution.py:230
  270.8 199.1 %reduce-scatter.11.cloned.1.call-start = ((), (), s32[]{:S(2)}) async-start(), calls=%async_computation.13 | async-start | bytes 5242880 | tf_op jit(solution)/shard_map/reduce_scatter | solution.py:235
  352.8 196.7 %reduce-scatter.15.cloned.1.call-start = ((), (), s32[]{:S(2)}) async-start(), calls=%async_computation.17 | async-start | bytes 5242880 | tf_op jit(solution)/shard_map/reduce_scatter | solution.py:235
  412.4 138.8 %copy-start.95 = (f32[1024]{0:T(1024)S(1)}, f32[1024]{0:T(1024)}, u32[]{:S(2)}) copy-start(f32[1024]{0:T(1024)} %param.27) | copy-start | bytes 12292
  412.4 141.8 %copy-start.100 = (f32[1024]{0:T(1024)S(1)}, f32[1024]{0:T(1024)}, u32[]{:S(2)}) copy-start(f32[1024]{0:T(1024)} %param.28) | copy-start | bytes 12292
  412.4 192.4 %all-gather.23.cloned.1.call-start = ((), (), s32[]{:S(2)}) async-start(), calls=%async_computation.18 | async-start | bytes 2621440 | tf_op jit(solution)/shard_map/all_gather | solution.py:274
  558.3 92.6 %all-gather.27.cloned.1.call-start = ((), (), s32[]{:S(2)}) async-start(), calls=%async_computation.22 | async-start | bytes 2621440 | tf_op jit(solution)/shard_map/all_gather | solution.py:274
  560.5 168.2 %reduce-scatter.17.cloned.1.call-start = ((), (), s32[]{:S(2)}) async-start(), calls=%async_computation.19 | async-start | bytes 5242880 | tf_op jit(solution)/shard_map/reduce_scatter | solution.py:280
  616.8 191.6 %reduce-scatter.21.cloned.1.call-start = ((), (), s32[]{:S(2)}) async-start(), calls=%async_computation.23 | async-start | bytes 5242880 | tf_op jit(solution)/shard_map/reduce_scatter | solution.py:280
  663.0 198.9 %all-gather.29.cloned.1.call-start = ((), (), s32[]{:S(2)}) async-start(), calls=%async_computation.24 | async-start | bytes 2621440 | tf_op jit(solution)/shard_map/all_gather | solution.py:283
  815.7 92.0 %all-gather.25.cloned.1.call-start = ((), (), s32[]{:S(2)}) async-start(), calls=%async_computation.20 | async-start | bytes 2621440 | tf_op jit(solution)/shard_map/all_gather | solution.py:283
  818.0 198.4 %all-reduce.3.cloned.1.call-start = ((), (), s32[]{:S(2)}) async-start(), calls=%async_computation.26 | async-start | bytes 819200 | tf_op jit(solution)/shard_map/psum | solution.py:300
  964.2 98.9 %reduce-scatter.23.cloned.1.call-start = ((), (), s32[]{:S(2)}) async-start(), calls=%async_computation.25 | async-start | bytes 2621440 | tf_op jit(solution)/shard_map/reduce_scatter | solution.py:291
  969.4 138.7 %reduce-scatter.19.cloned.1.call-start = ((), (), s32[]{:S(2)}) async-start(), calls=%async_computation.21 | async-start | bytes 2621440 | tf_op jit(solution)/shard_map/reduce_scatter | solution.py:291
  996.0 67.0 %copy-start.46 = (f32[1,256,1024]{2,1,0:T(8,128)S(1)}, f32[1,256,1024]{2,1,0:T(8,128)}, u32[]{:S(2)}) copy-start(f32[1,256,1024]{2,1,0:T(8,128)} %copy-done.45) | copy-start | bytes 3145732
  996.0 67.0 %copy-start.97 = (f32[256]{0:T(256)S(1)}, f32[256]{0:T(256)}, u32[]{:S(2)}) copy-start(f32[256]{0:T(256)} %copy-done.96) | copy-start | bytes 3076
  996.0 112.0 %copy-start.44 = (f32[1,256,1024]{2,1,0:T(8,128)S(1)}, f32[1,256,1024]{2,1,0:T(8,128)}, u32[]{:S(2)}) copy-start(f32[1,256,1024]{2,1,0:T(8,128)} %get-tuple-element.19) | copy-start | bytes 3145732
  996.0 112.0 %copy-start.99 = (f32[256]{0:T(256)S(1)}, f32[256]{0:T(256)}, u32[]{:S(2)}) copy-start(f32[256]{0:T(256)} %copy-done.98) | copy-start | bytes 3076
  1018.1 92.6 %copy-start.1 = (bf16[4,100,256]{2,0,1:T(4,128)(2,1)S(1)}, bf16[4,100,256]{2,0,1:T(4,128)(2,1)}, u32[]{:S(2)}) copy-start(bf16[4,100,256]{2,0,1:T(4,128)(2,1)} %param.30) | copy-start | bytes 614404
  (114 other events, 1405.5 us)
Sparse Core Ops, SparseCore 0:
  11.1 48.6 all-gather.10
  61.9 44.6 all-gather.18
  108.9 75.4 reduce-scatter.8
  186.6 77.2 reduce-scatter.12
  558.4 46.3 all-gather.22
  606.3 44.6 all-gather.26
  653.2 75.4 reduce-scatter.16
  731.1 77.2 reduce-scatter.20
Sparse Core Ops, SparseCore 1:
  130.4 26.4 all-gather.14
  269.5 46.0 all-gather.12
  317.4 26.8 all-gather.16
  346.4 45.5 all-gather.20
  394.3 75.5 reduce-scatter.10
  472.3 77.1 reduce-scatter.14
  815.8 46.0 all-gather.28
  863.3 44.3 all-gather.24
  964.2 52.1 all-reduce.2
  1019.3 43.7 reduce-scatter.22
  1065.3 42.7 reduce-scatter.18
where the time goes:
time: 1130 us; the launch traced here: 1120 us
  waiting for transfers between devices  795 us (70%)
  matrix products  173 us (15%)
  other arithmetic  75.8 us (7%)
  blocking collectives  40 us (4%)
  between operations  18.1 us (2%)
  local copies, waits for them, and re-layouts  15.2 us (1%)
    reduce_scatter x2, waiting for transfers between devices, shards(): lax.psum_scatter(up_terms, 'tp', scatter_dimension=1, tiled=True)  145 us
    reduce_scatter x2, waiting for transfers between devices, shards(): lax.psum_scatter(down_terms, 'tp', scatter_dimension=1, tiled=True)  135 us
    reduce_scatter x2, waiting for transfers between devices, shards(): lax.psum_scatter(attn_terms, 'tp', scatter_dimension=1, tiled=True)  135 us
    reduce_scatter x2, waiting for transfers between devices, shards(): lax.psum_scatter(in_terms.astype(jnp.bfloat16), 'tp', scatter_dimension=1...  86.9 us
    all_gather x2, waiting for transfers between devices, shards(): lax.all_gather(normed, 'tp', axis=1, tiled=True)  84 us
    all_gather x2, waiting for transfers between devices, shards(): lax.all_gather(d_second.astype(jnp.bfloat16), 'tp', axis=1, tiled=True)  77.9 us
    all_gather x2, waiting for transfers between devices, shards(): lax.all_gather(d_first.astype(jnp.bfloat16), 'tp', axis=1, tiled=True)  67.1 us
    dot_general x2, matrix products, plain_product(): jnp.einsum('rnd,de->rne', piece, matrix, preferred_element_type=jnp.float32)  27.2 us
  transfers between devices with their start and end apart: 19, of which 18 were waited for; matrix products, arithmetic and copies ran while one was open for 16% of the time, Pallas kernels for 0%

commit v1 on v0

v1 whole, which is shorter than its diff:
```python
import functools
import jax
import jax.numpy as jnp
from jax import lax
from jax.experimental import pallas as pl
from jax.experimental.pallas import tpu as pltpu
from jax.sharding import PartitionSpec as P


HD = 64
PAIR = 2 * HD
SLOTS = 128
QB = 256
KB = 256
NEG = -1e30
NT = (((1,), (1,)), ((), ()))


def mm(a, b):
    return jnp.dot(a, b, preferred_element_type=jnp.float32)


def mm_nt(a, b):
    return lax.dot_general(a, b, NT, preferred_element_type=jnp.float32)


def head_lanes(half):
    lane = lax.broadcasted_iota(jnp.int32, (1, PAIR), 1)
    return (lane >= half * HD) & (lane < (half + 1) * HD)


def only_head(a, half):
    return jnp.where(head_lanes(half), a, jnp.zeros_like(a))


def attend_block(q, keys, values, seg_col, seg_row, live_row):
    mixed = jnp.zeros((q.shape[0], PAIR), jnp.float32)
    totals = jnp.zeros((q.shape[0], PAIR), jnp.float32)
    lane = lax.broadcasted_iota(jnp.int32, (1, PAIR), 1)
    for half in range(2):
        qh = only_head(q, half) * jnp.asarray(0.125, jnp.bfloat16)
        scores = mm_nt(qh, keys)
        seq = jnp.where(seg_col == seg_row, scores[:, SLOTS:], NEG)
        pre = jnp.where(live_row > 0.5, scores[:, :SLOTS], NEG)
        top = jnp.maximum(
            jnp.max(seq, axis=1, keepdims=True), jnp.max(pre, axis=1, keepdims=True)
        )
        seq = jnp.exp(seq - top)
        pre = jnp.exp(pre - top)
        total = jnp.sum(seq, axis=1, keepdims=True) + jnp.sum(pre, axis=1, keepdims=True)
        scale = 1.0 / total
        low = jnp.concatenate([(pre * scale).astype(jnp.bfloat16), (seq * scale).astype(jnp.bfloat16)], axis=1)
        out = mm(low, values)
        mixed = jnp.where(head_lanes(half), out, mixed)
        totals = jnp.where(lane == half, top + jnp.log(total), totals)
    return mixed.astype(jnp.bfloat16), totals


def forward_kernel(q_ref, k_ref, v_ref, pk_ref, pv_ref, meta_ref, seg_ref, att_ref, lse_ref, keys, values):
    keys[0:SLOTS, :] = pk_ref[...]
    keys[SLOTS:, :] = k_ref[...]
    values[0:SLOTS, :] = pv_ref[...]
    values[SLOTS:, :] = v_ref[...]

    def block(b, carry):
        rows = pl.ds(pl.multiple_of(b * QB, QB), QB)
        mixed, totals = attend_block(
            q_ref[rows, :], keys[...], values[...], seg_ref[rows, 0:1],
            meta_ref[0:1, SLOTS:], meta_ref[0:1, :SLOTS],
        )
        att_ref[rows, :] = mixed
        lse_ref[0, :, rows] = jnp.transpose(totals)[0:8, :]
        return carry

    lax.fori_loop(0, q_ref.shape[0] // QB, block, 0)


def attend_forward(q, k, v, pk, pv, meta, seg_col):
    length, width = q.shape
    pairs = width // PAIR
    block = pl.BlockSpec((length, PAIR), lambda p: (0, p))
    pre = pl.BlockSpec((SLOTS, PAIR), lambda p: (0, p))
    whole = lambda a: pl.BlockSpec(a.shape, lambda p: (0,) * a.ndim)
    return pl.pallas_call(
        forward_kernel,
        grid=(pairs,),
        in_specs=[block, block, block, pre, pre, whole(meta), whole(seg_col)],
        out_specs=[block, pl.BlockSpec((1, 8, length), lambda p: (p, 0, 0))],
        out_shape=[
            jax.ShapeDtypeStruct((length, width), jnp.bfloat16),
            jax.ShapeDtypeStruct((pairs, 8, length), jnp.float32),
        ],
        scratch_shapes=[
            pltpu.VMEM((SLOTS + length, PAIR), jnp.bfloat16),
            pltpu.VMEM((SLOTS + length, PAIR), jnp.bfloat16),
        ],
        compiler_params=pltpu.CompilerParams(vmem_limit_bytes=48 * 2**20),
    )(q, k, v, pk, pv, meta, seg_col)


def backward_kernel(
    bounds_ref, q_ref, k_ref, v_ref, do_ref, att_ref, pk_ref, pv_ref, lse_ref, meta_ref, seg_ref, live_ref,
    dq_ref, dk_ref, dv_ref, dpk_ref, dpv_ref,
    dk_acc, dv_acc, dpk_acc, dpv_acc, k_t, pk_t,
):
    length = q_ref.shape[0]
    dk_acc[...] = jnp.zeros_like(dk_acc)
    dv_acc[...] = jnp.zeros_like(dv_acc)
    dpk_acc[...] = jnp.zeros_like(dpk_acc)
    dpv_acc[...] = jnp.zeros_like(dpv_acc)
    k_t[...] = jnp.transpose(k_ref[...])
    pk_t[...] = jnp.transpose(pk_ref[...])
    picks = lax.broadcasted_iota(jnp.int32, (8, PAIR), 0)
    lanes = lax.broadcasted_iota(jnp.int32, (8, PAIR), 1) // HD
    picker = jnp.where(picks == lanes, 1.0, 0.0)

    def block(b, carry):
        start = pl.multiple_of(b * QB, QB)
        rows = pl.ds(start, QB)
        q = q_ref[rows, :]
        do = do_ref[rows, :]
        prod = do.astype(jnp.float32) * att_ref[rows, :].astype(jnp.float32)
        inner = lax.dot_general(
            picker, prod, NT, preferred_element_type=jnp.float32, precision=lax.Precision.HIGHEST
        )
        seg_q = meta_ref[0:1, pl.ds(SLOTS + start, QB)]
        heads = []
        for half in range(2):
            qh = only_head(q, half) * jnp.asarray(0.125, jnp.bfloat16)
            dh = only_head(do, half)
            lse = lse_ref[0, half : half + 1, rows]
            delta = inner[half : half + 1, :]
            heads.append((qh, dh, lse, delta))

        def tile(kk, vv, kt, allowed, half):
            qh, dh, lse, delta = heads[half]
            s = mm_nt(kk, qh)
            p = jnp.exp(jnp.where(allowed, s, NEG) - lse)
            dp = mm_nt(vv, dh)
            ds = (p * (dp - delta)).astype(jnp.bfloat16)
            return mm(ds, qh), mm(p.astype(jnp.bfloat16), dh), mm(kt, ds)

        dqs = []
        for half in range(2):
            a, g, dq = tile(
                pk_ref[...], pv_ref[...], pk_t[half * HD : (half + 1) * HD, :], live_ref[:, 0:1] > 0.5, half
            )
            dpk_acc[...] += a
            dpv_acc[...] += g
            dqs.append(dq)

        def step(j, dqs):
            at = pl.multiple_of(j * KB, KB)
            krows = pl.ds(at, KB)
            allowed = seg_ref[krows, 0:1] == seg_q
            dk = dk_acc[krows, :]
            dv = dv_acc[krows, :]
            outs = []
            for half in range(2):
                a, g, dq = tile(
                    k_ref[krows, :], v_ref[krows, :], k_t[half * HD : (half + 1) * HD, krows], allowed, half
                )
                dk = dk + a
                dv = dv + g
                outs.append(dqs[half] + dq)
            dk_acc[krows, :] = dk
            dv_acc[krows, :] = dv
            return tuple(outs)

        dqs = lax.fori_loop(bounds_ref[0, b], bounds_ref[1, b], step, tuple(dqs))
        dq_ref[rows, :] = (jnp.transpose(jnp.concatenate(dqs, axis=0)) * 0.125).astype(jnp.bfloat16)
        return carry

    lax.fori_loop(0, length // QB, block, 0)
    dk_ref[...] = dk_acc[...].astype(jnp.bfloat16)
    dv_ref[...] = dv_acc[...].astype(jnp.bfloat16)
    dpk_ref[...] = dpk_acc[...]
    dpv_ref[...] = dpv_acc[...]


def attend_backward(bounds, q, k, v, do, att, pk, pv, lse, meta, seg_col, live_col):
    length, width = q.shape
    pairs = width // PAIR
    block = pl.BlockSpec((length, PAIR), lambda p, *_: (0, p))
    pre = pl.BlockSpec((SLOTS, PAIR), lambda p, *_: (0, p))
    whole = lambda a: pl.BlockSpec(a.shape, lambda p, *_: (0,) * a.ndim)
    low = jax.ShapeDtypeStruct((length, width), jnp.bfloat16)
    full = jax.ShapeDtypeStruct((SLOTS, width), jnp.float32)
    return pl.pallas_call(
        backward_kernel,
        grid_spec=pltpu.PrefetchScalarGridSpec(
            num_scalar_prefetch=1,
            grid=(pairs,),
            in_specs=[
                block, block, block, block, block, pre, pre,
                pl.BlockSpec((1, 8, length), lambda p, *_: (p, 0, 0)),
                whole(meta), whole(seg_col), whole(live_col),
            ],
            out_specs=[block, block, block, pre, pre],
            scratch_shapes=[
                pltpu.VMEM((length, PAIR), jnp.float32),
                pltpu.VMEM((length, PAIR), jnp.float32),
                pltpu.VMEM((SLOTS, PAIR), jnp.float32),
                pltpu.VMEM((SLOTS, PAIR), jnp.float32),
                pltpu.VMEM((PAIR, length), jnp.bfloat16),
                pltpu.VMEM((PAIR, SLOTS), jnp.bfloat16),
            ],
        ),
        out_shape=[low, low, low, full, full],
        compiler_params=pltpu.CompilerParams(vmem_limit_bytes=48 * 2**20),
    )(bounds, q, k, v, do, att, pk, pv, lse, meta, seg_col, live_col)


def block_bounds(seg):
    length = seg.shape[0]
    first = seg[::QB]
    last = seg[QB - 1 :: QB]
    low = jnp.sum((seg[None, :] < first[:, None]).astype(jnp.int32), axis=1)
    high = jnp.sum((seg[None, :] <= last[:, None]).astype(jnp.int32), axis=1)
    return jnp.stack([low // KB, (high + KB - 1) // KB])


MESH = pl.DeviceIdType.MESH
LINE = 4
LANES = 128


class Plan:
    def __init__(self, rows, tp):
        self.rows = rows
        self.tp = tp
        self.core_in_tp = tp > LINE
        self.shape = (rows // 8, 2, 4) if self.core_in_tp else (rows // 4, 2, 2)
        self.axes = (0, 1, 2) if self.core_in_tp else (0, 1)
        self.cores = 2 if self.core_in_tp else 1

    def here(self):
        r = lax.axis_index("rows")
        t = lax.axis_index("tp")
        a, b, c = self.shape
        coords = (r // (b * c), lax.rem(r // c, b), lax.rem(r, c))
        if self.core_in_tp:
            return coords, t // 2, lax.rem(t, 2)
        return coords, t, coords[2]

    def device(self, coords, line, core):
        a, b, c = self.shape
        if self.core_in_tp:
            return ((coords[0] * b + coords[1]) * c + coords[2], line * 2 + core)
        return ((coords[0] * b + coords[1]) * c + core, line)


def shifted(coords, axis, by, size):
    moved = list(coords)
    moved[axis] = lax.rem(coords[axis] + by, size)
    return tuple(moved)


def sibling(plan, coords, line, core):
    return plan.device(coords, line, 1 - core)


def greet(plan, coords, line, core):
    others = [
        plan.device(coords, lax.rem(line + by, LINE), side) for by in range(1, LINE) for side in range(2)
    ]
    others.append(sibling(plan, coords, line, core))
    for axis in plan.axes:
        for by in range(1, plan.shape[axis]):
            others.append(plan.device(shifted(coords, axis, by, plan.shape[axis]), line, core))
    barrier = pltpu.get_barrier_semaphore()
    for other in others:
        pl.semaphore_signal(barrier, inc=1, device_id=other, device_id_type=MESH)
    pl.semaphore_wait(barrier, len(others))


class Gather:
    def __init__(self, plan, place, source, whole, sems):
        self.plan = plan
        self.coords, self.line, self.core = place
        self.source = source
        self.whole = whole
        self.sems = sems
        self.count = source.shape[0] * (1 if plan.core_in_tp else 2)
        self.depth = source.shape[-2]
        self.orders = (plan.axes, plan.axes[::-1])

    def unit(self, i):
        if self.plan.core_in_tp:
            return (i, self.core)
        return (i // 2, lax.rem(i, 2))

    def remote(self, src, dst, send, recv, device):
        return pltpu.make_async_remote_copy(
            src_ref=src, dst_ref=dst, send_sem=send, recv_sem=recv, device_id=device, device_id_type=MESH
        )

    def own(self):
        lanes = pl.ds(pl.multiple_of(self.line * LANES, LANES), LANES)
        where = (slice(None),) + tuple(self.coords) + (slice(None), lanes)
        if self.plan.core_in_tp:
            pairs = [(self.source, self.whole.at[(slice(None), self.core) + where[1:]])]
        else:
            pairs = [
                (self.source.at[:, side], self.whole.at[(slice(None), side) + where[1:]]) for side in range(2)
            ]
        return pairs

    def line_copies(self, i):
        lanes = pl.ds(pl.multiple_of(self.line * LANES, LANES), LANES)
        unit = self.unit(i)
        src = self.source.at[i] if self.plan.core_in_tp else self.source.at[unit]
        dst = self.whole.at[unit + tuple(self.coords) + (slice(None), lanes)]
        for by in range(1, LINE):
            yield self.remote(
                src, dst, self.sems["line_send"].at[i, by - 1], self.sems["line_recv"].at[i, by - 1],
                self.plan.device(self.coords, lax.rem(self.line + by, LINE), self.core),
            )

    def axis_copies(self, i, step):
        rows = self.depth // 2
        for half in range(2):
            order = self.orders[half]
            axis = order[step]
            size = self.plan.shape[axis]
            index = [
                pl.ds(0, self.plan.shape[a]) if a in order[:step] else self.coords[a] for a in range(3)
            ]
            block = self.whole.at[self.unit(i) + tuple(index) + (pl.ds(half * rows, rows),)]
            for by in range(1, size):
                spot = (i, half, step, by - 1)
                yield self.remote(
                    block, block, self.sems["axis_send"].at[spot], self.sems["axis_recv"].at[spot],
                    self.plan.device(shifted(self.coords, axis, by, size), self.line, self.core),
                )

    def core_copy(self, i, side):
        if self.plan.core_in_tp:
            block = self.whole.at[i, side]
        else:
            block = self.whole.at[self.unit(i) + (slice(None), slice(None), side)]
        return self.remote(
            block, block, self.sems["core_send"].at[i], self.sems["core_recv"].at[i],
            sibling(self.plan, self.coords, self.line, self.core),
        )

    def core_roles(self, i):
        if self.plan.core_in_tp:
            wide = i >= 3
            return wide, wide
        side = lax.rem(i, 2)
        wide = i >= 6
        return wide | (side != self.core), wide | (side == self.core)

    def start_line(self, i):
        for copy in self.line_copies(i):
            copy.start()

    def start_axis(self, i, step):
        waits = self.line_copies(i) if step == 0 else self.axis_copies(i, step - 1)
        for copy in waits:
            copy.wait_recv()
        for copy in self.axis_copies(i, step):
            copy.start()

    def start_core(self, i):
        for copy in self.axis_copies(i, len(self.plan.axes) - 1):
            copy.wait_recv()
        sends, _ = self.core_roles(i)

        @pl.when(sends)
        def _():
            self.core_copy(i, self.core).start()

    def finish(self, i):
        _, gets = self.core_roles(i)

        @pl.when(gets)
        def _():
            self.core_copy(i, 1 - self.core).wait_recv()

    def drain(self, i):
        for copy in self.line_copies(i):
            copy.wait_send()
        for step in range(len(self.plan.axes)):
            for copy in self.axis_copies(i, step):
                copy.wait_send()
        sends, _ = self.core_roles(i)

        @pl.when(sends)
        def _():
            self.core_copy(i, self.core).wait_send()


def gather_semaphores(plan, count):
    steps = len(plan.axes)
    reach = max(plan.shape[a] for a in plan.axes) - 1
    shapes = {
        "line_send": (count, LINE - 1),
        "line_recv": (count, LINE - 1),
        "axis_send": (count, 2, steps, reach),
        "axis_recv": (count, 2, steps, reach),
        "core_send": (count,),
        "core_recv": (count,),
    }
    return {name: pltpu.SemaphoreType.DMA(shape) for name, shape in shapes.items()}


class Line:
    def __init__(self, plan, place, name, sems):
        self.plan = plan
        self.coords, self.line, self.core = place
        self.send_sems = sems[name + "_send"]
        self.recv_sems = sems[name + "_recv"]
        self.pieces = []

    def here(self, chip, side):
        return (chip == self.line) & (side == self.core)

    def send(self, src, dst, chip, side):
        at = len(self.pieces)
        far = pltpu.make_async_remote_copy(
            src_ref=src, dst_ref=dst, send_sem=self.send_sems.at[at],
            recv_sem=self.recv_sems.at[self.line, self.core],
            device_id=self.plan.device(self.coords, chip, side), device_id_type=MESH,
        )
        near = pltpu.make_async_copy(src, dst, self.send_sems.at[at])
        stays = self.here(chip, side)
        self.pieces.append((stays, far, near))
        pl.when(jnp.logical_not(stays))(far.start)
        pl.when(stays)(near.start)

    def settle(self):
        for stays, _, near in self.pieces:
            pl.when(stays)(near.wait)

    def drain(self):
        for stays, far, _ in self.pieces:
            pl.when(jnp.logical_not(stays))(far.wait_send)

    def receive(self, dst, chip, side):
        copy = pltpu.make_async_remote_copy(
            src_ref=dst, dst_ref=dst, send_sem=self.send_sems.at[0], recv_sem=self.recv_sems.at[chip, side],
            device_id=self.plan.device(self.coords, chip, side), device_id_type=MESH,
        )
        pl.when(jnp.logical_not(self.here(chip, side)))(copy.wait_recv)


def line_semaphores(name, count):
    return {
        name + "_send": pltpu.SemaphoreType.DMA((count,)),
        name + "_recv": pltpu.SemaphoreType.DMA((LINE, 2)),
    }


def gather_kernel(plan, names, source, tokens, grads, prefix, meta, whole, row, grad, pre, row_meta, *sems):
    sems = dict(zip(names, sems))
    place = plan.here()
    coords, line, core = place
    greet(plan, coords, line, core)
    rows_here = tokens.shape[0]
    spread = plan.core_in_tp
    base = 0 if spread else 2 * core
    slot = core if spread else 0
    holds = (line // 2 == core) if not spread else None
    other = sibling(plan, coords, line, core)

    def held(body):
        if holds is None:
            body()
        else:
            pl.when(holds)(body)

    lanes = pl.ds(pl.multiple_of(line * LANES, LANES), LANES)
    token_line = Line(plan, place, "token", sems)
    for j in range(rows_here):
        token_line.send(tokens.at[j], row.at[line, slot], base + j, core)
    gather = Gather(plan, place, source, whole, sems)
    own = [
        pltpu.make_async_copy(src, dst, sems["own"].at[i]) for i, (src, dst) in enumerate(gather.own())
    ]
    for copy in own:
        copy.start()
    lax.fori_loop(0, gather.count, lambda i, x: (gather.start_line(i), x)[1], 0)
    prefix_line = Line(plan, place, "prefix", sems)
    grad_line = Line(plan, place, "grad", sems)
    for j in range(rows_here):
        for side in range(2 // plan.cores):
            prefix_line.send(prefix.at[j, side], pre.at[:, :, lanes], base + j, core if spread else side)
    for j in range(rows_here):
        grad_line.send(grads.at[j], grad.at[lax.rem(line, 2), slot], base + j, line // 2)

    mine = line if spread else lax.rem(line, 2)
    meta_far = pltpu.make_async_remote_copy(
        src_ref=meta.at[mine], dst_ref=row_meta, send_sem=sems["meta"].at[0], recv_sem=sems["meta"].at[1],
        device_id=other, device_id_type=MESH,
    )
    meta_near = pltpu.make_async_copy(meta.at[mine], row_meta, sems["meta"].at[2])
    if spread:
        meta_near.start()
        meta_near.wait()
    else:
        @pl.when(holds)
        def _():
            meta_near.start()
            meta_far.start()
            meta_near.wait()
            meta_far.wait_send()

        @pl.when(jnp.logical_not(holds))
        def _():
            meta_far.wait_recv()

    for copy in own:
        copy.wait()

    token_line.settle()
    mine = row.at[:, slot]
    share = pltpu.make_async_remote_copy(
        src_ref=mine, dst_ref=mine, send_sem=sems["share"].at[0], recv_sem=sems["share"].at[1],
        device_id=other, device_id_type=MESH,
    )

    @held
    def _():
        for chip in range(LINE):
            token_line.receive(row.at[chip, slot], chip, core)
        share.start()
        share.wait_send()

    if spread:
        share.wait_recv()
    else:
        pl.when(jnp.logical_not(holds))(share.wait_recv)

    steps = len(plan.axes)
    lag = 2

    def tick(i, x):
        for step in range(steps + 1):
            at = i - lag * step

            def go(step=step, at=at):
                if step < steps:
                    gather.start_axis(at, step)
                else:
                    gather.start_core(at)

            pl.when((at >= 0) & (at < gather.count))(go)
        return x

    lax.fori_loop(0, gather.count + lag * steps, tick, 0)
    lax.fori_loop(0, gather.count, lambda i, x: (gather.finish(i), x)[1], 0)
    lax.fori_loop(0, gather.count, lambda i, x: (gather.drain(i), x)[1], 0)

    prefix_line.settle()
    grad_line.settle()
    for chip in range(LINE):
        prefix_line.receive(pre.at[:, :, pl.ds(chip * LANES, LANES)], chip, core if spread else line // 2)
    for part in range(2):
        for side in range(plan.cores):
            grad_line.receive(grad.at[part, side], 2 * core + part, side if spread else line // 2)
    token_line.drain()
    prefix_line.drain()
    grad_line.drain()


def gather_call(plan, source, tokens, grads, prefix, meta):
    count, depth = source.shape[0] * (source.shape[1] if not plan.core_in_tp else 1), source.shape[-2]
    held, places, width = tokens.shape
    sems = gather_semaphores(plan, count)
    for name, amount in (("token", held), ("prefix", held * 2), ("grad", held)):
        sems.update(line_semaphores(name, amount))
    for name in ("own", "meta", "share"):
        sems[name] = pltpu.SemaphoreType.DMA((4,))
    outs = [
        jax.ShapeDtypeStruct((12, 2) + plan.shape + (depth, LINE * LANES), jnp.bfloat16),
        jax.ShapeDtypeStruct((LINE, plan.cores, places, width), jnp.bfloat16),
        jax.ShapeDtypeStruct((2, plan.cores, places, width), jnp.bfloat16),
        jax.ShapeDtypeStruct((2, prefix.shape[3], LINE * LANES), jnp.bfloat16),
        jax.ShapeDtypeStruct(meta.shape[1:], jnp.float32),
    ]
    return pl.pallas_call(
        functools.partial(gather_kernel, plan, tuple(sems)),
        out_shape=outs,
        in_specs=[pl.BlockSpec(memory_space=pl.ANY)] * 5,
        out_specs=[pl.BlockSpec(memory_space=pl.ANY)] * 5,
        scratch_shapes=list(sems.values()),
        compiler_params=pltpu.CompilerParams(collective_id=0, has_side_effects=True),
    )(source, tokens, grads, prefix, meta)


def give_back_kernel(plan, names, parts, pieces, *sems):
    sems = dict(zip(names, sems))
    place = plan.here()
    coords, line, core = place
    greet(plan, coords, line, core)
    places = pieces.shape[2]
    back = Line(plan, place, "back", sems)
    for half in range(2):
        for side in range(plan.cores):
            start = (half * plan.cores + side) * places
            if plan.core_in_tp:
                slot, target = line, side
            else:
                slot, target = lax.rem(line, 2), line // 2
            back.send(parts.at[:, pl.ds(start, places)], pieces.at[:, slot], 2 * core + half, target)
    back.settle()
    for j in range(pieces.shape[1]):
        chip = j if plan.core_in_tp else 2 * core + j
        back.receive(pieces.at[:, j], chip, line // 2)
    back.drain()


def give_back(plan, parts, held, places):
    sems = line_semaphores("back", 4)
    return pl.pallas_call(
        functools.partial(give_back_kernel, plan, tuple(sems)),
        out_shape=jax.ShapeDtypeStruct((parts.shape[0], held, places, parts.shape[2]), parts.dtype),
        in_specs=[pl.BlockSpec(memory_space=pl.ANY)],
        out_specs=pl.BlockSpec(memory_space=pl.ANY),
        scratch_shapes=list(sems.values()),
        compiler_params=pltpu.CompilerParams(collective_id=1, has_side_effects=True),
    )(parts)


def layer_norm_parts(z):
    mean = jnp.mean(z, axis=-1, keepdims=True)
    centred = z - mean
    rstd = lax.rsqrt(jnp.mean(centred * centred, axis=-1, keepdims=True) + 1e-05)
    return centred * rstd, rstd


def layer_norm_grad(normal, rstd, gain, grad):
    g = grad * gain
    return rstd * (
        g
        - jnp.mean(g, axis=-1, keepdims=True)
        - normal * jnp.mean(g * normal, axis=-1, keepdims=True)
    )


def gelu_exact(v):
    return jax.nn.gelu(v, approximate=False)


def own_blocks(plan, w_query, w_key, w_value, w_attn_out, w_up, w_down):
    depth = w_query.shape[0]

    def cut(a):
        return jnp.transpose(a.reshape(depth, -1, LANES), (1, 0, 2))

    sides = 2 // plan.cores
    first = [cut(a) for a in (w_query, w_key, w_value, w_attn_out.T)]
    up, down = cut(w_up), cut(w_down.T)
    blocks = [a.reshape(1, sides, depth, LANES) for a in first]
    for j in range(up.shape[0] // sides):
        for a in (up, down):
            blocks.append(a[j * sides : (j + 1) * sides][None])
    joined = jnp.concatenate(blocks, axis=0)
    return joined[:, 0] if plan.core_in_tp else joined


def shards(
    plan, tokens, w_query, w_key, w_value, w_attn_out, w_up, w_down, first_gain, first_shift,
    second_gain, second_shift, prefix_keys, prefix_values, example_lengths, task_ids, prefix_lens,
    slot_masks, out_grad,
):
    f32, bf16 = jnp.float32, jnp.bfloat16
    held, places, width = tokens.shape
    tasks, slots, part = prefix_keys.shape
    length = places * plan.tp
    _, line, core = plan.here()
    half = length // 2

    ends = jnp.cumsum(example_lengths, axis=1)
    spots = jnp.arange(length, dtype=jnp.int32)
    segment = jnp.sum((spots[None, :, None] >= ends[:, None, :]).astype(jnp.int32), axis=-1)
    live = (jnp.arange(slots, dtype=jnp.int32)[None, :] < prefix_lens[:, None]) & (slot_masks == 1)
    onehot = task_ids[:, None] == jnp.arange(tasks, dtype=jnp.int32)[None, :]
    live_rows = jnp.any(onehot[:, :, None] & live[None], axis=1)
    meta = jnp.zeros((held, 8, SLOTS + length), f32)
    meta = meta.at[:, 0, :slots].set(live_rows.astype(f32))
    meta = meta.at[:, 0, SLOTS:].set(segment.astype(f32))
    meta = meta.at[:, 1, :tasks].set(onehot.astype(f32))
    picker = onehot.astype(bf16)
    prefix = jnp.stack([prefix_keys, prefix_values])
    prefix = jnp.einsum("rt,atpe->rape", picker, prefix, preferred_element_type=f32).astype(bf16)
    prefix = jnp.pad(prefix, ((0, 0), (0, 0), (0, SLOTS - slots), (0, 0)))
    sides = 2 // plan.cores
    prefix = jnp.transpose(prefix.reshape(held, 2, SLOTS, sides, LANES), (0, 3, 1, 2, 4))

    source = own_blocks(plan, w_query, w_key, w_value, w_attn_out, w_up, w_down)
    whole, row, grad, pre, row_meta = gather_call(plan, source, tokens, out_grad, prefix, meta)
    whole = whole.reshape(12, 2, width, LINE * LANES)
    x = row.reshape(length, width)
    cotangent = grad.reshape(half, width)

    def mine(a):
        return lax.dynamic_index_in_dim(a, core, 0, keepdims=False)

    def pick(a, which):
        return lax.dynamic_slice_in_dim(a, which * half, half, 0)

    def swap(a):
        if plan.core_in_tp:
            return lax.ppermute(a, "tp", [(i, i ^ 1) for i in range(plan.tp)])
        return lax.ppermute(a, "rows", [(i, i ^ 1) for i in range(plan.rows)])

    def paired(own, other):
        return jnp.where(core == 0, own, other), jnp.where(core == 0, other, own)

    w_q, w_k, w_v = (mine(whole[i]) for i in range(3))
    q, k, v = (jnp.dot(x, w, preferred_element_type=f32).astype(bf16) for w in (w_q, w_k, w_v))
    seg = row_meta[0, SLOTS:]
    seg_col = jnp.broadcast_to(seg[:, None], (length, LANES))
    live_col = jnp.broadcast_to(row_meta[0, :SLOTS][:, None], (SLOTS, LANES))
    att, lse = attend_forward(q, k, v, pre[0], pre[1], row_meta, seg_col)
    att_low, att_high = paired(pick(att, core), swap(pick(att, 1 - core)))
    first_sum = pick(x, core).astype(f32) + mm_nt(att_low, whole[3, 0]) + mm_nt(att_high, whole[3, 1])
    n_one, r_one = layer_norm_parts(first_sum)
    normed = (n_one * first_gain + first_shift).astype(bf16)
    up, down = whole[4::2].reshape(8, width, -1), whole[5::2].reshape(8, width, -1)
    upper = jnp.einsum("pd,udf->upf", normed, up, preferred_element_type=f32)
    acted, gelu_pull = jax.vjp(gelu_exact, upper)
    second_sum = normed.astype(f32) + jnp.einsum(
        "upf,udf->pd", acted.astype(bf16), down, preferred_element_type=f32
    )
    n_two, r_two = layer_norm_parts(second_sum)
    output = (n_two * second_gain + second_shift).astype(bf16)

    d_second = layer_norm_grad(n_two, r_two, second_gain, cotangent.astype(f32))
    d_acted = jnp.einsum("pd,udf->upf", d_second.astype(bf16), down, preferred_element_type=f32)
    d_upper = gelu_pull(d_acted)[0].astype(bf16)
    d_normed = d_second + jnp.einsum("upf,udf->pd", d_upper, up, preferred_element_type=f32)
    d_first = layer_norm_grad(n_one, r_one, first_gain, d_normed)
    d_att = jnp.einsum("pd,cde->cpe", d_first.astype(bf16), whole[3], preferred_element_type=f32).astype(bf16)
    d_att = jnp.concatenate(paired(mine(d_att), swap(lax.dynamic_index_in_dim(d_att, 1 - core, 0, keepdims=False))), axis=0)
    bounds = block_bounds(seg.astype(jnp.int32))
    dq, dk, dv, dpk, dpv = attend_backward(
        bounds, q, k, v, d_att, att, pre[0], pre[1], lse, row_meta, seg_col, live_col
    )
    shares = mm_nt(dq, w_q) + mm_nt(dk, w_k) + mm_nt(dv, w_v)
    other = swap(pick(shares, 1 - core).astype(bf16)).astype(f32)
    d_tokens = d_first + pick(shares, core) + other
    back = give_back(plan, jnp.stack([output, d_tokens.astype(bf16)]), held, places)

    d_pre = jnp.stack([dpk, dpv])[:, :slots].reshape(2, slots, LINE, LANES)
    side = (jnp.arange(2) == core).astype(f32)
    d_pre = row_meta[1, :tasks][None, :, None, None, None, None] * (
        d_pre[:, None, :, :, None, :] * side[None, None, None, None, :, None]
    )
    d_pre = d_pre.reshape(2, tasks, slots, width).astype(bf16)
    d_pre = lax.psum_scatter(d_pre, "tp", scatter_dimension=3, tiled=True)
    d_pre = lax.psum(d_pre, "rows").astype(f32)
    return back[0], back[1].astype(f32), d_pre[0], d_pre[1]


def solution(mesh):
    placed = (
        P("rows", "tp", None),
        P("rows", "tp"),
        P("rows", "tp"),
        P("rows", "tp"),
        P("tp", "rows"),
        P("rows", "tp"),
        P("tp", "rows"),
        P(),
        P(),
        P(),
        P(),
        P(None, None, "tp"),
        P(None, None, "tp"),
        P("rows", None),
        P("rows"),
        P(),
        P(),
        P("rows", "tp", None),
    )
    plan = Plan(mesh.shape["rows"], mesh.shape["tp"])
    return jax.shard_map(
        functools.partial(shards, plan),
        mesh=mesh,
        in_specs=placed,
        out_specs=(
            P("rows", "tp", None),
            P("rows", "tp", None),
            P(None, None, "tp"),
            P(None, None, "tp"),
        ),
        check_vma=False,
    )
```

time: 1130 us -> 689 us (0.61)
  waiting for transfers between devices: 795 us -> 66.9 us
  Pallas kernels: 0 us -> 320 us
  local copies, waits for them, and re-layouts: 15.2 us -> 164 us
  matrix products: 173 us -> 86.8 us
  other arithmetic: 75.8 us -> 22.6 us
  blocking collectives: 40 us -> 0 us
    reduce_scatter x8 -> x0, waiting for transfers between devices: 503 us -> none  [the longest x2 145 us: shards(): lax.psum_scatter(up_terms, 'tp', scatter_dimension=1, tiled=True)]
    pallas_call x0 -> x4, Pallas kernels: none -> 320 us  [the longest x1 180 us: gather_call(): pl.pallas_call(functools.partial(gather_kernel, plan, tuple(sems)), out_s...]
    all_gather x10 -> x0, waiting for transfers between devices: 270 us -> none  [the longest x2 84 us: shards(): lax.all_gather(normed, 'tp', axis=1, tiled=True)]
    unnamed x256 -> x85, local copies, waits for them, and re-layouts: 7.7 us -> 135 us
    dot_general x67 -> x13, matrix products: 173 us -> 86.8 us  [the longest x1 25.8 us: shards(): upper = jnp.einsum('pd,udf->upf', normed, up, preferred_element_type=f32)]
    psum x1, waiting for transfers between devices: 19.3 us -> 62.8 us  [shards(): d_pre = lax.psum(d_pre, 'rows').astype(f32)]
    all_gather x4 -> x0, blocking collectives: 40 us -> none  [the longest x1 11.3 us: shards(): lax.all_gather(w_query, 'rows', axis=0, tiled=True)]
    convert_element_type x14 -> x7, other arithmetic: 37.5 us -> 5.68 us  [the longest x1 1.99 us: shards(): return (back[0], back[1].astype(f32), d_pre[0], d_pre[1])]
  transfers between devices with their start and end apart: 19 -> 5, of which waited for: 18 -> 3; matrix products, arithmetic and copies ran while one was open for 16% -> 3% of each run, Pallas kernels for 0% -> 11%
where the time goes in v1:
time: 689 us; the launch traced here: 677 us
  Pallas kernels  320 us (46%)
  local copies, waits for them, and re-layouts  164 us (24%)
  matrix products  86.8 us (13%)
  waiting for transfers between devices  66.9 us (10%)
  other arithmetic  22.6 us (3%)
  between operations  15.2 us (2%)
    pallas_call x1, Pallas kernels, gather_call(): pl.pallas_call(functools.partial(gather_kernel, plan, tuple(sems)), out_s...  180 us
    unnamed x85, local copies, waits for them, and re-layouts  135 us
    pallas_call x1, Pallas kernels, give_back(): pl.pallas_call(functools.partial(give_back_kernel, plan, tuple(sems)), ou...  74.1 us
    psum x1, waiting for transfers between devices, shards(): d_pre = lax.psum(d_pre, 'rows').astype(f32)  62.8 us
    pallas_call x1, Pallas kernels, attend_backward(): pl.pallas_call(backward_kernel, grid_spec=pltpu.PrefetchScalarGridSpec(nu...  37.2 us
    pallas_call x1, Pallas kernels, attend_forward(): pl.pallas_call(forward_kernel, grid=(pairs,), in_specs=[block, block, blo...  28.1 us
    dot_general x1, matrix products, shards(): upper = jnp.einsum('pd,udf->upf', normed, up, preferred_element_type=f32)  25.8 us
    dot_general x1, matrix products, shards(): jnp.einsum('upf,udf->pd', d_upper, up, preferred_element_type=f32)  24.9 us
  transfers between devices with their start and end apart: 5, of which 3 were waited for; matrix products, arithmetic and copies ran while one was open for 3% of the time, Pallas kernels for 11%

profile of v1, /device:TPU:0, one launch (start us, length us, event | category | flops | bytes accessed | tf_op | source)
XLA Modules:
  0.0 676.8 jit_solution(14354163977173862763)
XLA Ops:
  16.8 2.0 broadcast_select_fusion
  18.8 1.6 scatter.19
  24.8 180.2 %shard_map.201 = (bf16[12,2,2,2,2,128,512]{6,5,4,3,2,1,0:T(8,128)(2,1)}, bf16[4,1,256,1024]{3,2,1,0:T(8,128)(2,1)}, bf16[2,1,256,1024]{3,2,1,0:T(8,128)(2,1)}, bf16[2,128,512]{2,1,0:T(8,128)(2,1)}, f32[8,1152]{1,0:T(8,128)}) custom-call(bf16[12,2,128,128]{3,2,1,0:T(8,128)(2,1)} %copy-done.22, bf16[2,256,1024]{2,1,0:T(8,128)(2,1)} %tokens.1, ...), custom_call_target="tpu_custom_call" | custom-call | tf_op jit(solution)/shard_map/pallas_call | solution.py:583
  206.8 6.0 fusion.87
  212.8 3.2 convolution_convert_fusion.1.v_ref
  216.1 2.2 convolution_convert_fusion.2.k_ref
  218.3 2.2 convolution_convert_fusion.3.q_ref
  223.2 28.1 %shard_map.202 = (bf16[1024,512]{1,0:T(8,128)(2,1)S(1)}, f32[4,8,1024]{2,1,0:T(8,128)S(1)}) custom-call(bf16[1024,512]{1,0:T(8,128)(2,1)S(1)} %copy-done.3, bf16[1024,512]{1,0:T(8,128)(2,1)S(1)} %copy-done.2, bf16[1024,512]{1,0:T(8,128)(2,1)S(1)} %convolution_convert_fusion.1.v_ref, bf16[128,512]{1,0:T(8,128)(2,1)S(1)} %get-tuple-element.83.pk_ref, ...), custom_call_target="tpu_custom_call" | custom-call | tf_op jit(solution)/shard_map/pallas_call | solution.py:84
  252.3 11.6 %fusion.86 = (bf16[4,2,1024,512]{3,2,1,0:T(8,128)(2,1)}, bf16[4,2,1024,512]{3,2,1,0:T(8,128)(2,1)}) fusion(bf16[12,2,1024,512]{3,2,1,0:T(8,128)(2,1)} %bitcast.307), kind=kLoop, calls=%fused_computation.178 | loop fusion | bytes 33554432 | tf_op jit(solution)/shard_map/slice | solution.py:723
  264.7 2.1 fusion.32
  266.9 2.2 fusion.90
  269.5 1.8 copy-done.15
  271.3 25.8 %fusion = (f32[8,512,512]{1,2,0:T(8,128)}, f32[8,512,512]{2,1,0:T(8,128)}) fusion(bf16[8,1024,512]{2,1,0:T(8,128)(2,1)S(1)} %bitcast.311, f32[1024]{0:T(1024)S(1)} %copy-done.30, f32[1024]{0:T(1024)S(1)} %copy-done.31, f32[512]{0:T(512)S(1)} %add_rsqrt_fusion.1, f32[512,1024]{1,0:T(8,128)S(1)} %get-tuple-element.89, f32[512]{0:T(512)S(1)} %broadcast_multiply_fusion.5), kind=kOutput, calls=%fused_computation.1 | convolution fusion | flops 4427612160 | bytes 27275264 | tf_op jit(solution)/shard_map/pd,udf->upf/dot_general | solution.py:724
  297.2 13.7 %fusion.91 = (f32[512]{0:T(512)S(1)}, f32[512,1024]{1,0:T(8,128)S(1)}) fusion(bf16[8,1024,512]{2,1,0:T(8,128)(2,1)} %bitcast.312, f32[8,512,512]{1,2,0:T(8,128)} %get-tuple-element.90, f32[8,512,512]{2,1,0:T(8,128)} %get-tuple-element.91, f32[1024]{0:T(1024)S(1)} %copy-done.30, f32[1024]{0:T(1024)S(1)} %copy-done.31, f32[512]{0:T(512)S(1)} %add_rsqrt_fusion.1, ...), kind=kOutput, calls=%fused_computation.183 | convolution fusion | flops 4305452544 | bytes 29374464 | tf_op jit(solution)/shard_map/upf,udf->pd/dot_general | solution.py:726
  311.3 1.6 copy-done.13
  312.9 1.7 fusion.29
  314.5 3.7 subtract_multiply_fusion.1
  318.2 24.9 %fusion.85 = (f32[512]{0:T(512)S(1)}, f32[512]{0:T(512)S(1)}, f32[512,1024]{1,0:T(8,128)}) fusion(f32[512]{0:T(512)S(1)} %add_rsqrt_fusion.1, f32[512,1024]{1,0:T(8,128)S(1)} %copy-done.9, f32[512]{0:T(512)S(1)} %broadcast_multiply_fusion.5, f32[1024]{0:T(1024)S(1)} %copy-done.31, f32[512,1024]{1,0:T(8,128)} %subtract_multiply_fusion.1, ...), kind=kOutput, calls=%fused_computation.177 | convolution fusion | flops 8623489024 | bytes 39858176 | tf_op jit(solution)/shard_map/upf,udf->pd/dot_general | solution.py:735
  343.1 3.7 convolution_convert_fusion
  347.2 1.6 collective-permute-done.1
  350.1 37.2 %shard_map.203 = (bf16[1024,512]{1,0:T(8,128)(2,1)S(1)}, bf16[1024,512]{1,0:T(8,128)(2,1)S(1)}, bf16[1024,512]{1,0:T(8,128)(2,1)S(1)}, f32[128,512]{1,0:T(8,128)S(1)}, f32[128,512]{1,0:T(8,128)S(1)}) custom-call(s32[2,4]{1,0:T(2,128)S(1)} %pad_add_fusion.bounds_ref, bf16[1024,512]{1,0:T(8,128)(2,1)S(1)} %copy-done.4, ...), custom_call_target="tpu_custom_call" | custom-call | tf_op jit(solution)/shard_map/pallas_call | solution.py:189
  389.6 1.8 mul.216
  391.6 1.8 multiply_convert_fusion
  393.4 42.5 %copy.96 = bf16[2,4,100,1024]{1,2,0,3:T(8,128)(2,1)} copy(bf16[2,4,100,1024]{3,1,2,0:T(4,128)(2,1)} %multiply_convert_fusion) | data formatting | bytes 3276800
  435.9 51.7 %reshape.437 = bf16[1024,800]{1,0:T(8,128)(2,1)} reshape(bf16[1024,2,100,4]{3,2,1,0:T(8,128)(2,1)} %bitcast.305) | data formatting | bytes 3276800
  487.7 2.7 fusion.43
  494.1 2.4 collective-permute-done.2
  498.9 74.1 %shard_map.204 = bf16[2,2,256,1024]{3,2,1,0:T(8,128)(2,1)} custom-call(bf16[2,512,1024]{2,1,0:T(8,128)(2,1)} %pad_maximum_fusion.parts), custom_call_target="tpu_custom_call" | custom-call | tf_op jit(solution)/shard_map/pallas_call | solution.py:617
  573.0 14.9 %reshape.438 = bf16[256,2,100,4]{3,2,1,0:T(8,128)(2,1)} reshape(bf16[256,800]{1,0:T(8,128)(2,1)} %reduce-scatter.4.cloned.1.call-done) | data formatting | bytes 819200
  587.9 14.6 %copy.97 = bf16[2,4,100,256]{3,1,2,0:T(4,128)(2,1)} copy(bf16[2,4,100,256]{1,2,0,3:T(8,128)(2,1)} %bitcast.306) | data formatting | bytes 819200
  602.5 2.0 bitcast_convert_fusion
  604.5 62.8 %all-reduce.4.cloned.1.call-done = bf16[2,4,100,256]{3,1,2,0:T(4,128)(2,1)} async-done(((bf16[2,4,100,256]{3,1,2,0:T(4,128)(2,1)}), bf16[2,4,100,256]{3,1,2,0:T(4,128)(2,1)}) %all-reduce.4.cloned.1.call-update) | async-done | bytes 409616 | tf_op jit(solution)/shard_map/psum | solution.py:755
  (150 shorter events, 32.9 us)
Async XLA Ops:
  7.2 15.9 %copy-start.26 = (bf16[128,1024]{1,0:T(8,128)(2,1)S(1)}, bf16[128,1024]{1,0:T(8,128)(2,1)}, u32[]{:S(2)}) copy-start(bf16[128,1024]{1,0:T(8,128)(2,1)} %param.29) | copy-start | bytes 786436
  7.2 565.8 %reduce-scatter.4.cloned.1.call-start = ((), (), s32[]{:S(2)}) async-start(), calls=%async_computation.2 | async-start | bytes 2293760
  14.4 9.1 %copy-start.27 = (bf16[1024,128]{1,0:T(8,128)(2,1)S(1)}, bf16[1024,128]{1,0:T(8,128)(2,1)}, u32[]{:S(2)}) copy-start(bf16[1024,128]{1,0:T(8,128)(2,1)} %param.30) | copy-start | bytes 786436
  212.8 3.3 copy-start.17
  212.8 3.3 copy-start.23
  216.1 4.7 copy-start.1
  216.1 2.2 copy-start.19
  218.3 2.4 copy-start.7
  251.4 15.5 %copy-start = (bf16[1024,512]{1,0:T(8,128)(2,1)}, bf16[1024,512]{1,0:T(8,128)(2,1)S(1)}, u32[]{:S(2)}) copy-start(bf16[1024,512]{1,0:T(8,128)(2,1)S(1)} %get-tuple-element.56.att_ref) | copy-start | bytes 3145732
  251.4 13.3 %collective-permute-start = (bf16[512,512]{1,0:T(8,128)(2,1)S(1)}, bf16[512,512]{1,0:T(8,128)(2,1)S(1)}, u32[]{:S(2)}, u32[]{:S(2)}) collective-permute-start(bf16[512,512]{1,0:T(8,128)(2,1)S(1)} %constant_dynamic-slice_fusion), channel_id=1, source_target_pairs={{0,4},{4,0},{8,12},{12,8},{16,20},{20,16},{24,28},{28,24},{1,5},{5... | collective-permute-start | bytes 1572872 | tf_op jit(solution)/shard_map/ppermute | solution.py:708
  252.3 11.6 %copy-start.12 = (bf16[2,1,256,1024]{3,2,1,0:T(8,128)(2,1)S(1)}, bf16[2,1,256,1024]{3,2,1,0:T(8,128)(2,1)}, u32[]{:S(2)}) copy-start(bf16[2,1,256,1024]{3,2,1,0:T(8,128)(2,1)} %get-tuple-element.57) | copy-start | bytes 3145732
  252.3 11.6 %copy-start.28 = (f32[1024]{0:T(1024)S(1)}, f32[1024]{0:T(1024)}, u32[]{:S(2)}) copy-start(f32[1024]{0:T(1024)} %param.33) | copy-start | bytes 12292
  264.7 2.2 copy-start.24
  266.9 4.5 copy-start.15
  269.1 28.0 %copy-start.8 = (f32[512,1024]{1,0:T(8,128)}, f32[512,1024]{1,0:T(8,128)S(1)}, u32[]{:S(2)}) copy-start(f32[512,1024]{1,0:T(8,128)S(1)} %get-tuple-element.89) | copy-start | bytes 6291460
  269.1 2.2 copy-start.30
  269.1 2.2 copy-start.31
  310.9 3.7 copy-start.11
  310.9 2.0 copy-start.13
  310.9 2.0 copy-start.29
  314.5 3.7 copy-start.9
  346.9 2.0 collective-permute-start.1
  347.2 2.8 copy-start.4
  487.6 179.7 %all-reduce.4.cloned.1.call-start = ((), (), s32[]{:S(2)}) async-start(), calls=%async_computation.1 | async-start | bytes 819200 | tf_op jit(solution)/shard_map/psum | solution.py:755
  487.7 2.7 copy-start.18
  490.4 1.3 copy-start.6
  490.4 1.9 copy-start.16
  492.3 4.2 copy-start.21
  493.6 2.9 copy-start.10
  493.8 3.6 copy-start.20
  493.8 2.7 collective-permute-start.2
  587.9 14.6 %copy-start.14 = (bf16[2,2,256,1024]{3,2,1,0:T(8,128)(2,1)S(1)}, bf16[2,2,256,1024]{3,2,1,0:T(8,128)(2,1)}, u32[]{:S(2)}) copy-start(bf16[2,2,256,1024]{3,2,1,0:T(8,128)(2,1)} %shard_map.204) | copy-start | bytes 6291460
  (5 other events, 4.9 us)
Sparse Core Ops, SparseCore 0:
  487.8 79.4 reduce-scatter.3
  602.6 64.6 all-reduce.3

commit v2 on v1

v2 whole, which is shorter than its diff:
```python
import functools
import math
import jax
import jax.numpy as jnp
from jax import lax
from jax.experimental import pallas as pl
from jax.experimental.pallas import tpu as pltpu
from jax.sharding import PartitionSpec as P

HD = 64
PAIR = 2 * HD
SLOTS = 128
QB = 256
KB = 256
NEG = -1e30
NT = (((1,), (1,)), ((), ()))


def mm(a, b):
    return jnp.dot(a, b, preferred_element_type=jnp.float32)


def mm_nt(a, b):
    return lax.dot_general(a, b, NT, preferred_element_type=jnp.float32)


def head_lanes(half):
    lane = lax.broadcasted_iota(jnp.int32, (1, PAIR), 1)
    return (lane >= half * HD) & (lane < (half + 1) * HD)


def only_head(a, half):
    return jnp.where(head_lanes(half), a, jnp.zeros_like(a))


def attend_block(q, keys, values, seg_col, seg_row, live_row):
    mixed = jnp.zeros((q.shape[0], PAIR), jnp.float32)
    totals = jnp.zeros((q.shape[0], PAIR), jnp.float32)
    lane = lax.broadcasted_iota(jnp.int32, (1, PAIR), 1)
    for half in range(2):
        qh = only_head(q, half) * jnp.asarray(0.125, jnp.bfloat16)
        scores = mm_nt(qh, keys)
        seq = jnp.where(seg_col == seg_row, scores[:, SLOTS:], NEG)
        pre = jnp.where(live_row > 0.5, scores[:, :SLOTS], NEG)
        top = jnp.maximum(
            jnp.max(seq, axis=1, keepdims=True), jnp.max(pre, axis=1, keepdims=True)
        )
        seq = jnp.exp(seq - top)
        pre = jnp.exp(pre - top)
        total = jnp.sum(seq, axis=1, keepdims=True) + jnp.sum(pre, axis=1, keepdims=True)
        scale = 1.0 / total
        low = jnp.concatenate([(pre * scale).astype(jnp.bfloat16), (seq * scale).astype(jnp.bfloat16)], axis=1)
        out = mm(low, values)
        mixed = jnp.where(head_lanes(half), out, mixed)
        totals = jnp.where(lane == half, top + jnp.log(total), totals)
    return mixed.astype(jnp.bfloat16), totals


def backward_kernel(
    bounds_ref, q_ref, k_ref, v_ref, do_ref, att_ref, pk_ref, pv_ref, lse_ref, meta_ref, seg_ref, live_ref,
    dq_ref, dk_ref, dv_ref, dpk_ref, dpv_ref,
    dk_acc, dv_acc, dpk_acc, dpv_acc, k_t, pk_t,
):
    length = q_ref.shape[0]
    dk_acc[...] = jnp.zeros_like(dk_acc)
    dv_acc[...] = jnp.zeros_like(dv_acc)
    dpk_acc[...] = jnp.zeros_like(dpk_acc)
    dpv_acc[...] = jnp.zeros_like(dpv_acc)
    k_t[...] = jnp.transpose(k_ref[...])
    pk_t[...] = jnp.transpose(pk_ref[...])
    picks = lax.broadcasted_iota(jnp.int32, (8, PAIR), 0)
    lanes = lax.broadcasted_iota(jnp.int32, (8, PAIR), 1) // HD
    picker = jnp.where(picks == lanes, 1.0, 0.0)

    def block(b, carry):
        start = pl.multiple_of(b * QB, QB)
        rows = pl.ds(start, QB)
        q = q_ref[rows, :]
        do = do_ref[rows, :]
        prod = do.astype(jnp.float32) * att_ref[rows, :].astype(jnp.float32)
        inner = lax.dot_general(
            picker, prod, NT, preferred_element_type=jnp.float32, precision=lax.Precision.HIGHEST
        )
        seg_q = meta_ref[0:1, pl.ds(SLOTS + start, QB)]
        heads = []
        for half in range(2):
            qh = only_head(q, half) * jnp.asarray(0.125, jnp.bfloat16)
            dh = only_head(do, half)
            lse = lse_ref[0, half : half + 1, rows]
            delta = inner[half : half + 1, :]
            heads.append((qh, dh, lse, delta))

        def tile(kk, vv, kt, allowed, half):
            qh, dh, lse, delta = heads[half]
            s = mm_nt(kk, qh)
            p = jnp.exp(jnp.where(allowed, s, NEG) - lse)
            dp = mm_nt(vv, dh)
            ds = (p * (dp - delta)).astype(jnp.bfloat16)
            return mm(ds, qh), mm(p.astype(jnp.bfloat16), dh), mm(kt, ds)

        dqs = []
        for half in range(2):
            a, g, dq = tile(
                pk_ref[...], pv_ref[...], pk_t[half * HD : (half + 1) * HD, :], live_ref[:, 0:1] > 0.5, half
            )
            dpk_acc[...] += a
            dpv_acc[...] += g
            dqs.append(dq)

        def step(j, dqs):
            at = pl.multiple_of(j * KB, KB)
            krows = pl.ds(at, KB)
            allowed = seg_ref[krows, 0:1] == seg_q
            dk = dk_acc[krows, :]
            dv = dv_acc[krows, :]
            outs = []
            for half in range(2):
                a, g, dq = tile(
                    k_ref[krows, :], v_ref[krows, :], k_t[half * HD : (half + 1) * HD, krows], allowed, half
                )
                dk = dk + a
                dv = dv + g
                outs.append(dqs[half] + dq)
            dk_acc[krows, :] = dk
            dv_acc[krows, :] = dv
            return tuple(outs)

        dqs = lax.fori_loop(bounds_ref[0, b], bounds_ref[1, b], step, tuple(dqs))
        dq_ref[rows, :] = (jnp.transpose(jnp.concatenate(dqs, axis=0)) * 0.125).astype(jnp.bfloat16)
        return carry

    lax.fori_loop(0, length // QB, block, 0)
    dk_ref[...] = dk_acc[...].astype(jnp.bfloat16)
    dv_ref[...] = dv_acc[...].astype(jnp.bfloat16)
    dpk_ref[...] = dpk_acc[...]
    dpv_ref[...] = dpv_acc[...]


def attend_backward(bounds, q, k, v, do, att, pk, pv, lse, meta, seg_col, live_col):
    length, width = q.shape
    pairs = width // PAIR
    block = pl.BlockSpec((length, PAIR), lambda p, *_: (0, p))
    pre = pl.BlockSpec((SLOTS, PAIR), lambda p, *_: (0, p))
    whole = lambda a: pl.BlockSpec(a.shape, lambda p, *_: (0,) * a.ndim)
    low = jax.ShapeDtypeStruct((length, width), jnp.bfloat16)
    full = jax.ShapeDtypeStruct((SLOTS, width), jnp.float32)
    return pl.pallas_call(
        backward_kernel,
        grid_spec=pltpu.PrefetchScalarGridSpec(
            num_scalar_prefetch=1,
            grid=(pairs,),
            in_specs=[
                block, block, block, block, block, pre, pre,
                pl.BlockSpec((1, 8, length), lambda p, *_: (p, 0, 0)),
                whole(meta), whole(seg_col), whole(live_col),
            ],
            out_specs=[block, block, block, pre, pre],
            scratch_shapes=[
                pltpu.VMEM((length, PAIR), jnp.float32),
                pltpu.VMEM((length, PAIR), jnp.float32),
                pltpu.VMEM((SLOTS, PAIR), jnp.float32),
                pltpu.VMEM((SLOTS, PAIR), jnp.float32),
                pltpu.VMEM((PAIR, length), jnp.bfloat16),
                pltpu.VMEM((PAIR, SLOTS), jnp.bfloat16),
            ],
        ),
        out_shape=[low, low, low, full, full],
        compiler_params=pltpu.CompilerParams(vmem_limit_bytes=48 * 2**20),
    )(bounds, q, k, v, do, att, pk, pv, lse, meta, seg_col, live_col)


def block_bounds(seg):
    length = seg.shape[0]
    first = seg[::QB]
    last = seg[QB - 1 :: QB]
    low = jnp.sum((seg[None, :] < first[:, None]).astype(jnp.int32), axis=1)
    high = jnp.sum((seg[None, :] <= last[:, None]).astype(jnp.int32), axis=1)
    return jnp.stack([low // KB, (high + KB - 1) // KB])


MESH = pl.DeviceIdType.MESH
LINE = 4
LANES = 128
WIDE = LINE * LANES
KINDS = 12
FIRST_UP = 4
CHUNK = 256


class Plan:
    def __init__(self, rows, tp):
        self.rows = rows
        self.tp = tp
        self.core_in_tp = tp > LINE
        self.shape = (rows // 8, 2, 4) if self.core_in_tp else (rows // 4, 2, 2)
        self.axes = (0, 1, 2) if self.core_in_tp else (0, 1)
        self.cores = 2 if self.core_in_tp else 1
        self.sides = 2 // self.cores

    def here(self):
        r = lax.axis_index("rows")
        t = lax.axis_index("tp")
        a, b, c = self.shape
        coords = (r // (b * c), lax.rem(r // c, b), lax.rem(r, c))
        if self.core_in_tp:
            return coords, t // 2, lax.rem(t, 2)
        return coords, t, coords[2]

    def device(self, coords, line, core):
        a, b, c = self.shape
        if self.core_in_tp:
            return ((coords[0] * b + coords[1]) * c + coords[2], line * 2 + core)
        return ((coords[0] * b + coords[1]) * c + core, line)

    def row_core(self, chip):
        return None if self.core_in_tp else chip // 2


def shifted(coords, axis, by, size):
    moved = list(coords)
    moved[axis] = lax.rem(coords[axis] + by, size)
    return tuple(moved)


def sibling(plan, place):
    coords, line, core = place
    return plan.device(coords, line, 1 - core)


def greet(plan, place):
    coords, line, core = place
    others = [
        plan.device(coords, lax.rem(line + by, LINE), side) for by in range(1, LINE) for side in range(2)
    ]
    others.append(sibling(plan, place))
    for axis in plan.axes:
        for by in range(1, plan.shape[axis]):
            others.append(plan.device(shifted(coords, axis, by, plan.shape[axis]), line, core))
    barrier = pltpu.get_barrier_semaphore()
    for other in others:
        pl.semaphore_signal(barrier, inc=1, device_id=other, device_id_type=MESH)
    pl.semaphore_wait(barrier, len(others))


def remote(src, dst, send, recv, device):
    return pltpu.make_async_remote_copy(
        src_ref=src, dst_ref=dst, send_sem=send, recv_sem=recv, device_id=device, device_id_type=MESH
    )


class Gather:
    def __init__(self, plan, place, source, whole, sems):
        self.plan = plan
        self.place = place
        self.coords, self.line, self.core = place
        self.source = source
        self.whole = whole
        self.sems = sems
        self.count = KINDS * plan.sides
        self.depth = source.shape[-2]
        self.orders = (plan.axes, plan.axes[::-1])
        self.lanes = pl.ds(pl.multiple_of(self.line * LANES, LANES), LANES)

    def unit(self, i):
        if self.plan.core_in_tp:
            return (i, self.core)
        return (i // 2, lax.rem(i, 2))

    def own_copies(self):
        where = tuple(self.coords) + (slice(None), self.lanes)
        for at in range(self.plan.sides):
            side = self.core if self.plan.core_in_tp else at
            yield pltpu.make_async_copy(
                self.source.at[:, at], self.whole.at[(slice(None), side) + where], self.sems["own"].at[at]
            )

    def line_copies(self, i):
        src = self.source.at[(i, 0) if self.plan.core_in_tp else self.unit(i)]
        dst = self.whole.at[self.unit(i) + tuple(self.coords) + (slice(None), self.lanes)]
        for by in range(1, LINE):
            yield remote(
                src, dst, self.sems["line_send"].at[i, by - 1], self.sems["line_recv"].at[i, by - 1],
                self.plan.device(self.coords, lax.rem(self.line + by, LINE), self.core),
            )

    def axis_copies(self, i, step):
        rows = self.depth // 2
        for half in range(2):
            order = self.orders[half]
            axis = order[step]
            size = self.plan.shape[axis]
            index = [
                pl.ds(0, self.plan.shape[a]) if a in order[:step] else self.coords[a] for a in range(3)
            ]
            block = self.whole.at[self.unit(i) + tuple(index) + (pl.ds(half * rows, rows),)]
            for by in range(1, size):
                spot = (i, half, step, by - 1)
                yield remote(
                    block, block, self.sems["axis_send"].at[spot], self.sems["axis_recv"].at[spot],
                    self.plan.device(shifted(self.coords, axis, by, size), self.line, self.core),
                )

    def core_copy(self, i, side):
        if self.plan.core_in_tp:
            block = self.whole.at[i, side]
        else:
            block = self.whole.at[self.unit(i) + (slice(None), slice(None), side)]
        return remote(
            block, block, self.sems["core_send"].at[i], self.sems["core_recv"].at[i], sibling(self.plan, self.place)
        )

    def core_roles(self, i):
        if self.plan.core_in_tp:
            wide = i >= 3
            return wide, wide
        side = lax.rem(i, 2)
        wide = i >= 6
        return wide | (side != self.core), wide | (side == self.core)

    def start_line(self, i):
        for copy in self.line_copies(i):
            copy.start()

    def start_axis(self, i, step):
        for copy in self.line_copies(i) if step == 0 else self.axis_copies(i, step - 1):
            copy.wait_recv()
        for copy in self.axis_copies(i, step):
            copy.start()

    def start_core(self, i):
        for copy in self.axis_copies(i, len(self.plan.axes) - 1):
            copy.wait_recv()
        sends, _ = self.core_roles(i)
        pl.when(sends)(lambda: self.core_copy(i, self.core).start())

    def finish(self, i):
        _, gets = self.core_roles(i)
        pl.when(gets)(lambda: self.core_copy(i, 1 - self.core).wait_recv())

    def drain(self, i):
        for copy in self.line_copies(i):
            copy.wait_send()
        for step in range(len(self.plan.axes)):
            for copy in self.axis_copies(i, step):
                copy.wait_send()
        sends, _ = self.core_roles(i)
        pl.when(sends)(lambda: self.core_copy(i, self.core).wait_send())

    def tick(self, i, ahead, lag):
        steps = len(self.plan.axes)

        def guarded(at, body):
            pl.when((at >= 0) & (at < self.count))(functools.partial(body, at))

        guarded(i + ahead, self.start_line)
        for step in range(steps):
            guarded(i - lag * step, lambda at, step=step: self.start_axis(at, step))
        guarded(i - lag * steps, self.start_core)

    def ticks(self, lag):
        return self.count + lag * len(self.plan.axes)


def gather_semaphores(plan):
    count = KINDS * plan.sides
    steps = len(plan.axes)
    reach = max(plan.shape[a] for a in plan.axes) - 1
    shapes = {
        "line_send": (count, LINE - 1),
        "line_recv": (count, LINE - 1),
        "axis_send": (count, 2, steps, reach),
        "axis_recv": (count, 2, steps, reach),
        "core_send": (count,),
        "core_recv": (count,),
        "own": (2,),
    }
    return {name: pltpu.SemaphoreType.DMA(shape) for name, shape in shapes.items()}


class Line:
    def __init__(self, plan, place, name, sems):
        self.plan = plan
        self.coords, self.line, self.core = place
        self.send_sems = sems[name + "_send"]
        self.recv_sems = sems[name + "_recv"]
        self.pieces = []

    def here(self, chip, side):
        return (chip == self.line) & (side == self.core)

    def send(self, src, dst, chip, side):
        at = len(self.pieces)
        far = remote(
            src, dst, self.send_sems.at[at], self.recv_sems.at[self.line, self.core],
            self.plan.device(self.coords, chip, side),
        )
        near = pltpu.make_async_copy(src, dst, self.send_sems.at[at])
        stays = self.here(chip, side)
        self.pieces.append((stays, far, near))
        pl.when(jnp.logical_not(stays))(far.start)
        pl.when(stays)(near.start)

    def settle(self):
        for stays, _, near in self.pieces:
            pl.when(stays)(near.wait)

    def drain(self):
        for stays, far, _ in self.pieces:
            pl.when(jnp.logical_not(stays))(far.wait_send)

    def receive(self, dst, chip, side):
        copy = remote(
            dst, dst, self.send_sems.at[0], self.recv_sems.at[chip, side],
            self.plan.device(self.coords, chip, side),
        )
        pl.when(jnp.logical_not(self.here(chip, side)))(copy.wait_recv)


def line_semaphores(name, count):
    return {
        name + "_send": pltpu.SemaphoreType.DMA((count,)),
        name + "_recv": pltpu.SemaphoreType.DMA((LINE, 2)),
    }


class Sibling:
    def __init__(self, plan, place, name, sems):
        self.sems = sems
        self.name = name
        self.device = sibling(plan, place)

    def copy(self, src, dst, at):
        return remote(src, dst, self.sems[self.name + "_send"].at[at], self.sems[self.name + "_recv"].at[at], self.device)


def sibling_semaphores(name, count):
    return {
        name + "_send": pltpu.SemaphoreType.DMA((count,)),
        name + "_recv": pltpu.SemaphoreType.DMA((count,)),
    }


def give_back_kernel(plan, names, parts, pieces, *sems):
    sems = dict(zip(names, sems))
    place = plan.here()
    coords, line, core = place
    greet(plan, place)
    places = pieces.shape[2]
    back = Line(plan, place, "back", sems)
    for half in range(2):
        for side in range(plan.cores):
            start = (half * plan.cores + side) * places
            if plan.core_in_tp:
                slot, target = line, side
            else:
                slot, target = lax.rem(line, 2), line // 2
            back.send(parts.at[:, pl.ds(start, places)], pieces.at[:, slot], 2 * core + half, target)
    back.settle()
    for j in range(pieces.shape[1]):
        chip = j if plan.core_in_tp else 2 * core + j
        back.receive(pieces.at[:, j], chip, line // 2)
    back.drain()


def give_back(plan, parts, held, places):
    sems = line_semaphores("back", 4)
    return pl.pallas_call(
        functools.partial(give_back_kernel, plan, tuple(sems)),
        out_shape=jax.ShapeDtypeStruct((parts.shape[0], held, places, parts.shape[2]), parts.dtype),
        in_specs=[pl.BlockSpec(memory_space=pl.ANY)],
        out_specs=pl.BlockSpec(memory_space=pl.ANY),
        scratch_shapes=list(sems.values()),
        compiler_params=pltpu.CompilerParams(collective_id=1, has_side_effects=True),
    )(parts)

def normalise(z):
    mean = jnp.mean(z, axis=1, keepdims=True)
    centred = z - mean
    rstd = lax.rsqrt(jnp.mean(centred * centred, axis=1, keepdims=True) + 1e-05)
    return centred * rstd, rstd


def normalise_grad(normal, rstd, gain, grad):
    g = grad * gain
    return rstd * (
        g - jnp.mean(g, axis=1, keepdims=True) - normal * jnp.mean(g * normal, axis=1, keepdims=True)
    )


def forward_inputs(plan, place, refs, scratch):
    coords, line, core = place
    source, prefix, meta = scratch["source"], scratch["prefix"], scratch["meta"]
    sides = plan.sides

    def put(kind, block, first):
        for side in range(sides):
            at = (first + side) * LANES
            source[kind, side] = block[:, at : at + LANES]

    put(0, refs["w_query"], 0)
    put(1, refs["w_key"], 0)
    put(2, refs["w_value"], 0)
    put(3, jnp.transpose(refs["w_attn_out"][...]), 0)
    down = jnp.transpose(refs["w_down"][...])
    for j in range((KINDS - FIRST_UP) // 2):
        put(FIRST_UP + 2 * j, refs["w_up"], j * sides)
        put(FIRST_UP + 2 * j + 1, down, j * sides)

    slots = refs["prefix_keys"].shape[1]
    prefix[...] = jnp.zeros_like(prefix)
    for j in range(refs["tokens"].shape[0]):
        task = refs["task_ids"][j]
        for which, name in enumerate(("prefix_keys", "prefix_values")):
            rows = refs[name][task]
            for side in range(sides):
                prefix[j, side, which, 0:slots, :] = rows[:, side * LANES : (side + 1) * LANES]

    mine = line if plan.core_in_tp else lax.rem(line, 2)
    task = refs["task_ids"][mine]
    meta[...] = jnp.zeros_like(meta)
    length = meta.shape[1] - SLOTS
    spots = lax.broadcasted_iota(jnp.int32, (1, length), 1)
    lane = lax.broadcasted_iota(jnp.int32, (1, SLOTS), 1)
    segment = jnp.zeros((1, length), jnp.float32)
    ends = jnp.zeros((1, SLOTS), jnp.float32)
    end = jnp.int32(0)
    for j in range(refs["lengths"].shape[1]):
        end = end + refs["lengths"][mine, j]
        segment = segment + jnp.where(spots >= end, 1.0, 0.0)
        ends = jnp.where(lane == j, end.astype(jnp.float32), ends)
    masks = refs["slot_masks"]
    used = jnp.zeros((1, slots), jnp.int32)
    limit = jnp.int32(0)
    for t in range(masks.shape[0]):
        used = jnp.where(task == t, masks[t : t + 1, :], used)
        limit = jnp.where(task == t, refs["prefix_lens"][t], limit)
    live = jnp.where((used == 1) & (lane[:, :slots] < limit), 1.0, 0.0)
    meta[0:1, 0:slots] = live
    meta[0:1, SLOTS:] = segment
    meta[1:2, 0:SLOTS] = jnp.where(lane == task, 1.0, 0.0)
    meta[2:3, 0:SLOTS] = ends


F_IN = (
    "task_ids", "lengths", "prefix_lens", "slot_masks", "tokens", "out_grad", "w_query", "w_key", "w_value",
    "w_attn_out", "w_up", "w_down", "gain_one", "shift_one", "gain_two", "shift_two", "prefix_keys",
    "prefix_values",
)
F_OUT = (
    "q_out", "k_out", "v_out", "att_out", "lse_out", "pre_out", "meta_out", "d_att_out", "d_first_out",
    "w_out", "pieces",
)
F_SCRATCH = (
    "source", "prefix", "meta", "whole", "row", "grad", "pre", "q", "k", "v", "att", "lse", "att_other",
    "keys", "values", "meta_cols", "normal_one", "rstd_one", "normed", "slope", "acc", "low", "out", "d_att",
    "d_att_away",
)
AHEAD = 3
LAG = 2


def forward_backward_kernel(plan, sem_names, *args):
    names = F_IN + F_OUT + F_SCRATCH + sem_names
    refs = dict(zip(names, args))
    sems = refs
    place = plan.here()
    coords, line, core = place
    bf16, f32 = jnp.bfloat16, jnp.float32
    spread = plan.core_in_tp
    tokens, row, grad, pre = refs["tokens"], refs["row"], refs["grad"], refs["pre"]
    whole, meta = refs["whole"], refs["meta"]
    q, k, v, att, lse = (refs[n] for n in ("q", "k", "v", "att", "lse"))
    held = tokens.shape[0]
    width = row.shape[-1]
    length = q.shape[0]
    half = length // 2
    base = 0 if spread else 2 * core
    slot = core if spread else 0
    holds = None if spread else line // 2 == core

    forward_inputs(plan, place, refs, refs)
    greet(plan, place)

    gather = Gather(plan, place, refs["source"], whole, sems)
    gather.start_line(0)
    gather.start_line(1)
    token_line = Line(plan, place, "token", sems)
    for j in range(held):
        token_line.send(tokens.at[j], row.at[line, slot], base + j, core)
    for copy in gather.own_copies():
        copy.start()
    for i in range(2, AHEAD):
        gather.start_line(i)
    prefix_line = Line(plan, place, "prefix", sems)
    for j in range(held):
        for side in range(plan.sides):
            prefix_line.send(
                refs["prefix"].at[j, side], pre.at[:, :, gather.lanes], base + j, core if spread else side
            )
    share = Sibling(plan, place, "share", sems)
    meta_copy = share.copy(meta, meta, 4)
    if not spread:
        pl.when(holds)(meta_copy.start)
    for copy in gather.own_copies():
        copy.wait()

    last = gather.ticks(LAG)

    def beat(i, x=0):
        gather.tick(i, AHEAD, LAG)
        return x

    steps = LAG * len(plan.axes) + 1
    done = min(last, steps)
    lax.fori_loop(0, done, beat, 0)

    token_line.settle()

    def share_token(chip):
        if spread:
            token_line.receive(row.at[chip, core], chip, core)
            share.copy(row.at[chip, core], row.at[chip, core], chip).start()
        else:
            @pl.when(holds)
            def _():
                token_line.receive(row.at[chip, 0], chip, core)
                share.copy(row.at[chip, 0], row.at[chip, 0], chip).start()

    for chip in range(LINE):
        share_token(chip)
    grad_line = Line(plan, place, "grad", sems)
    for j in range(held):
        grad_line.send(refs["out_grad"].at[j], grad.at[lax.rem(line, 2), slot], base + j, line // 2)
    for chip in range(LINE):
        if spread:
            share.copy(row.at[chip, 1 - core], row.at[chip, 1 - core], chip).wait_recv()
        else:
            pl.when(jnp.logical_not(holds))(share.copy(row.at[chip, 0], row.at[chip, 0], chip).wait_recv)
    if not spread:
        pl.when(jnp.logical_not(holds))(meta_copy.wait_recv)
    prefix_line.settle()
    for chip in range(LINE):
        prefix_line.receive(pre.at[:, :, pl.ds(chip * LANES, LANES)], chip, core if spread else line // 2)
    refs["meta_cols"][...] = jnp.transpose(meta[...])

    def publish(name, out, at):
        return pltpu.make_async_copy(refs[name], refs[out], sems["publish"].at[at])

    def ready(first, amount, done):
        until = min(last, first + amount - 1 + steps)
        if until > done:
            lax.fori_loop(done, until, beat, 0)
        for i in range(first, first + amount):
            gather.finish(i)
        return max(done, until)

    for kind, target in enumerate((q, k, v)):
        done = ready(kind * plan.sides, plan.sides, done)
        weight = whole.at[kind, core]

        def project(b, x, weight=weight, target=target):
            block = row[b].reshape(CHUNK, width)
            target[pl.ds(pl.multiple_of(b * CHUNK, CHUNK), CHUNK), :] = mm(
                block, weight[...].reshape(width, WIDE)
            ).astype(bf16)
            return x

        lax.fori_loop(0, LINE, project, 0)
    keep = [publish(n, n + "_out", at) for at, n in enumerate(("q", "k", "v", "pre", "meta"))]
    keep.append(pltpu.make_async_copy(whole.at[pl.ds(0, 3), core], refs["w_out"], sems["publish"].at[5]))
    for copy in keep:
        copy.start()

    att_share = Sibling(plan, place, "att", sems)
    here = pl.ds(pl.multiple_of(core * half, half), half)
    there = pl.ds(pl.multiple_of((1 - core) * half, half), half)
    keys, values = refs["keys"], refs["values"]
    blocks = length // QB

    def att_copy(p):
        lanes = pl.ds(pl.multiple_of(p * PAIR, PAIR), PAIR)
        return att_share.copy(att.at[there, lanes], refs["att_other"].at[:, lanes], p)

    def pair(p, x):
        lanes = pl.ds(pl.multiple_of(p * PAIR, PAIR), PAIR)
        keys[0:SLOTS, :] = pre[0, :, lanes]
        keys[SLOTS:, :] = k[:, lanes]
        values[0:SLOTS, :] = pre[1, :, lanes]
        values[SLOTS:, :] = v[:, lanes]

        def block(b, x):
            rows = pl.ds(pl.multiple_of(b * QB, QB), QB)
            mixed, totals = attend_block(
                q[rows, lanes], keys[...], values[...],
                refs["meta_cols"][pl.ds(pl.multiple_of(SLOTS + b * QB, SLOTS), QB), 0:1],
                meta[0:1, SLOTS:], meta[0:1, :SLOTS],
            )
            att[rows, lanes] = mixed
            lse[p, :, rows] = jnp.transpose(totals)[0:8, :]
            return x

        lax.fori_loop(0, blocks // 2, block, 0)
        beat(done + plan.sides * p)
        lax.fori_loop(blocks // 2, blocks, block, 0)
        if plan.sides > 1:
            beat(done + plan.sides * p + 1)
        att_copy(p).start()
        return x

    pairs = WIDE // PAIR
    lax.fori_loop(0, pairs, pair, 0)
    done = min(last, done + plan.sides * pairs)
    keep += [publish(n, n + "_out", 6 + at) for at, n in enumerate(("att", "lse"))]
    for copy in keep[-2:]:
        copy.start()
    for p in range(pairs):
        att_copy(p).wait_recv()

    done = ready(3 * plan.sides, plan.sides, done)
    normal_one, rstd_one, normed, acc = (refs[n] for n in ("normal_one", "rstd_one", "normed", "acc"))
    low, slope, out = refs["low"], refs["slope"], refs["out"]
    parts = half // CHUNK

    def weight(kind, side):
        return whole[kind, side].reshape(width, WIDE)

    def mix(b, x):
        rows = pl.ds(pl.multiple_of(b * CHUNK, CHUNK), CHUNK)
        own = att[pl.ds(pl.multiple_of(core * half + b * CHUNK, CHUNK), CHUNK), :]
        total = row[2 * core + b].reshape(CHUNK, width).astype(f32)
        total = total + mm_nt(own, weight(3, core)) + mm_nt(refs["att_other"][rows, :], weight(3, 1 - core))
        normal, rstd = normalise(total)
        normal_one[rows, :] = normal
        rstd_one[rows, :] = jnp.broadcast_to(rstd, (CHUNK, LANES))
        low_normed = (normal * refs["gain_one"][...] + refs["shift_one"][...]).astype(bf16)
        normed[rows, :] = low_normed
        acc[rows, :] = low_normed.astype(f32)
        return x

    lax.fori_loop(0, parts, mix, 0)

    def feed(n, x):
        j, side = n // 2, lax.rem(n, 2)
        kind = FIRST_UP + 2 * j

        def part(b, x):
            rows = pl.ds(pl.multiple_of(b * CHUNK, CHUNK), CHUNK)
            upper = mm(normed[rows, :], weight(kind, side))
            bell = (1.0 + lax.erf(upper * (0.5**0.5))) * 0.5
            acted = (upper * bell).astype(bf16)
            slope[n, rows, :] = (
                bell + upper * jnp.exp(upper * upper * -0.5) * (1.0 / (2.0 * math.pi) ** 0.5)
            ).astype(bf16)
            acc[rows, :] += mm_nt(acted, weight(kind + 1, side))
            return x

        lax.fori_loop(0, parts, part, 0)
        return x

    groups = (KINDS - FIRST_UP) // 2
    for j in range(groups):
        done = ready((FIRST_UP + 2 * j) * plan.sides, 2 * plan.sides, done)
        lax.fori_loop(2 * j, 2 * j + 2, feed, 0)

    grad_line.settle()
    for part in range(2):
        for side in range(plan.cores):
            grad_line.receive(grad.at[part, side], 2 * core + part, side if spread else line // 2)

    back = Line(plan, place, "back", sems)
    places = tokens.shape[1]

    def close(b, x):
        rows = pl.ds(pl.multiple_of(b * CHUNK, CHUNK), CHUNK)
        normal, rstd = normalise(acc[rows, :])
        out[rows, :] = (normal * refs["gain_two"][...] + refs["shift_two"][...]).astype(bf16)
        d_second = normalise_grad(
            normal, rstd, refs["gain_two"][...], grad[b].reshape(CHUNK, width).astype(f32)
        )
        acc[rows, :] = d_second
        low[rows, :] = d_second.astype(bf16)
        return x

    lax.fori_loop(0, parts, close, 0)
    for b in range(2):
        for side in range(plan.cores):
            spot, target = (line, side) if spread else (lax.rem(line, 2), line // 2)
            back.send(
                out.at[pl.ds((b * plan.cores + side) * places, places)], refs["pieces"].at[spot],
                2 * core + b, target,
            )

    def feed_back(n, x):
        j, side = n // 2, lax.rem(n, 2)
        kind = FIRST_UP + 2 * j

        def part(b, x):
            rows = pl.ds(pl.multiple_of(b * CHUNK, CHUNK), CHUNK)
            d_acted = mm(low[rows, :], weight(kind + 1, side))
            d_upper = (d_acted * slope[n, rows, :].astype(f32)).astype(bf16)
            acc[rows, :] += mm_nt(d_upper, weight(kind, side))
            return x

        lax.fori_loop(0, parts, part, 0)
        return x

    lax.fori_loop(0, 2 * groups, feed_back, 0)

    d_att, away = refs["d_att"], refs["d_att_away"]
    d_share = Sibling(plan, place, "d_att", sems)

    def d_copy(b):
        mine = pl.ds(pl.multiple_of(core * half + b * CHUNK, CHUNK), CHUNK)
        return d_share.copy(away.at[pl.ds(pl.multiple_of(b * CHUNK, CHUNK), CHUNK)], d_att.at[mine], b)

    def open_(b, x):
        rows = pl.ds(pl.multiple_of(b * CHUNK, CHUNK), CHUNK)
        d_first = normalise_grad(normal_one[rows, :], rstd_one[rows, 0:1], refs["gain_one"][...], acc[rows, :])
        acc[rows, :] = d_first
        d_low = d_first.astype(bf16)
        away[rows, :] = mm(d_low, weight(3, 1 - core)).astype(bf16)
        d_copy(b).start()
        mine = pl.ds(pl.multiple_of(core * half + b * CHUNK, CHUNK), CHUNK)
        d_att[mine, :] = mm(d_low, weight(3, core)).astype(bf16)
        return x

    lax.fori_loop(0, parts, open_, 0)
    keep.append(publish("acc", "d_first_out", 8))
    keep[-1].start()
    for b in range(parts):
        d_copy(b).wait_recv()
    keep.append(publish("d_att", "d_att_out", 9))
    keep[-1].start()

    lax.fori_loop(0, gather.count, lambda i, x: (gather.drain(i), x)[1], 0)
    token_line.drain()
    prefix_line.drain()
    grad_line.drain()
    for chip in range(LINE):
        if spread:
            share.copy(row.at[chip, core], row.at[chip, core], chip).wait_send()
        else:
            pl.when(holds)(share.copy(row.at[chip, 0], row.at[chip, 0], chip).wait_send)
    if not spread:
        pl.when(holds)(meta_copy.wait_send)
    for p in range(pairs):
        att_copy(p).wait_send()
    for b in range(parts):
        d_copy(b).wait_send()
    back.settle()
    for j in range(held):
        back.receive(refs["pieces"].at[j], j if spread else 2 * core + j, line // 2)
    back.drain()
    for copy in keep:
        copy.wait()


def forward_backward(plan, task_ids, lengths, prefix_lens, slot_masks, *rest):
    tokens, _, w_query = rest[:3]
    held, places, width = tokens.shape
    depth = w_query.shape[0]
    length = places * plan.tp
    half = length // 2
    pairs = WIDE // PAIR
    bf16, f32 = jnp.bfloat16, jnp.float32
    S = jax.ShapeDtypeStruct
    outs = {
        "q_out": S((length, WIDE), bf16),
        "k_out": S((length, WIDE), bf16),
        "v_out": S((length, WIDE), bf16),
        "att_out": S((length, WIDE), bf16),
        "lse_out": S((pairs, 8, length), f32),
        "pre_out": S((2, SLOTS, WIDE), bf16),
        "meta_out": S((8, SLOTS + length), f32),
        "d_att_out": S((length, WIDE), bf16),
        "d_first_out": S((half, width), f32),
        "w_out": S((3,) + plan.shape + (depth, WIDE), bf16),
        "pieces": S((held, places, width), bf16),
    }
    units = 2 * (KINDS - FIRST_UP) // 2
    scratch = {
        "source": ((KINDS, plan.sides, depth, LANES), bf16),
        "prefix": ((held, plan.sides, 2, SLOTS, LANES), bf16),
        "meta": ((8, SLOTS + length), f32),
        "whole": ((KINDS, 2) + plan.shape + (depth, WIDE), bf16),
        "row": ((LINE, plan.cores, places, width), bf16),
        "grad": ((2, plan.cores, places, width), bf16),
        "pre": ((2, SLOTS, WIDE), bf16),
        "q": ((length, WIDE), bf16),
        "k": ((length, WIDE), bf16),
        "v": ((length, WIDE), bf16),
        "att": ((length, WIDE), bf16),
        "lse": ((pairs, 8, length), f32),
        "att_other": ((half, WIDE), bf16),
        "keys": ((SLOTS + length, PAIR), bf16),
        "values": ((SLOTS + length, PAIR), bf16),
        "meta_cols": ((SLOTS + length, 8), f32),
        "normal_one": ((half, width), f32),
        "rstd_one": ((half, LANES), f32),
        "normed": ((half, width), bf16),
        "slope": ((units, half, WIDE), bf16),
        "acc": ((half, width), f32),
        "low": ((half, width), bf16),
        "out": ((half, width), bf16),
        "d_att": ((length, WIDE), bf16),
        "d_att_away": ((half, WIDE), bf16),
    }
    sems = gather_semaphores(plan)
    for name, amount in (("token", held), ("prefix", held * plan.sides), ("grad", held), ("back", 4)):
        sems.update(line_semaphores(name, amount))
    for name, amount in (("share", 5), ("att", pairs), ("d_att", half // CHUNK)):
        sems.update(sibling_semaphores(name, amount))
    sems["publish"] = pltpu.SemaphoreType.DMA((10,))
    smem = pl.BlockSpec(memory_space=pltpu.SMEM)
    vmem = pl.BlockSpec(memory_space=pltpu.VMEM)
    hbm = pl.BlockSpec(memory_space=pl.ANY)
    results = pl.pallas_call(
        functools.partial(forward_backward_kernel, plan, tuple(sems)),
        out_shape=[outs[n] for n in F_OUT],
        in_specs=[smem, smem, smem, vmem, hbm, hbm] + [vmem] * 12,
        out_specs=[hbm] * len(F_OUT),
        scratch_shapes=[pltpu.VMEM(*scratch[n]) for n in F_SCRATCH] + list(sems.values()),
        compiler_params=pltpu.CompilerParams(
            collective_id=0, has_side_effects=True, vmem_limit_bytes=62 * 2**20
        ),
    )(task_ids, lengths, prefix_lens, slot_masks, *rest)
    return dict(zip(F_OUT, results))


def shards(
    plan, tokens, w_query, w_key, w_value, w_attn_out, w_up, w_down, first_gain, first_shift,
    second_gain, second_shift, prefix_keys, prefix_values, example_lengths, task_ids, prefix_lens,
    slot_masks, out_grad,
):
    f32, bf16 = jnp.float32, jnp.bfloat16
    held, places, width = tokens.shape
    tasks, slots, part = prefix_keys.shape
    length = places * plan.tp
    _, line, core = plan.here()
    half = length // 2
    done = forward_backward(
        plan, task_ids, example_lengths, prefix_lens, slot_masks, tokens, out_grad, w_query, w_key, w_value,
        w_attn_out, w_up, w_down, first_gain[None], first_shift[None], second_gain[None], second_shift[None],
        prefix_keys, prefix_values,
    )
    q, k, v, att, lse, pre, row_meta, d_att, d_first = (
        done[n + "_out"] for n in ("q", "k", "v", "att", "lse", "pre", "meta", "d_att", "d_first")
    )
    w_q, w_k, w_v = (done["w_out"][i].reshape(width, WIDE) for i in range(3))

    def pick(a, which):
        return lax.dynamic_slice_in_dim(a, which * half, half, 0)

    def swap(a):
        if plan.core_in_tp:
            return lax.ppermute(a, "tp", [(i, i ^ 1) for i in range(plan.tp)])
        return lax.ppermute(a, "rows", [(i, i ^ 1) for i in range(plan.rows)])

    seg = row_meta[0, SLOTS:]
    seg_col = jnp.broadcast_to(seg[:, None], (length, LANES))
    live_col = jnp.broadcast_to(row_meta[0, :SLOTS][:, None], (SLOTS, LANES))
    bounds = block_bounds(seg.astype(jnp.int32))
    dq, dk, dv, dpk, dpv = attend_backward(
        bounds, q, k, v, d_att, att, pre[0], pre[1], lse, row_meta, seg_col, live_col
    )
    shares = mm_nt(dq, w_q) + mm_nt(dk, w_k) + mm_nt(dv, w_v)
    other = swap(pick(shares, 1 - core).astype(bf16)).astype(f32)
    d_tokens = d_first + pick(shares, core) + other
    back = give_back(plan, d_tokens.astype(bf16)[None], held, places)

    d_pre = jnp.stack([dpk, dpv])[:, :slots].reshape(2, slots, LINE, LANES)
    side = (jnp.arange(2) == core).astype(f32)
    d_pre = row_meta[1, :tasks][None, :, None, None, None, None] * (
        d_pre[:, None, :, :, None, :] * side[None, None, None, None, :, None]
    )
    d_pre = d_pre.reshape(2, tasks, slots, width).astype(bf16)
    d_pre = lax.psum_scatter(d_pre, "tp", scatter_dimension=3, tiled=True)
    d_pre = lax.psum(d_pre, "rows").astype(f32)
    return done["pieces"], back[0].astype(f32), d_pre[0], d_pre[1]


def solution(mesh):
    placed = (
        P("rows", "tp", None),
        P("rows", "tp"),
        P("rows", "tp"),
        P("rows", "tp"),
        P("tp", "rows"),
        P("rows", "tp"),
        P("tp", "rows"),
        P(),
        P(),
        P(),
        P(),
        P(None, None, "tp"),
        P(None, None, "tp"),
        P("rows", None),
        P("rows"),
        P(),
        P(),
        P("rows", "tp", None),
    )
    plan = Plan(mesh.shape["rows"], mesh.shape["tp"])
    return jax.shard_map(
        functools.partial(shards, plan),
        mesh=mesh,
        in_specs=placed,
        out_specs=(
            P("rows", "tp", None),
            P("rows", "tp", None),
            P(None, None, "tp"),
            P(None, None, "tp"),
        ),
        check_vma=False,
    )
```

time: 689 us -> 528 us (0.77); the launches traced: 677 us -> 523 us
  matrix products: 86.8 us -> 5.8 us
  Pallas kernels: 320 us -> 286 us
  local copies, waits for them, and re-layouts: 164 us -> 146 us
  other arithmetic: 22.6 us -> 11.2 us
    dot_general x8 -> x0, matrix products: 77.3 us -> none  [the longest x1 25.8 us: shards(): upper = jnp.einsum('pd,udf->upf', normed, up, preferred_element_type=f32)]
    pallas_call x1, Pallas kernels: 74.1 us -> 42.4 us  [give_back(): pl.pallas_call(functools.partial(give_back_kernel, plan, tuple(sems)), ou...]
    slice x2 -> x1, local copies, waits for them, and re-layouts: 17.6 us -> 2.1 us  [shards(): w_q, w_k, w_v = (done['w_out'][i].reshape(width, WIDE) for i in range(3))]
    pallas_call x2 -> x1, Pallas kernels: 208 us -> 196 us  [forward_backward(): pl.pallas_call(functools.partial(forward_backward_kernel, plan, tuple(sem...]
    pallas_call x1, Pallas kernels: 37.2 us -> 47.5 us  [attend_backward(): pl.pallas_call(backward_kernel, grid_spec=pltpu.PrefetchScalarGridSpec(nu...]
    another operation x7 -> x0, other arithmetic: 8.24 us -> none  [the longest x3 3.98 us: shards(): jnp.stack([output, d_tokens.astype(bf16)])]
    unnamed x85 -> x21, local copies, waits for them, and re-layouts: 135 us -> 131 us
  transfers between devices with their start and end apart: 5 -> 3, of which waited for: 3 -> 2; matrix products, arithmetic and copies ran while one was open for 3% -> 3% of each run, Pallas kernels for 11% -> 8%
where the time goes in v2:
time: 528 us; the launch traced here: 523 us
  Pallas kernels  286 us (54%)
  local copies, waits for them, and re-layouts  146 us (28%)
  waiting for transfers between devices  60.5 us (11%)
  between operations  14.2 us (3%)
  other arithmetic  11.2 us (2%)
  matrix products  5.8 us (1%)
    pallas_call x1, Pallas kernels, forward_backward(): pl.pallas_call(functools.partial(forward_backward_kernel, plan, tuple(sem...  196 us
    unnamed x21, local copies, waits for them, and re-layouts  131 us
    psum x1, waiting for transfers between devices, shards(): d_pre = lax.psum(d_pre, 'rows').astype(f32)  57.6 us
    pallas_call x1, Pallas kernels, attend_backward(): pl.pallas_call(backward_kernel, grid_spec=pltpu.PrefetchScalarGridSpec(nu...  47.5 us
    pallas_call x1, Pallas kernels, give_back(): pl.pallas_call(functools.partial(give_back_kernel, plan, tuple(sems)), ou...  42.4 us
  transfers between devices with their start and end apart: 3, of which 2 were waited for; matrix products, arithmetic and copies ran while one was open for 3% of the time, Pallas kernels for 8%

profile of v2, /device:TPU:0, one launch (start us, length us, event | category | flops | bytes accessed | tf_op | source)
XLA Modules:
  0.0 523.0 jit_solution(2657555304304512623)
XLA Ops:
  7.2 1.6 copy.28.args_16_
  8.9 1.6 copy.29.args_17_
  10.5 195.7 %shard_map.201 = (bf16[1024,512]{1,0:T(8,128)(2,1)}, bf16[1024,512]{1,0:T(8,128)(2,1)}, bf16[1024,512]{1,0:T(8,128)(2,1)}, bf16[1024,512]{1,0:T(8,128)(2,1)}, f3...) custom-call(s32[2]{0:T(128)} %args_0_.4, ...), custom_call_target="tpu_custom_call" | custom-call | tf_op jit(solution)/shard_map/pallas_call | solution.py:917
  206.2 1.2 slice_bitcast_fusion.4
  209.5 1.0 slice_bitcast_fusion.2
  211.0 1.2 copy-done
  212.3 0.9 copy-done.1
  213.2 0.8 copy-done.2
  213.9 47.5 %shard_map.202 = (bf16[1024,512]{1,0:T(8,128)(2,1)S(1)}, bf16[1024,512]{1,0:T(8,128)(2,1)S(1)}, bf16[1024,512]{1,0:T(8,128)(2,1)S(1)}, f32[128,512]{1,0:T(8,128)S(1)}, f32[128,512]{1,0:T(8,128)S(1)}) custom-call(s32[2,4]{1,0:T(2,128)S(1)} %pad_add_fusion.bounds_ref, bf16[1024,512]{1,0:T(8,128)(2,1)S(1)} %copy-done, ...), custom_call_target="tpu_custom_call" | custom-call | tf_op jit(solution)/shard_map/pallas_call | solution.py:147
  261.5 0.8 pad_maximum_fusion
  262.2 1.1 mul.52
  263.4 1.2 mul.53
  264.6 2.7 mul.54
  268.0 1.2 broadcast_multiply_fusion
  269.3 1.8 multiply_convert_fusion
  271.1 42.3 %copy.30 = bf16[2,4,100,1024]{1,2,0,3:T(8,128)(2,1)} copy(bf16[2,4,100,1024]{3,1,2,0:T(4,128)(2,1)} %multiply_convert_fusion) | data formatting | bytes 3276800
  313.4 51.4 %reshape.136 = bf16[1024,800]{1,0:T(8,128)(2,1)} reshape(bf16[1024,2,100,4]{3,2,1,0:T(8,128)(2,1)} %bitcast.56) | data formatting | bytes 3276800
  364.9 2.1 fusion.1
  367.0 1.3 fusion.4
  368.3 1.3 fusion.3
  369.6 3.2 add_add_fusion
  372.8 2.9 dynamic-slice_convert_fusion
  375.7 2.9 collective-permute-done
  378.6 3.2 fusion.parts
  381.7 42.4 %shard_map.203 = bf16[1,2,256,1024]{3,2,1,0:T(8,128)(2,1)} custom-call(bf16[1,512,1024]{2,1,0:T(8,128)(2,1)} %fusion.parts), custom_call_target="tpu_custom_call" | custom-call | tf_op jit(solution)/shard_map/pallas_call | solution.py:467
  424.1 15.1 %reshape.137 = bf16[256,2,100,4]{3,2,1,0:T(8,128)(2,1)} reshape(bf16[256,800]{1,0:T(8,128)(2,1)} %reduce-scatter.4.cloned.1.call-done) | data formatting | bytes 819200
  439.3 14.5 %copy.31 = bf16[2,4,100,256]{3,1,2,0:T(4,128)(2,1)} copy(bf16[2,4,100,256]{1,2,0,3:T(8,128)(2,1)} %bitcast.57) | data formatting | bytes 819200
  453.8 1.6 bitcast_convert_fusion
  455.4 57.6 %all-reduce.2.cloned.1.call-done = bf16[2,4,100,256]{3,1,2,0:T(4,128)(2,1)} async-done(((bf16[2,4,100,256]{3,1,2,0:T(4,128)(2,1)}), bf16[2,4,100,256]{3,1,2,0:T(4,128)(2,1)}) %all-reduce.2.cloned.1.call-update) | async-done | bytes 409616 | tf_op jit(solution)/shard_map/psum | solution.py:978
  513.0 1.2 convert_element_type.51
  514.1 1.0 slice_bitcast_fusion
  515.2 1.0 copy.34
  (29 shorter events, 3.5 us)
Async XLA Ops:
  7.2 417.0 %reduce-scatter.4.cloned.1.call-start = ((), (), s32[]{:S(2)}) async-start(), calls=%async_computation.2 | async-start | bytes 2293760
  211.0 1.2 copy-start
  212.3 0.9 copy-start.1
  213.2 0.8 copy-start.2
  264.6 4.7 copy-start.6
  364.9 148.1 %all-reduce.2.cloned.1.call-start = ((), (), s32[]{:S(2)}) async-start(), calls=%async_computation.1 | async-start | bytes 819200 | tf_op jit(solution)/shard_map/psum | solution.py:978
  372.8 5.8 %copy-start.4 = (f32[512,1024]{1,0:T(8,128)S(1)}, f32[512,1024]{1,0:T(8,128)}, u32[]{:S(2)}) copy-start(f32[512,1024]{1,0:T(8,128)} %get-tuple-element.21) | copy-start | bytes 6291460
  375.7 2.9 collective-permute-start
  439.3 14.5 %copy-start.3 = (bf16[1,2,256,1024]{3,2,1,0:T(8,128)(2,1)S(1)}, bf16[1,2,256,1024]{3,2,1,0:T(8,128)(2,1)}, u32[]{:S(2)}) copy-start(bf16[1,2,256,1024]{3,2,1,0:T(8,128)(2,1)} %shard_map.203) | copy-start | bytes 3145732
  453.8 61.4 %copy-start.5 = (bf16[2,256,1024]{2,1,0:T(8,128)(2,1)S(1)}, bf16[2,256,1024]{2,1,0:T(8,128)(2,1)}, u32[]{:S(2)}) copy-start(bf16[2,256,1024]{2,1,0:T(8,128)(2,1)} %get-tuple-element.53) | copy-start | bytes 3145732
Sparse Core Ops, SparseCore 0:
  365.0 57.7 reduce-scatter.3
  453.9 59.0 all-reduce.1

commit v3 on v2

--- a/solution.py
+++ b/solution.py
@@ -1,5 +1,7 @@
 import functools
 import math
+from types import SimpleNamespace
+
 import jax
 import jax.numpy as jnp
 from jax import lax
@@ -57,11 +59,18 @@
 
 
 def backward_kernel(
-    bounds_ref, q_ref, k_ref, v_ref, do_ref, att_ref, pk_ref, pv_ref, lse_ref, meta_ref, seg_ref, live_ref,
-    dq_ref, dk_ref, dv_ref, dpk_ref, dpv_ref,
-    dk_acc, dv_acc, dpk_acc, dpv_acc, k_t, pk_t,
+    examples, ends_ref, q_ref, k_ref, v_ref, do_ref, att_ref, pre_ref, lse_ref, meta_ref,
+    dq_ref, dk_ref, dv_ref, dpre_ref,
+    dk_acc, dv_acc, dpk_acc, dpv_acc, k_t, pk_t, columns,
 ):
     length = q_ref.shape[0]
+    pk_ref, pv_ref = pre_ref.at[0], pre_ref.at[1]
+    live_ref, seg_ref = columns.at[0:SLOTS], columns.at[SLOTS:]
+
+    @pl.when(pl.program_id(0) == 0)
+    def _():
+        columns[...] = jnp.transpose(meta_ref[...])
+
     dk_acc[...] = jnp.zeros_like(dk_acc)
     dv_acc[...] = jnp.zeros_like(dv_acc)
     dpk_acc[...] = jnp.zeros_like(dpk_acc)
@@ -71,6 +80,14 @@
     picks = lax.broadcasted_iota(jnp.int32, (8, PAIR), 0)
     lanes = lax.broadcasted_iota(jnp.int32, (8, PAIR), 1) // HD
     picker = jnp.where(picks == lanes, 1.0, 0.0)
+
+    def bounds(start):
+        low, high = jnp.int32(0), jnp.int32(length)
+        for j in range(examples):
+            end = ends_ref[2, j].astype(jnp.int32)
+            low = jnp.where(end <= start, jnp.maximum(low, end), low)
+            high = jnp.where(end >= start + QB, jnp.minimum(high, end), high)
+        return low // KB, (high + KB - 1) // KB
 
     def block(b, carry):
         start = pl.multiple_of(b * QB, QB)
@@ -125,57 +142,45 @@
             dv_acc[krows, :] = dv
             return tuple(outs)
 
-        dqs = lax.fori_loop(bounds_ref[0, b], bounds_ref[1, b], step, tuple(dqs))
+        dqs = lax.fori_loop(*bounds(start), step, tuple(dqs))
         dq_ref[rows, :] = (jnp.transpose(jnp.concatenate(dqs, axis=0)) * 0.125).astype(jnp.bfloat16)
         return carry
 
     lax.fori_loop(0, length // QB, block, 0)
     dk_ref[...] = dk_acc[...].astype(jnp.bfloat16)
     dv_ref[...] = dv_acc[...].astype(jnp.bfloat16)
-    dpk_ref[...] = dpk_acc[...]
-    dpv_ref[...] = dpv_acc[...]
-
-
-def attend_backward(bounds, q, k, v, do, att, pk, pv, lse, meta, seg_col, live_col):
+    dpre_ref[0] = dpk_acc[...]
+    dpre_ref[1] = dpv_acc[...]
+
+
+def attend_backward(examples, q, k, v, do, att, pre, lse, meta):
     length, width = q.shape
     pairs = width // PAIR
-    block = pl.BlockSpec((length, PAIR), lambda p, *_: (0, p))
-    pre = pl.BlockSpec((SLOTS, PAIR), lambda p, *_: (0, p))
-    whole = lambda a: pl.BlockSpec(a.shape, lambda p, *_: (0,) * a.ndim)
+    block = pl.BlockSpec((length, PAIR), lambda p: (0, p))
+    pre_block = pl.BlockSpec((2, SLOTS, PAIR), lambda p: (0, 0, p))
     low = jax.ShapeDtypeStruct((length, width), jnp.bfloat16)
-    full = jax.ShapeDtypeStruct((SLOTS, width), jnp.float32)
     return pl.pallas_call(
-        backward_kernel,
-        grid_spec=pltpu.PrefetchScalarGridSpec(
-            num_scalar_prefetch=1,
-            grid=(pairs,),
-            in_specs=[
-                block, block, block, block, block, pre, pre,
-                pl.BlockSpec((1, 8, length), lambda p, *_: (p, 0, 0)),
-                whole(meta), whole(seg_col), whole(live_col),
-            ],
-            out_specs=[block, block, block, pre, pre],
-            scratch_shapes=[
-                pltpu.VMEM((length, PAIR), jnp.float32),
-                pltpu.VMEM((length, PAIR), jnp.float32),
-                pltpu.VMEM((SLOTS, PAIR), jnp.float32),
-                pltpu.VMEM((SLOTS, PAIR), jnp.float32),
-                pltpu.VMEM((PAIR, length), jnp.bfloat16),
-                pltpu.VMEM((PAIR, SLOTS), jnp.bfloat16),
-            ],
-        ),
-        out_shape=[low, low, low, full, full],
+        functools.partial(backward_kernel, examples),
+        grid=(pairs,),
+        in_specs=[
+            pl.BlockSpec((8, SLOTS), lambda p: (0, 0), memory_space=pltpu.SMEM),
+            block, block, block, block, block, pre_block,
+            pl.BlockSpec((1, 8, length), lambda p: (p, 0, 0)),
+            pl.BlockSpec(meta.shape, lambda p: (0, 0)),
+        ],
+        out_specs=[block, block, block, pre_block],
+        out_shape=[low, low, low, jax.ShapeDtypeStruct((2, SLOTS, width), jnp.float32)],
+        scratch_shapes=[
+            pltpu.VMEM((length, PAIR), jnp.float32),
+            pltpu.VMEM((length, PAIR), jnp.float32),
+            pltpu.VMEM((SLOTS, PAIR), jnp.float32),
+            pltpu.VMEM((SLOTS, PAIR), jnp.float32),
+            pltpu.VMEM((PAIR, length), jnp.bfloat16),
+            pltpu.VMEM((PAIR, SLOTS), jnp.bfloat16),
+            pltpu.VMEM((meta.shape[1], 8), jnp.float32),
+        ],
         compiler_params=pltpu.CompilerParams(vmem_limit_bytes=48 * 2**20),
-    )(bounds, q, k, v, do, att, pk, pv, lse, meta, seg_col, live_col)
-
-
-def block_bounds(seg):
-    length = seg.shape[0]
-    first = seg[::QB]
-    last = seg[QB - 1 :: QB]
-    low = jnp.sum((seg[None, :] < first[:, None]).astype(jnp.int32), axis=1)
-    high = jnp.sum((seg[None, :] <= last[:, None]).astype(jnp.int32), axis=1)
-    return jnp.stack([low // KB, (high + KB - 1) // KB])
+    )(meta, q, k, v, do, att, pre, lse, meta)
 
 
 MESH = pl.DeviceIdType.MESH
@@ -271,7 +276,7 @@
         for at in range(self.plan.sides):
             side = self.core if self.plan.core_in_tp else at
             yield pltpu.make_async_copy(
-                self.source.at[:, at], self.whole.at[(slice(None), side) + where], self.sems["own"].at[at]
+                self.source.at[:, at], self.whole.at[(slice(None), side) + where], self.sems.own.at[at]
             )
 
     def line_copies(self, i):
@@ -279,7 +284,7 @@
         dst = self.whole.at[self.unit(i) + tuple(self.coords) + (slice(None), self.lanes)]
         for by in range(1, LINE):
             yield remote(
-                src, dst, self.sems["line_send"].at[i, by - 1], self.sems["line_recv"].at[i, by - 1],
+                src, dst, self.sems.line_send.at[i, by - 1], self.sems.line_recv.at[i, by - 1],
                 self.plan.device(self.coords, lax.rem(self.line + by, LINE), self.core),
             )
 
@@ -296,7 +301,7 @@
             for by in range(1, size):
                 spot = (i, half, step, by - 1)
                 yield remote(
-                    block, block, self.sems["axis_send"].at[spot], self.sems["axis_recv"].at[spot],
+                    block, block, self.sems.axis_send.at[spot], self.sems.axis_recv.at[spot],
                     self.plan.device(shifted(self.coords, axis, by, size), self.line, self.core),
                 )
 
@@ -306,7 +311,7 @@
         else:
             block = self.whole.at[self.unit(i) + (slice(None), slice(None), side)]
         return remote(
-            block, block, self.sems["core_send"].at[i], self.sems["core_recv"].at[i], sibling(self.plan, self.place)
+            block, block, self.sems.core_send.at[i], self.sems.core_recv.at[i], sibling(self.plan, self.place)
         )
 
     def core_roles(self, i):
@@ -361,28 +366,31 @@
         return self.count + lag * len(self.plan.axes)
 
 
+def semaphores(*shape):
+    return pltpu.SemaphoreType.DMA(shape)
+
+
 def gather_semaphores(plan):
     count = KINDS * plan.sides
     steps = len(plan.axes)
     reach = max(plan.shape[a] for a in plan.axes) - 1
-    shapes = {
-        "line_send": (count, LINE - 1),
-        "line_recv": (count, LINE - 1),
-        "axis_send": (count, 2, steps, reach),
-        "axis_recv": (count, 2, steps, reach),
-        "core_send": (count,),
-        "core_recv": (count,),
-        "own": (2,),
-    }
-    return {name: pltpu.SemaphoreType.DMA(shape) for name, shape in shapes.items()}
+    return dict(
+        line_send=semaphores(count, LINE - 1),
+        line_recv=semaphores(count, LINE - 1),
+        axis_send=semaphores(count, 2, steps, reach),
+        axis_recv=semaphores(count, 2, steps, reach),
+        core_send=semaphores(count),
+        core_recv=semaphores(count),
+        own=semaphores(2),
+    )
 
 
 class Line:
-    def __init__(self, plan, place, name, sems):
+    def __init__(self, plan, place, send_sems, recv_sems):
         self.plan = plan
         self.coords, self.line, self.core = place
-        self.send_sems = sems[name + "_send"]
-        self.recv_sems = sems[name + "_recv"]
+        self.send_sems = send_sems
+        self.recv_sems = recv_sems
         self.pieces = []
 
     def here(self, chip, side):
@@ -416,62 +424,15 @@
         pl.when(jnp.logical_not(self.here(chip, side)))(copy.wait_recv)
 
 
-def line_semaphores(name, count):
-    return {
-        name + "_send": pltpu.SemaphoreType.DMA((count,)),
-        name + "_recv": pltpu.SemaphoreType.DMA((LINE, 2)),
-    }
-
-
 class Sibling:
-    def __init__(self, plan, place, name, sems):
-        self.sems = sems
-        self.name = name
+    def __init__(self, plan, place, send_sems, recv_sems):
+        self.send_sems = send_sems
+        self.recv_sems = recv_sems
         self.device = sibling(plan, place)
 
     def copy(self, src, dst, at):
-        return remote(src, dst, self.sems[self.name + "_send"].at[at], self.sems[self.name + "_recv"].at[at], self.device)
-
-
-def sibling_semaphores(name, count):
-    return {
-        name + "_send": pltpu.SemaphoreType.DMA((count,)),
-        name + "_recv": pltpu.SemaphoreType.DMA((count,)),
-    }
-
-
-def give_back_kernel(plan, names, parts, pieces, *sems):
-    sems = dict(zip(names, sems))
-    place = plan.here()
-    coords, line, core = place
-    greet(plan, place)
-    places = pieces.shape[2]
-    back = Line(plan, place, "back", sems)
-    for half in range(2):
-        for side in range(plan.cores):
-            start = (half * plan.cores + side) * places
-            if plan.core_in_tp:
-                slot, target = line, side
-            else:
-                slot, target = lax.rem(line, 2), line // 2
-            back.send(parts.at[:, pl.ds(start, places)], pieces.at[:, slot], 2 * core + half, target)
-    back.settle()
-    for j in range(pieces.shape[1]):
-        chip = j if plan.core_in_tp else 2 * core + j
-        back.receive(pieces.at[:, j], chip, line // 2)
-    back.drain()
-
-
-def give_back(plan, parts, held, places):
-    sems = line_semaphores("back", 4)
-    return pl.pallas_call(
-        functools.partial(give_back_kernel, plan, tuple(sems)),
-        out_shape=jax.ShapeDtypeStruct((parts.shape[0], held, places, parts.shape[2]), parts.dtype),
-        in_specs=[pl.BlockSpec(memory_space=pl.ANY)],
-        out_specs=pl.BlockSpec(memory_space=pl.ANY),
-        scratch_shapes=list(sems.values()),
-        compiler_params=pltpu.CompilerParams(collective_id=1, has_side_effects=True),
-    )(parts)
+        return remote(src, dst, self.send_sems.at[at], self.recv_sems.at[at], self.device)
+
 
 def normalise(z):
     mean = jnp.mean(z, axis=1, keepdims=True)
@@ -489,7 +450,7 @@
 
 def forward_inputs(plan, place, refs, scratch):
     coords, line, core = place
-    source, prefix, meta = scratch["source"], scratch["prefix"], scratch["meta"]
+    source, prefix, meta = scratch.source, scratch.prefix, scratch.meta
     sides = plan.sides
 
     def put(kind, block, first):
@@ -497,26 +458,26 @@
             at = (first + side) * LANES
             source[kind, side] = block[:, at : at + LANES]
 
-    put(0, refs["w_query"], 0)
-    put(1, refs["w_key"], 0)
-    put(2, refs["w_value"], 0)
-    put(3, jnp.transpose(refs["w_attn_out"][...]), 0)
-    down = jnp.transpose(refs["w_down"][...])
+    put(0, refs.w_query, 0)
+    put(1, refs.w_key, 0)
+    put(2, refs.w_value, 0)
+    put(3, jnp.transpose(refs.w_attn_out[...]), 0)
+    down = jnp.transpose(refs.w_down[...])
     for j in range((KINDS - FIRST_UP) // 2):
-        put(FIRST_UP + 2 * j, refs["w_up"], j * sides)
+        put(FIRST_UP + 2 * j, refs.w_up, j * sides)
         put(FIRST_UP + 2 * j + 1, down, j * sides)
 
-    slots = refs["prefix_keys"].shape[1]
+    slots = refs.prefix_keys.shape[1]
     prefix[...] = jnp.zeros_like(prefix)
-    for j in range(refs["tokens"].shape[0]):
-        task = refs["task_ids"][j]
-        for which, name in enumerate(("prefix_keys", "prefix_values")):
-            rows = refs[name][task]
+    for j in range(refs.tokens.shape[0]):
+        task = refs.task_ids[j]
+        for which, table in enumerate((refs.prefix_keys, refs.prefix_values)):
+            rows = table[task]
             for side in range(sides):
                 prefix[j, side, which, 0:slots, :] = rows[:, side * LANES : (side + 1) * LANES]
 
     mine = line if plan.core_in_tp else lax.rem(line, 2)
-    task = refs["task_ids"][mine]
+    task = refs.task_ids[mine]
     meta[...] = jnp.zeros_like(meta)
     length = meta.shape[1] - SLOTS
     spots = lax.broadcasted_iota(jnp.int32, (1, length), 1)
@@ -524,16 +485,16 @@
     segment = jnp.zeros((1, length), jnp.float32)
     ends = jnp.zeros((1, SLOTS), jnp.float32)
     end = jnp.int32(0)
-    for j in range(refs["lengths"].shape[1]):
-        end = end + refs["lengths"][mine, j]
+    for j in range(refs.lengths.shape[1]):
+        end = end + refs.lengths[mine, j]
         segment = segment + jnp.where(spots >= end, 1.0, 0.0)
         ends = jnp.where(lane == j, end.astype(jnp.float32), ends)
-    masks = refs["slot_masks"]
+    masks = refs.slot_masks
     used = jnp.zeros((1, slots), jnp.int32)
     limit = jnp.int32(0)
     for t in range(masks.shape[0]):
         used = jnp.where(task == t, masks[t : t + 1, :], used)
-        limit = jnp.where(task == t, refs["prefix_lens"][t], limit)
+        limit = jnp.where(task == t, refs.prefix_lens[t], limit)
     live = jnp.where((used == 1) & (lane[:, :slots] < limit), 1.0, 0.0)
     meta[0:1, 0:slots] = live
     meta[0:1, SLOTS:] = segment
@@ -541,35 +502,20 @@
     meta[2:3, 0:SLOTS] = ends
 
 
-F_IN = (
-    "task_ids", "lengths", "prefix_lens", "slot_masks", "tokens", "out_grad", "w_query", "w_key", "w_value",
-    "w_attn_out", "w_up", "w_down", "gain_one", "shift_one", "gain_two", "shift_two", "prefix_keys",
-    "prefix_values",
-)
-F_OUT = (
-    "q_out", "k_out", "v_out", "att_out", "lse_out", "pre_out", "meta_out", "d_att_out", "d_first_out",
-    "w_out", "pieces",
-)
-F_SCRATCH = (
-    "source", "prefix", "meta", "whole", "row", "grad", "pre", "q", "k", "v", "att", "lse", "att_other",
-    "keys", "values", "meta_cols", "normal_one", "rstd_one", "normed", "slope", "acc", "low", "out", "d_att",
-    "d_att_away",
-)
 AHEAD = 3
 LAG = 2
 
 
-def forward_backward_kernel(plan, sem_names, *args):
-    names = F_IN + F_OUT + F_SCRATCH + sem_names
-    refs = dict(zip(names, args))
+def forward_backward_kernel(plan, names, *args):
+    refs = SimpleNamespace(**dict(zip(names, args)))
     sems = refs
     place = plan.here()
     coords, line, core = place
     bf16, f32 = jnp.bfloat16, jnp.float32
     spread = plan.core_in_tp
-    tokens, row, grad, pre = refs["tokens"], refs["row"], refs["grad"], refs["pre"]
-    whole, meta = refs["whole"], refs["meta"]
-    q, k, v, att, lse = (refs[n] for n in ("q", "k", "v", "att", "lse"))
+    tokens, row, grad, pre = refs.tokens, refs.row, refs.grad, refs.pre
+    whole, meta = refs.whole, refs.meta
+    q, k, v, att, lse = refs.q, refs.k, refs.v, refs.att, refs.lse
     held = tokens.shape[0]
     width = row.shape[-1]
     length = q.shape[0]
@@ -581,23 +527,23 @@
     forward_inputs(plan, place, refs, refs)
     greet(plan, place)
 
-    gather = Gather(plan, place, refs["source"], whole, sems)
+    gather = Gather(plan, place, refs.source, whole, sems)
     gather.start_line(0)
     gather.start_line(1)
-    token_line = Line(plan, place, "token", sems)
+    token_line = Line(plan, place, sems.token_send, sems.token_recv)
     for j in range(held):
         token_line.send(tokens.at[j], row.at[line, slot], base + j, core)
     for copy in gather.own_copies():
         copy.start()
     for i in range(2, AHEAD):
         gather.start_line(i)
-    prefix_line = Line(plan, place, "prefix", sems)
+    prefix_line = Line(plan, place, sems.prefix_send, sems.prefix_recv)
     for j in range(held):
         for side in range(plan.sides):
             prefix_line.send(
-                refs["prefix"].at[j, side], pre.at[:, :, gather.lanes], base + j, core if spread else side
+                refs.prefix.at[j, side], pre.at[:, :, gather.lanes], base + j, core if spread else side
             )
-    share = Sibling(plan, place, "share", sems)
+    share = Sibling(plan, place, sems.share_send, sems.share_recv)
     meta_copy = share.copy(meta, meta, 4)
     if not spread:
         pl.when(holds)(meta_copy.start)
@@ -628,9 +574,9 @@
 
     for chip in range(LINE):
         share_token(chip)
-    grad_line = Line(plan, place, "grad", sems)
+    grad_line = Line(plan, place, sems.grad_send, sems.grad_recv)
     for j in range(held):
-        grad_line.send(refs["out_grad"].at[j], grad.at[lax.rem(line, 2), slot], base + j, line // 2)
+        grad_line.send(refs.out_grad.at[j], grad.at[lax.rem(line, 2), slot], base + j, line // 2)
     for chip in range(LINE):
         if spread:
             share.copy(row.at[chip, 1 - core], row.at[chip, 1 - core], chip).wait_recv()
@@ -641,10 +587,10 @@
     prefix_line.settle()
     for chip in range(LINE):
         prefix_line.receive(pre.at[:, :, pl.ds(chip * LANES, LANES)], chip, core if spread else line // 2)
-    refs["meta_cols"][...] = jnp.transpose(meta[...])
-
-    def publish(name, out, at):
-        return pltpu.make_async_copy(refs[name], refs[out], sems["publish"].at[at])
+    refs.meta_cols[...] = jnp.transpose(meta[...])
+
+    def publish(ref, out, at):
+        return pltpu.make_async_copy(ref, out, sems.publish.at[at])
 
     def ready(first, amount, done):
         until = min(last, first + amount - 1 + steps)
@@ -666,20 +612,21 @@
             return x
 
         lax.fori_loop(0, LINE, project, 0)
-    keep = [publish(n, n + "_out", at) for at, n in enumerate(("q", "k", "v", "pre", "meta"))]
-    keep.append(pltpu.make_async_copy(whole.at[pl.ds(0, 3), core], refs["w_out"], sems["publish"].at[5]))
+    kept = ((q, refs.q_out), (k, refs.k_out), (v, refs.v_out), (pre, refs.pre_out), (meta, refs.meta_out))
+    keep = [publish(ref, out, at) for at, (ref, out) in enumerate(kept)]
+    keep.append(pltpu.make_async_copy(whole.at[pl.ds(0, 3), core], refs.w_out, sems.publish.at[5]))
     for copy in keep:
         copy.start()
 
-    att_share = Sibling(plan, place, "att", sems)
+    att_share = Sibling(plan, place, sems.att_send, sems.att_recv)
     here = pl.ds(pl.multiple_of(core * half, half), half)
     there = pl.ds(pl.multiple_of((1 - core) * half, half), half)
-    keys, values = refs["keys"], refs["values"]
+    keys, values = refs.keys, refs.values
     blocks = length // QB
 
     def att_copy(p):
         lanes = pl.ds(pl.multiple_of(p * PAIR, PAIR), PAIR)
-        return att_share.copy(att.at[there, lanes], refs["att_other"].at[:, lanes], p)
+        return att_share.copy(att.at[there, lanes], refs.att_other.at[:, lanes], p)
 
     def pair(p, x):
         lanes = pl.ds(pl.multiple_of(p * PAIR, PAIR), PAIR)
@@ -692,7 +639,7 @@
             rows = pl.ds(pl.multiple_of(b * QB, QB), QB)
             mixed, totals = attend_block(
                 q[rows, lanes], keys[...], values[...],
-                refs["meta_cols"][pl.ds(pl.multiple_of(SLOTS + b * QB, SLOTS), QB), 0:1],
+                refs.meta_cols[pl.ds(pl.multiple_of(SLOTS + b * QB, SLOTS), QB), 0:1],
                 meta[0:1, SLOTS:], meta[0:1, :SLOTS],
             )
             att[rows, lanes] = mixed
@@ -710,15 +657,15 @@
     pairs = WIDE // PAIR
     lax.fori_loop(0, pairs, pair, 0)
     done = min(last, done + plan.sides * pairs)
-    keep += [publish(n, n + "_out", 6 + at) for at, n in enumerate(("att", "lse"))]
+    keep += [publish(att, refs.att_out, 6), publish(lse, refs.lse_out, 7)]
     for copy in keep[-2:]:
         copy.start()
     for p in range(pairs):
         att_copy(p).wait_recv()
 
     done = ready(3 * plan.sides, plan.sides, done)
-    normal_one, rstd_one, normed, acc = (refs[n] for n in ("normal_one", "rstd_one", "normed", "acc"))
-    low, slope, out = refs["low"], refs["slope"], refs["out"]
+    normal_one, rstd_one, normed, acc = refs.normal_one, refs.rstd_one, refs.normed, refs.acc
+    low, slope, out = refs.low, refs.slope, refs.out
     parts = half // CHUNK
 
     def weight(kind, side):
@@ -728,11 +675,11 @@
         rows = pl.ds(pl.multiple_of(b * CHUNK, CHUNK), CHUNK)
         own = att[pl.ds(pl.multiple_of(core * half + b * CHUNK, CHUNK), CHUNK), :]
         total = row[2 * core + b].reshape(CHUNK, width).astype(f32)
-        total = total + mm_nt(own, weight(3, core)) + mm_nt(refs["att_other"][rows, :], weight(3, 1 - core))
+        total = total + mm_nt(own, weight(3, core)) + mm_nt(refs.att_other[rows, :], weight(3, 1 - core))
         normal, rstd = normalise(total)
         normal_one[rows, :] = normal
         rstd_one[rows, :] = jnp.broadcast_to(rstd, (CHUNK, LANES))
-        low_normed = (normal * refs["gain_one"][...] + refs["shift_one"][...]).astype(bf16)
+        low_normed = (normal * refs.gain_one[...] + refs.shift_one[...]).astype(bf16)
         normed[rows, :] = low_normed
         acc[rows, :] = low_normed.astype(f32)
         return x
@@ -767,15 +714,15 @@
         for side in range(plan.cores):
             grad_line.receive(grad.at[part, side], 2 * core + part, side if spread else line // 2)
 
-    back = Line(plan, place, "back", sems)
+    back = Line(plan, place, sems.back_send, sems.back_recv)
     places = tokens.shape[1]
 
     def close(b, x):
         rows = pl.ds(pl.multiple_of(b * CHUNK, CHUNK), CHUNK)
         normal, rstd = normalise(acc[rows, :])
-        out[rows, :] = (normal * refs["gain_two"][...] + refs["shift_two"][...]).astype(bf16)
+        out[rows, :] = (normal * refs.gain_two[...] + refs.shift_two[...]).astype(bf16)
         d_second = normalise_grad(
-            normal, rstd, refs["gain_two"][...], grad[b].reshape(CHUNK, width).astype(f32)
+            normal, rstd, refs.gain_two[...], grad[b].reshape(CHUNK, width).astype(f32)
         )
         acc[rows, :] = d_second
         low[rows, :] = d_second.astype(bf16)
@@ -786,7 +733,7 @@
         for side in range(plan.cores):
             spot, target = (line, side) if spread else (lax.rem(line, 2), line // 2)
             back.send(
-                out.at[pl.ds((b * plan.cores + side) * places, places)], refs["pieces"].at[spot],
+                out.at[pl.ds((b * plan.cores + side) * places, places)], refs.pieces.at[spot],
                 2 * core + b, target,
             )
 
@@ -806,8 +753,8 @@
 
     lax.fori_loop(0, 2 * groups, feed_back, 0)
 
-    d_att, away = refs["d_att"], refs["d_att_away"]
-    d_share = Sibling(plan, place, "d_att", sems)
+    d_att, away = refs.d_att, refs.d_att_away
+    d_share = Sibling(plan, place, sems.d_send, sems.d_recv)
 
     def d_copy(b):
         mine = pl.ds(pl.multiple_of(core * half + b * CHUNK, CHUNK), CHUNK)
@@ -815,7 +762,7 @@
 
     def open_(b, x):
         rows = pl.ds(pl.multiple_of(b * CHUNK, CHUNK), CHUNK)
-        d_first = normalise_grad(normal_one[rows, :], rstd_one[rows, 0:1], refs["gain_one"][...], acc[rows, :])
+        d_first = normalise_grad(normal_one[rows, :], rstd_one[rows, 0:1], refs.gain_one[...], acc[rows, :])
         acc[rows, :] = d_first
         d_low = d_first.astype(bf16)
         away[rows, :] = mm(d_low, weight(3, 1 - core)).astype(bf16)
@@ -825,11 +772,11 @@
         return x
 
     lax.fori_loop(0, parts, open_, 0)
-    keep.append(publish("acc", "d_first_out", 8))
+    keep.append(publish(acc, refs.d_first_out, 8))
     keep[-1].start()
     for b in range(parts):
         d_copy(b).wait_recv()
-    keep.append(publish("d_att", "d_att_out", 9))
+    keep.append(publish(d_att, refs.d_att_out, 9))
     keep[-1].start()
 
     lax.fori_loop(0, gather.count, lambda i, x: (gather.drain(i), x)[1], 0)
@@ -849,82 +796,256 @@
         d_copy(b).wait_send()
     back.settle()
     for j in range(held):
-        back.receive(refs["pieces"].at[j], j if spread else 2 * core + j, line // 2)
+        back.receive(refs.pieces.at[j], j if spread else 2 * core + j, line // 2)
     back.drain()
     for copy in keep:
         copy.wait()
 
 
-def forward_backward(plan, task_ids, lengths, prefix_lens, slot_masks, *rest):
-    tokens, _, w_query = rest[:3]
-    held, places, width = tokens.shape
-    depth = w_query.shape[0]
+def forward_backward(plan, given):
+    held, places, width = given.tokens.shape
+    depth = given.w_query.shape[0]
     length = places * plan.tp
     half = length // 2
     pairs = WIDE // PAIR
     bf16, f32 = jnp.bfloat16, jnp.float32
     S = jax.ShapeDtypeStruct
-    outs = {
-        "q_out": S((length, WIDE), bf16),
-        "k_out": S((length, WIDE), bf16),
-        "v_out": S((length, WIDE), bf16),
-        "att_out": S((length, WIDE), bf16),
-        "lse_out": S((pairs, 8, length), f32),
-        "pre_out": S((2, SLOTS, WIDE), bf16),
-        "meta_out": S((8, SLOTS + length), f32),
-        "d_att_out": S((length, WIDE), bf16),
-        "d_first_out": S((half, width), f32),
-        "w_out": S((3,) + plan.shape + (depth, WIDE), bf16),
-        "pieces": S((held, places, width), bf16),
-    }
+    outs = dict(
+        q_out=S((length, WIDE), bf16),
+        k_out=S((length, WIDE), bf16),
+        v_out=S((length, WIDE), bf16),
+        att_out=S((length, WIDE), bf16),
+        lse_out=S((pairs, 8, length), f32),
+        pre_out=S((2, SLOTS, WIDE), bf16),
+        meta_out=S((8, SLOTS + length), f32),
+        d_att_out=S((length, WIDE), bf16),
+        d_first_out=S((half, width), f32),
+        w_out=S((3,) + plan.shape + (depth, WIDE), bf16),
+        pieces=S((held, places, width), bf16),
+    )
     units = 2 * (KINDS - FIRST_UP) // 2
-    scratch = {
-        "source": ((KINDS, plan.sides, depth, LANES), bf16),
-        "prefix": ((held, plan.sides, 2, SLOTS, LANES), bf16),
-        "meta": ((8, SLOTS + length), f32),
-        "whole": ((KINDS, 2) + plan.shape + (depth, WIDE), bf16),
-        "row": ((LINE, plan.cores, places, width), bf16),
-        "grad": ((2, plan.cores, places, width), bf16),
-        "pre": ((2, SLOTS, WIDE), bf16),
-        "q": ((length, WIDE), bf16),
-        "k": ((length, WIDE), bf16),
-        "v": ((length, WIDE), bf16),
-        "att": ((length, WIDE), bf16),
-        "lse": ((pairs, 8, length), f32),
-        "att_other": ((half, WIDE), bf16),
-        "keys": ((SLOTS + length, PAIR), bf16),
-        "values": ((SLOTS + length, PAIR), bf16),
-        "meta_cols": ((SLOTS + length, 8), f32),
-        "normal_one": ((half, width), f32),
-        "rstd_one": ((half, LANES), f32),
-        "normed": ((half, width), bf16),
-        "slope": ((units, half, WIDE), bf16),
-        "acc": ((half, width), f32),
-        "low": ((half, width), bf16),
-        "out": ((half, width), bf16),
-        "d_att": ((length, WIDE), bf16),
-        "d_att_away": ((half, WIDE), bf16),
-    }
+    scratch = dict(
+        source=((KINDS, plan.sides, depth, LANES), bf16),
+        prefix=((held, plan.sides, 2, SLOTS, LANES), bf16),
+        meta=((8, SLOTS + length), f32),
+        whole=((KINDS, 2) + plan.shape + (depth, WIDE), bf16),
+        row=((LINE, plan.cores, places, width), bf16),
+        grad=((2, plan.cores, places, width), bf16),
+        pre=((2, SLOTS, WIDE), bf16),
+        q=((length, WIDE), bf16),
+        k=((length, WIDE), bf16),
+        v=((length, WIDE), bf16),
+        att=((length, WIDE), bf16),
+        lse=((pairs, 8, length), f32),
+        att_other=((half, WIDE), bf16),
+        keys=((SLOTS + length, PAIR), bf16),
+        values=((SLOTS + length, PAIR), bf16),
+        meta_cols=((SLOTS + length, 8), f32),
+        normal_one=((half, width), f32),
+        rstd_one=((half, LANES), f32),
+        normed=((half, width), bf16),
+        slope=((units, half, WIDE), bf16),
+        acc=((half, width), f32),
+        low=((half, width), bf16),
+        out=((half, width), bf16),
+        d_att=((length, WIDE), bf16),
+        d_att_away=((half, WIDE), bf16),
+    )
     sems = gather_semaphores(plan)
-    for name, amount in (("token", held), ("prefix", held * plan.sides), ("grad", held), ("back", 4)):
-        sems.update(line_semaphores(name, amount))
-    for name, amount in (("share", 5), ("att", pairs), ("d_att", half // CHUNK)):
-        sems.update(sibling_semaphores(name, amount))
-    sems["publish"] = pltpu.SemaphoreType.DMA((10,))
+    sems.update(
+        token_send=semaphores(held),
+        token_recv=semaphores(LINE, 2),
+        prefix_send=semaphores(held * plan.sides),
+        prefix_recv=semaphores(LINE, 2),
+        grad_send=semaphores(held),
+        grad_recv=semaphores(LINE, 2),
+        back_send=semaphores(4),
+        back_recv=semaphores(LINE, 2),
+        share_send=semaphores(5),
+        share_recv=semaphores(5),
+        att_send=semaphores(pairs),
+        att_recv=semaphores(pairs),
+        d_send=semaphores(half // CHUNK),
+        d_recv=semaphores(half // CHUNK),
+        publish=semaphores(10),
+    )
     smem = pl.BlockSpec(memory_space=pltpu.SMEM)
     vmem = pl.BlockSpec(memory_space=pltpu.VMEM)
     hbm = pl.BlockSpec(memory_space=pl.ANY)
     results = pl.pallas_call(
-        functools.partial(forward_backward_kernel, plan, tuple(sems)),
-        out_shape=[outs[n] for n in F_OUT],
+        functools.partial(forward_backward_kernel, plan, (*vars(given), *outs, *scratch, *sems)),
+        out_shape=list(outs.values()),
         in_specs=[smem, smem, smem, vmem, hbm, hbm] + [vmem] * 12,
-        out_specs=[hbm] * len(F_OUT),
-        scratch_shapes=[pltpu.VMEM(*scratch[n]) for n in F_SCRATCH] + list(sems.values()),
+        out_specs=[hbm] * len(outs),
+        scratch_shapes=[pltpu.VMEM(*spec) for spec in scratch.values()] + list(sems.values()),
         compiler_params=pltpu.CompilerParams(
             collective_id=0, has_side_effects=True, vmem_limit_bytes=62 * 2**20
         ),
-    )(task_ids, lengths, prefix_lens, slot_masks, *rest)
-    return dict(zip(F_OUT, results))
+    )(*vars(given).values())
+    return SimpleNamespace(**dict(zip(outs, results)))
+
+
+def finish_kernel(plan, names, *args):
+    refs = SimpleNamespace(**dict(zip(names, args)))
+    place = plan.here()
+    coords, line, core = place
+    bf16, f32 = jnp.bfloat16, jnp.float32
+    spread = plan.core_in_tp
+    width = refs.d_first.shape[1]
+    half = refs.d_first.shape[0]
+    held, places = refs.pieces.shape[:2]
+    tasks, slots = refs.keys_grad.shape[:2]
+    parts = half // CHUNK
+    kept = refs.total.shape[2]
+
+    for chip in range(LINE):
+        lanes = slice(chip * LANES, (chip + 1) * LANES)
+        for which in range(2):
+            refs.terms[chip, which] = refs.d_pre[which, :, lanes].astype(bf16)
+        refs.terms[chip, 0, SLOTS - 16 :, :] = jnp.broadcast_to(refs.meta[1:2, 0:SLOTS], (16, SLOTS)).astype(bf16)
+    greet(plan, place)
+    terms = Line(plan, place, refs.terms_send, refs.terms_recv)
+    for chip in range(LINE):
+        terms.send(refs.terms.at[chip], refs.row_terms.at[line], chip, core)
+
+    swap = Sibling(plan, place, refs.swap_send, refs.swap_recv)
+    back = Line(plan, place, refs.back_send, refs.back_recv)
+
+    def share(which, b):
+        rows = pl.ds(pl.multiple_of(which * half + b * CHUNK, CHUNK), CHUNK)
+        total = mm_nt(refs.dq[rows, :], refs.w[0].reshape(width, WIDE))
+        total = total + mm_nt(refs.dk[rows, :], refs.w[1].reshape(width, WIDE))
+        return total + mm_nt(refs.dv[rows, :], refs.w[2].reshape(width, WIDE))
+
+    def swap_copy(b):
+        rows = pl.ds(b * CHUNK, CHUNK)
+        return swap.copy(refs.away.at[rows], refs.other.at[rows], b)
+
+    for b in range(parts):
+        rows = pl.ds(b * CHUNK, CHUNK)
+        refs.away[rows, :] = share(1 - core, b).astype(bf16)
+        swap_copy(b).start()
+        own = share(core, b) + refs.d_first[rows, :]
+        swap_copy(b).wait_recv()
+        refs.sums[rows, :] = (own + refs.other[rows, :].astype(f32)).astype(bf16)
+        for side in range(plan.cores):
+            spot, target = (line, side) if spread else (lax.rem(line, 2), line // 2)
+            back.send(
+                refs.sums.at[pl.ds(b * CHUNK + side * places, places)], refs.pieces.at[spot], 2 * core + b, target
+            )
+
+    terms.settle()
+    total = refs.total
+    total[...] = jnp.zeros_like(total)
+    for chip in range(LINE):
+        terms.receive(refs.row_terms.at[chip], chip, core)
+        marks = refs.row_terms[chip, 0, SLOTS - 16 :, :].astype(f32)
+        for task in range(tasks):
+            for which in range(2):
+                total[task, which] += refs.row_terms[chip, which, 0:kept, :].astype(f32) * marks[0:1, task : task + 1]
+    for step, axis in enumerate(plan.axes):
+        size = plan.shape[axis]
+        refs.gone[step] = total[...].astype(bf16)
+        copies = [
+            remote(
+                refs.gone.at[step], refs.come.at[step, by - 1], refs.axis_send.at[step, by - 1],
+                refs.axis_recv.at[step, by - 1],
+                plan.device(shifted(coords, axis, by, size), line, core),
+            )
+            for by in range(1, size)
+        ]
+        for copy in copies:
+            copy.start()
+        for by, copy in enumerate(copies):
+            copy.wait_recv()
+            total[...] += refs.come[step, by].astype(f32)
+        for copy in copies:
+            copy.wait_send()
+
+    def put(block, lanes):
+        for task in range(tasks):
+            refs.keys_grad[task, :, lanes] = block[task, 0, 0:slots, :]
+            refs.values_grad[task, :, lanes] = block[task, 1, 0:slots, :]
+
+    if spread:
+        put(total, slice(None))
+    else:
+        last = swap.copy(total, refs.total_other, parts)
+        last.start()
+
+        @pl.when(core == 0)
+        def _():
+            put(total, slice(0, LANES))
+
+        @pl.when(core == 1)
+        def _():
+            put(total, slice(LANES, 2 * LANES))
+
+        last.wait_recv()
+
+        @pl.when(core == 0)
+        def _():
+            put(refs.total_other, slice(LANES, 2 * LANES))
+
+        @pl.when(core == 1)
+        def _():
+            put(refs.total_other, slice(0, LANES))
+
+        last.wait_send()
+
+    back.settle()
+    for j in range(held):
+        back.receive(refs.pieces.at[j], j if spread else 2 * core + j, line // 2)
+    back.drain()
+    terms.drain()
+    for b in range(parts):
+        swap_copy(b).wait_send()
+
+
+def finish(plan, held, places, tasks, slots, part, given):
+    half, width = given.d_first.shape
+    steps = len(plan.axes)
+    reach = max(plan.shape[a] for a in plan.axes) - 1
+    kept = -(-slots // 16) * 16
+    bf16, f32 = jnp.bfloat16, jnp.float32
+    outs = dict(
+        pieces=jax.ShapeDtypeStruct((held, places, width), bf16),
+        keys_grad=jax.ShapeDtypeStruct((tasks, slots, part), f32),
+        values_grad=jax.ShapeDtypeStruct((tasks, slots, part), f32),
+    )
+    scratch = dict(
+        terms=((LINE, 2, SLOTS, LANES), bf16),
+        row_terms=((LINE, 2, SLOTS, LANES), bf16),
+        away=((half, width), bf16),
+        other=((half, width), bf16),
+        sums=((half, width), bf16),
+        total=((tasks, 2, kept, LANES), f32),
+        total_other=((tasks, 2, kept, LANES), f32),
+        gone=((steps, tasks, 2, kept, LANES), bf16),
+        come=((steps, reach, tasks, 2, kept, LANES), bf16),
+    )
+    sems = dict(
+        terms_send=semaphores(LINE),
+        terms_recv=semaphores(LINE, 2),
+        swap_send=semaphores(half // CHUNK + 1),
+        swap_recv=semaphores(half // CHUNK + 1),
+        back_send=semaphores(4),
+        back_recv=semaphores(LINE, 2),
+        axis_send=semaphores(steps, reach),
+        axis_recv=semaphores(steps, reach),
+    )
+    vmem = pl.BlockSpec(memory_space=pltpu.VMEM)
+    results = pl.pallas_call(
+        functools.partial(finish_kernel, plan, (*vars(given), *outs, *scratch, *sems)),
+        out_shape=list(outs.values()),
+        in_specs=[vmem] * len(vars(given)),
+        out_specs=[pl.BlockSpec(memory_space=pl.ANY), vmem, vmem],
+        scratch_shapes=[pltpu.VMEM(*spec) for spec in scratch.values()] + list(sems.values()),
+        compiler_params=pltpu.CompilerParams(
+            collective_id=1, has_side_effects=True, vmem_limit_bytes=48 * 2**20
+        ),
+    )(*vars(given).values())
+    return results
 
 
 def shards(
@@ -932,51 +1053,41 @@
     second_gain, second_shift, prefix_keys, prefix_values, example_lengths, task_ids, prefix_lens,
     slot_masks, out_grad,
 ):
-    f32, bf16 = jnp.float32, jnp.bfloat16
-    held, places, width = tokens.shape
-    tasks, slots, part = prefix_keys.shape
-    length = places * plan.tp
-    _, line, core = plan.here()
-    half = length // 2
+    held, places, _ = tokens.shape
     done = forward_backward(
-        plan, task_ids, example_lengths, prefix_lens, slot_masks, tokens, out_grad, w_query, w_key, w_value,
-        w_attn_out, w_up, w_down, first_gain[None], first_shift[None], second_gain[None], second_shift[None],
-        prefix_keys, prefix_values,
-    )
-    q, k, v, att, lse, pre, row_meta, d_att, d_first = (
-        done[n + "_out"] for n in ("q", "k", "v", "att", "lse", "pre", "meta", "d_att", "d_first")
-    )
-    w_q, w_k, w_v = (done["w_out"][i].reshape(width, WIDE) for i in range(3))
-
-    def pick(a, which):
-        return lax.dynamic_slice_in_dim(a, which * half, half, 0)
-
-    def swap(a):
-        if plan.core_in_tp:
-            return lax.ppermute(a, "tp", [(i, i ^ 1) for i in range(plan.tp)])
-        return lax.ppermute(a, "rows", [(i, i ^ 1) for i in range(plan.rows)])
-
-    seg = row_meta[0, SLOTS:]
-    seg_col = jnp.broadcast_to(seg[:, None], (length, LANES))
-    live_col = jnp.broadcast_to(row_meta[0, :SLOTS][:, None], (SLOTS, LANES))
-    bounds = block_bounds(seg.astype(jnp.int32))
-    dq, dk, dv, dpk, dpv = attend_backward(
-        bounds, q, k, v, d_att, att, pre[0], pre[1], lse, row_meta, seg_col, live_col
-    )
-    shares = mm_nt(dq, w_q) + mm_nt(dk, w_k) + mm_nt(dv, w_v)
-    other = swap(pick(shares, 1 - core).astype(bf16)).astype(f32)
-    d_tokens = d_first + pick(shares, core) + other
-    back = give_back(plan, d_tokens.astype(bf16)[None], held, places)
-
-    d_pre = jnp.stack([dpk, dpv])[:, :slots].reshape(2, slots, LINE, LANES)
-    side = (jnp.arange(2) == core).astype(f32)
-    d_pre = row_meta[1, :tasks][None, :, None, None, None, None] * (
-        d_pre[:, None, :, :, None, :] * side[None, None, None, None, :, None]
-    )
-    d_pre = d_pre.reshape(2, tasks, slots, width).astype(bf16)
-    d_pre = lax.psum_scatter(d_pre, "tp", scatter_dimension=3, tiled=True)
-    d_pre = lax.psum(d_pre, "rows").astype(f32)
-    return done["pieces"], back[0].astype(f32), d_pre[0], d_pre[1]
+        plan,
+        SimpleNamespace(
+            task_ids=task_ids,
+            lengths=example_lengths,
+            prefix_lens=prefix_lens,
+            slot_masks=slot_masks,
+            tokens=tokens,
+            out_grad=out_grad,
+            w_query=w_query,
+            w_key=w_key,
+            w_value=w_value,
+            w_attn_out=w_attn_out,
+            w_up=w_up,
+            w_down=w_down,
+            gain_one=first_gain[None],
+            shift_one=first_shift[None],
+            gain_two=second_gain[None],
+            shift_two=second_shift[None],
+            prefix_keys=prefix_keys,
+            prefix_values=prefix_values,
+        ),
+    )
+    dq, dk, dv, d_pre = attend_backward(
+        example_lengths.shape[1], done.q_out, done.k_out, done.v_out, done.d_att_out, done.att_out,
+        done.pre_out, done.lse_out, done.meta_out,
+    )
+    d_tokens, keys_grad, values_grad = finish(
+        plan, held, places, *prefix_keys.shape,
+        SimpleNamespace(
+            dq=dq, dk=dk, dv=dv, w=done.w_out, d_first=done.d_first_out, d_pre=d_pre, meta=done.meta_out
+        ),
+    )
+    return done.pieces, d_tokens.astype(jnp.float32), keys_grad, values_grad
 
 
 def solution(mesh):

time: 528 us -> 294 us (0.56)
  local copies, waits for them, and re-layouts: 146 us -> 11.1 us
  waiting for transfers between devices: 60.5 us -> 0 us
  between operations: 14.2 us -> 0.67 us
  Pallas kernels: 286 us -> 275 us
  other arithmetic: 11.2 us -> 1.58 us
  matrix products: 5.8 us -> 0 us
    unnamed x21 -> x17, local copies, waits for them, and re-layouts: 131 us -> 11.1 us
    psum x1 -> x0, waiting for transfers between devices: 57.6 us -> none  [shards(): d_pre = lax.psum(d_pre, 'rows').astype(f32)]
    pallas_call x3, Pallas kernels: 286 us -> 275 us  [the longest x1 196 us: forward_backward(): pl.pallas_call(functools.partial(forward_backward_kernel, plan, (*vars(gi...]
    mul x5 -> x0, local copies, waits for them, and re-layouts: 6.94 us -> none  [the longest x4 5.75 us: shards(): d_pre[:, None, :, :, None, :] * side[None, None, None, None, :, None]]
    dot_general x3 -> x0, matrix products: 5.8 us -> none  [mm_nt(): return lax.dot_general(a, b, NT, preferred_element_type=jnp.float32)]
  transfers between devices with their start and end apart: 3 -> 0, of which waited for: 2 -> 0; matrix products, arithmetic and copies ran while one was open for 3% -> 0% of each run, Pallas kernels for 8% -> 0%
where the time goes in v3:
time: 294 us; the launch traced here: 288 us
  Pallas kernels  275 us (94%)
  local copies, waits for them, and re-layouts  11.1 us (4%)
    pallas_call x1, Pallas kernels, forward_backward(): pl.pallas_call(functools.partial(forward_backward_kernel, plan, (*vars(gi...  196 us
    pallas_call x1, Pallas kernels, attend_backward(): pl.pallas_call(functools.partial(backward_kernel, examples), grid=(pairs,...  47.2 us
    pallas_call x1, Pallas kernels, finish(): pl.pallas_call(functools.partial(finish_kernel, plan, (*vars(given), *out...  32 us
    unnamed x17, local copies, waits for them, and re-layouts  11.1 us

profile of v3, /device:TPU:0, one launch (start us, length us, event | category | flops | bytes accessed | tf_op | source)
XLA Modules:
  0.0 288.3 jit_solution(12873490599163416436)
XLA Ops:
  0.6 1.6 copy.22.args_16_
  2.3 1.6 copy.23.args_17_
  3.9 195.7 %shard_map.201 = (bf16[1024,512]{1,0:T(8,128)(2,1)}, bf16[1024,512]{1,0:T(8,128)(2,1)}, bf16[1024,512]{1,0:T(8,128)(2,1)}, bf16[1024,512]{1,0:T(8,128)(2,1)}, f3...) custom-call(s32[2]{0:T(128)} %args_0_.4, ...), custom_call_target="tpu_custom_call" | custom-call | tf_op jit(solution)/shard_map/pallas_call | solution.py:875
  199.6 0.0 copy-start
  199.6 1.2 copy-done
  200.8 0.0 copy-start.1
  200.8 1.2 copy-done.1
  202.0 0.0 copy-start.2
  202.1 0.8 copy-done.2
  202.8 0.0 copy-start.3
  202.8 0.9 copy-done.3
  203.8 0.0 copy-start.4
  203.8 0.9 copy-done.4
  204.7 47.2 %shard_map.202 = (bf16[1024,512]{1,0:T(8,128)(2,1)S(1)}, bf16[1024,512]{1,0:T(8,128)(2,1)S(1)}, bf16[1024,512]{1,0:T(8,128)(2,1)S(1)}, f32[2,128,512]{2,1,0:T(8,128)S(1)}) custom-call(f32[8,1152]{1,0:T(8,128)S(1)} %copy-done.2, bf16[1024,512]{1,0:T(8,128)(2,1)S(1)} %copy-done, bf16[1024,512]{1,0:T(8,128)(2,1)S(1)} %copy-done.1, ...), custom_call_target="tpu_custom_call" | custom-call | tf_op jit(solution)/shard_map/pallas_call | solution.py:162
  251.9 32.0 %shard_map.203 = (bf16[2,256,1024]{2,1,0:T(8,128)(2,1)S(1)}, f32[4,100,256]{2,1,0:T(8,128)S(1)}, f32[4,100,256]{2,1,0:T(8,128)S(1)}) custom-call(bf16[1024,512]{1,0:T(8,128)(2,1)S(1)} %get-tuple-element.31.args_0_, bf16[1024,512]{1,0:T(8,128)(2,1)S(1)} %get-tuple-element.32.args_1_, bf16[1024,512]{1,0:T(8,128)(2,1)S(1)} %get-tuple-element.33.args_2_, ...), custom_call_target="tpu_custom_call" | custom-call | tf_op jit(solution)/shard_map/pallas_call | solution.py:1038
  283.9 0.9 copy.24
  284.8 0.0 copy-start.5
  284.8 0.9 copy.25
  285.8 1.6 convert_element_type.3
  287.3 0.0 copy-done.5
  287.3 1.0 copy.27
Async XLA Ops:
  199.6 1.2 copy-start
  200.8 1.2 copy-start.1
  202.0 0.8 copy-start.2
  202.8 0.9 copy-start.3
  203.8 0.9 copy-start.4
  284.8 2.5 copy-start.5

commit v4 on v3

--- a/solution.py
+++ b/solution.py
@@ -1,4 +1,5 @@
 import functools
+import itertools
 import math
 from types import SimpleNamespace
 
@@ -180,6 +181,9 @@
             pltpu.VMEM((meta.shape[1], 8), jnp.float32),
         ],
         compiler_params=pltpu.CompilerParams(vmem_limit_bytes=48 * 2**20),
+        cost_estimate=pl.CostEstimate(
+            flops=40 * length * length * width, bytes_accessed=16 * length * width, transcendentals=0
+        ),
     )(meta, q, k, v, do, att, pre, lse, meta)
 
 
@@ -189,6 +193,7 @@
 WIDE = LINE * LANES
 KINDS = 12
 FIRST_UP = 4
+GROUPS = (KINDS - FIRST_UP) // 2
 CHUNK = 256
 
 
@@ -279,14 +284,34 @@
                 self.source.at[:, at], self.whole.at[(slice(None), side) + where], self.sems.own.at[at]
             )
 
+    def block(self, i, chip):
+        lanes = pl.ds(pl.multiple_of(chip * LANES, LANES), LANES)
+        return self.whole.at[self.unit(i) + tuple(self.coords) + (slice(None), lanes)]
+
     def line_copies(self, i):
         src = self.source.at[(i, 0) if self.plan.core_in_tp else self.unit(i)]
-        dst = self.whole.at[self.unit(i) + tuple(self.coords) + (slice(None), self.lanes)]
-        for by in range(1, LINE):
-            yield remote(
-                src, dst, self.sems.line_send.at[i, by - 1], self.sems.line_recv.at[i, by - 1],
-                self.plan.device(self.coords, lax.rem(self.line + by, LINE), self.core),
+        for at, by in enumerate((1, -1, 2, -2)):
+            chip = self.line + by
+            there = (chip >= 0) & (chip < LINE)
+            yield there, remote(
+                src, self.block(i, self.line), self.sems.line_send.at[i, at], self.sems.line_recv.at[i, self.line],
+                self.plan.device(self.coords, jnp.clip(chip, 0, LINE - 1), self.core),
             )
+
+    def pass_copies(self, i):
+        for middle, first, target in ((2, 0, 3), (1, 3, 0)):
+            block = self.block(i, first)
+            yield self.line == middle, remote(
+                block, block, self.sems.line_send.at[i, 4], self.sems.line_recv.at[i, first],
+                self.plan.device(self.coords, target, self.core),
+            )
+
+    def line_arrived(self, i, chip):
+        block = self.block(i, chip)
+        remote(
+            block, block, self.sems.line_send.at[i, 0], self.sems.line_recv.at[i, chip],
+            self.plan.device(self.coords, chip, self.core),
+        ).wait_recv()
 
     def axis_copies(self, i, step):
         rows = self.depth // 2
@@ -323,12 +348,25 @@
         return wide | (side != self.core), wide | (side == self.core)
 
     def start_line(self, i):
-        for copy in self.line_copies(i):
-            copy.start()
+        for there, copy in self.line_copies(i):
+            pl.when(there)(copy.start)
+
+    def pass_on(self, i):
+        for (here, copy), first in zip(self.pass_copies(i), (0, 3)):
+
+            @pl.when(here)
+            def _(copy=copy, first=first):
+                self.line_arrived(i, first)
+                copy.start()
 
     def start_axis(self, i, step):
-        for copy in self.line_copies(i) if step == 0 else self.axis_copies(i, step - 1):
-            copy.wait_recv()
+        if step == 0:
+            for chip in range(LINE):
+                passed = ((chip == 0) & (self.line == 2)) | ((chip == 3) & (self.line == 1))
+                pl.when((self.line != chip) & jnp.logical_not(passed))(functools.partial(self.line_arrived, i, chip))
+        else:
+            for copy in self.axis_copies(i, step - 1):
+                copy.wait_recv()
         for copy in self.axis_copies(i, step):
             copy.start()
 
@@ -343,8 +381,8 @@
         pl.when(gets)(lambda: self.core_copy(i, 1 - self.core).wait_recv())
 
     def drain(self, i):
-        for copy in self.line_copies(i):
-            copy.wait_send()
+        for there, copy in (*self.line_copies(i), *self.pass_copies(i)):
+            pl.when(there)(copy.wait_send)
         for step in range(len(self.plan.axes)):
             for copy in self.axis_copies(i, step):
                 copy.wait_send()
@@ -358,6 +396,7 @@
             pl.when((at >= 0) & (at < self.count))(functools.partial(body, at))
 
         guarded(i + ahead, self.start_line)
+        guarded(i + 1, self.pass_on)
         for step in range(steps):
             guarded(i - lag * step, lambda at, step=step: self.start_axis(at, step))
         guarded(i - lag * steps, self.start_core)
@@ -375,8 +414,8 @@
     steps = len(plan.axes)
     reach = max(plan.shape[a] for a in plan.axes) - 1
     return dict(
-        line_send=semaphores(count, LINE - 1),
-        line_recv=semaphores(count, LINE - 1),
+        line_send=semaphores(count, 5),
+        line_recv=semaphores(count, LINE),
         axis_send=semaphores(count, 2, steps, reach),
         axis_recv=semaphores(count, 2, steps, reach),
         core_send=semaphores(count),
@@ -396,25 +435,36 @@
     def here(self, chip, side):
         return (chip == self.line) & (side == self.core)
 
+    def add(self, src, dst, chip, side):
+        at = len(self.pieces)
+        device = self.plan.device(self.coords, chip, side)
+
+        def far(src, dst):
+            return remote(src, dst, self.send_sems.at[at], self.recv_sems.at[self.line, self.core], device)
+
+        near = pltpu.make_async_copy(src, dst, self.send_sems.at[at])
+        self.pieces.append((self.here(chip, side), src, dst, far, near))
+
+    def start(self, part=0, parts=1):
+        for stays, src, dst, far, near in self.pieces:
+            rows = src.shape[0] // parts
+            cut = pl.ds(pl.multiple_of(part * rows, rows), rows) if parts > 1 else slice(None)
+            pl.when(jnp.logical_not(stays))(far(src.at[cut], dst.at[cut]).start)
+            pl.when(stays & (part == 0))(near.start)
+
     def send(self, src, dst, chip, side):
-        at = len(self.pieces)
-        far = remote(
-            src, dst, self.send_sems.at[at], self.recv_sems.at[self.line, self.core],
-            self.plan.device(self.coords, chip, side),
-        )
-        near = pltpu.make_async_copy(src, dst, self.send_sems.at[at])
-        stays = self.here(chip, side)
-        self.pieces.append((stays, far, near))
-        pl.when(jnp.logical_not(stays))(far.start)
+        self.add(src, dst, chip, side)
+        stays, src, dst, far, near = self.pieces[-1]
+        pl.when(jnp.logical_not(stays))(far(src, dst).start)
         pl.when(stays)(near.start)
 
     def settle(self):
-        for stays, _, near in self.pieces:
+        for stays, *_, near in self.pieces:
             pl.when(stays)(near.wait)
 
     def drain(self):
-        for stays, far, _ in self.pieces:
-            pl.when(jnp.logical_not(stays))(far.wait_send)
+        for stays, src, dst, far, _ in self.pieces:
+            pl.when(jnp.logical_not(stays))(far(src, dst).wait_send)
 
     def receive(self, dst, chip, side):
         copy = remote(
@@ -448,6 +498,14 @@
     )
 
 
+def up_kind(j):
+    return FIRST_UP + j + jnp.maximum(j - 1, 0) if not isinstance(j, int) else FIRST_UP + j + max(j - 1, 0)
+
+
+def down_kind(j):
+    return jnp.minimum(FIRST_UP + 2 + 2 * j, KINDS - 1) if not isinstance(j, int) else min(FIRST_UP + 2 + 2 * j, KINDS - 1)
+
+
 def forward_inputs(plan, place, refs, scratch):
     coords, line, core = place
     source, prefix, meta = scratch.source, scratch.prefix, scratch.meta
@@ -463,9 +521,9 @@
     put(2, refs.w_value, 0)
     put(3, jnp.transpose(refs.w_attn_out[...]), 0)
     down = jnp.transpose(refs.w_down[...])
-    for j in range((KINDS - FIRST_UP) // 2):
-        put(FIRST_UP + 2 * j, refs.w_up, j * sides)
-        put(FIRST_UP + 2 * j + 1, down, j * sides)
+    for j in range(GROUPS):
+        put(up_kind(j), refs.w_up, j * sides)
+        put(down_kind(j), down, j * sides)
 
     slots = refs.prefix_keys.shape[1]
     prefix[...] = jnp.zeros_like(prefix)
@@ -504,6 +562,10 @@
 
 AHEAD = 3
 LAG = 2
+CUTS = 8
+TOKENS = 4
+ATT_BEATS = 2
+GRADS = 14
 
 
 def forward_backward_kernel(plan, names, *args):
@@ -532,33 +594,41 @@
     gather.start_line(1)
     token_line = Line(plan, place, sems.token_send, sems.token_recv)
     for j in range(held):
-        token_line.send(tokens.at[j], row.at[line, slot], base + j, core)
+        token_line.add(tokens.at[j], row.at[line, slot], base + j, core)
+    grad_line = Line(plan, place, sems.grad_send, sems.grad_recv)
+    for j in range(held):
+        grad_line.add(refs.out_grad.at[j], grad.at[lax.rem(line, 2), slot], base + j, line // 2)
     for copy in gather.own_copies():
         copy.start()
     for i in range(2, AHEAD):
         gather.start_line(i)
+    share = Sibling(plan, place, sems.share_send, sems.share_recv)
+    meta_copy = share.copy(meta, meta, 4)
+    if not spread:
+        pl.when(holds)(meta_copy.start)
+    for copy in gather.own_copies():
+        copy.wait()
+
+    last = gather.ticks(LAG)
+
+    grads = min(GRADS, last - CUTS)
+
+    def beat(i, x=0):
+        gather.tick(i, AHEAD, LAG)
+        pl.when((i >= TOKENS) & (i < TOKENS + CUTS))(lambda: token_line.start(i - TOKENS, CUTS))
+        pl.when((i >= grads) & (i < grads + CUTS))(lambda: grad_line.start(i - grads, CUTS))
+        return x
+
+    gather.pass_on(0)
+    steps = LAG * len(plan.axes) + 1
+    done = TOKENS + CUTS
+    lax.fori_loop(0, done, beat, 0)
     prefix_line = Line(plan, place, sems.prefix_send, sems.prefix_recv)
     for j in range(held):
         for side in range(plan.sides):
             prefix_line.send(
                 refs.prefix.at[j, side], pre.at[:, :, gather.lanes], base + j, core if spread else side
             )
-    share = Sibling(plan, place, sems.share_send, sems.share_recv)
-    meta_copy = share.copy(meta, meta, 4)
-    if not spread:
-        pl.when(holds)(meta_copy.start)
-    for copy in gather.own_copies():
-        copy.wait()
-
-    last = gather.ticks(LAG)
-
-    def beat(i, x=0):
-        gather.tick(i, AHEAD, LAG)
-        return x
-
-    steps = LAG * len(plan.axes) + 1
-    done = min(last, steps)
-    lax.fori_loop(0, done, beat, 0)
 
     token_line.settle()
 
@@ -574,9 +644,6 @@
 
     for chip in range(LINE):
         share_token(chip)
-    grad_line = Line(plan, place, sems.grad_send, sems.grad_recv)
-    for j in range(held):
-        grad_line.send(refs.out_grad.at[j], grad.at[lax.rem(line, 2), slot], base + j, line // 2)
     for chip in range(LINE):
         if spread:
             share.copy(row.at[chip, 1 - core], row.at[chip, 1 - core], chip).wait_recv()
@@ -612,11 +679,14 @@
             return x
 
         lax.fori_loop(0, LINE, project, 0)
+        beat(done)
+        done = done + 1
     kept = ((q, refs.q_out), (k, refs.k_out), (v, refs.v_out), (pre, refs.pre_out), (meta, refs.meta_out))
     keep = [publish(ref, out, at) for at, (ref, out) in enumerate(kept)]
     keep.append(pltpu.make_async_copy(whole.at[pl.ds(0, 3), core], refs.w_out, sems.publish.at[5]))
     for copy in keep:
         copy.start()
+
 
     att_share = Sibling(plan, place, sems.att_send, sems.att_recv)
     here = pl.ds(pl.multiple_of(core * half, half), half)
@@ -647,16 +717,16 @@
             return x
 
         lax.fori_loop(0, blocks // 2, block, 0)
-        beat(done + plan.sides * p)
+        beat(done + ATT_BEATS * p)
         lax.fori_loop(blocks // 2, blocks, block, 0)
-        if plan.sides > 1:
-            beat(done + plan.sides * p + 1)
+        if ATT_BEATS > 1:
+            beat(done + ATT_BEATS * p + 1)
         att_copy(p).start()
         return x
 
     pairs = WIDE // PAIR
     lax.fori_loop(0, pairs, pair, 0)
-    done = min(last, done + plan.sides * pairs)
+    done = done + ATT_BEATS * pairs
     keep += [publish(att, refs.att_out, 6), publish(lse, refs.lse_out, 7)]
     for copy in keep[-2:]:
         copy.start()
@@ -682,40 +752,48 @@
         low_normed = (normal * refs.gain_one[...] + refs.shift_one[...]).astype(bf16)
         normed[rows, :] = low_normed
         acc[rows, :] = low_normed.astype(f32)
+        beat(done + b)
         return x
 
     lax.fori_loop(0, parts, mix, 0)
-
-    def feed(n, x):
-        j, side = n // 2, lax.rem(n, 2)
-        kind = FIRST_UP + 2 * j
-
-        def part(b, x):
-            rows = pl.ds(pl.multiple_of(b * CHUNK, CHUNK), CHUNK)
-            upper = mm(normed[rows, :], weight(kind, side))
-            bell = (1.0 + lax.erf(upper * (0.5**0.5))) * 0.5
-            acted = (upper * bell).astype(bf16)
-            slope[n, rows, :] = (
-                bell + upper * jnp.exp(upper * upper * -0.5) * (1.0 / (2.0 * math.pi) ** 0.5)
-            ).astype(bf16)
-            acc[rows, :] += mm_nt(acted, weight(kind + 1, side))
+    done = done + parts
+
+    acted = refs.acted
+    chunks = [slice(b * CHUNK, (b + 1) * CHUNK) for b in range(parts)]
+
+    def act(j, done):
+        def unit(side, x):
+            for rows in chunks:
+                upper = mm(normed[rows, :], weight(up_kind(j), side))
+                bell = (1.0 + lax.erf(upper * (0.5**0.5))) * 0.5
+                acted[2 * j + side, rows, :] = (upper * bell).astype(bf16)
+                slope[2 * j + side, rows, :] = (
+                    bell + upper * jnp.exp(upper * upper * -0.5) * (1.0 / (2.0 * math.pi) ** 0.5)
+                ).astype(bf16)
+            if done < last:
+                beat(done + side)
             return x
 
-        lax.fori_loop(0, parts, part, 0)
-        return x
-
-    groups = (KINDS - FIRST_UP) // 2
-    for j in range(groups):
-        done = ready((FIRST_UP + 2 * j) * plan.sides, 2 * plan.sides, done)
-        lax.fori_loop(2 * j, 2 * j + 2, feed, 0)
+        lax.fori_loop(0, 2, unit, 0)
+
+    def add(j, done):
+        def unit(side, x):
+            for rows in chunks:
+                acc[rows, :] += mm_nt(acted[2 * j + side, rows, :], weight(down_kind(j), side))
+            return x
+
+        lax.fori_loop(0, 2, unit, 0)
+
+    steps_of = sorted([(up_kind(j), act, j) for j in range(GROUPS)] + [(down_kind(j), add, j) for j in range(GROUPS)], key=lambda s: s[0])
+    for kind, body, j in steps_of:
+        done = ready(kind * plan.sides, plan.sides, done)
+        body(j, done)
+        done = done + 2 if body is act else done
 
     grad_line.settle()
     for part in range(2):
         for side in range(plan.cores):
             grad_line.receive(grad.at[part, side], 2 * core + part, side if spread else line // 2)
-
-    back = Line(plan, place, sems.back_send, sems.back_recv)
-    places = tokens.shape[1]
 
     def close(b, x):
         rows = pl.ds(pl.multiple_of(b * CHUNK, CHUNK), CHUNK)
@@ -729,29 +807,18 @@
         return x
 
     lax.fori_loop(0, parts, close, 0)
-    for b in range(2):
-        for side in range(plan.cores):
-            spot, target = (line, side) if spread else (lax.rem(line, 2), line // 2)
-            back.send(
-                out.at[pl.ds((b * plan.cores + side) * places, places)], refs.pieces.at[spot],
-                2 * core + b, target,
-            )
+    keep.append(publish(out, refs.out_out, 10))
+    keep[-1].start()
 
     def feed_back(n, x):
         j, side = n // 2, lax.rem(n, 2)
-        kind = FIRST_UP + 2 * j
-
-        def part(b, x):
-            rows = pl.ds(pl.multiple_of(b * CHUNK, CHUNK), CHUNK)
-            d_acted = mm(low[rows, :], weight(kind + 1, side))
+        for rows in chunks:
+            d_acted = mm(low[rows, :], weight(down_kind(j), side))
             d_upper = (d_acted * slope[n, rows, :].astype(f32)).astype(bf16)
-            acc[rows, :] += mm_nt(d_upper, weight(kind, side))
-            return x
-
-        lax.fori_loop(0, parts, part, 0)
+            acc[rows, :] += mm_nt(d_upper, weight(up_kind(j), side))
         return x
 
-    lax.fori_loop(0, 2 * groups, feed_back, 0)
+    lax.fori_loop(0, 2 * GROUPS, feed_back, 0)
 
     d_att, away = refs.d_att, refs.d_att_away
     d_share = Sibling(plan, place, sems.d_send, sems.d_recv)
@@ -794,10 +861,6 @@
         att_copy(p).wait_send()
     for b in range(parts):
         d_copy(b).wait_send()
-    back.settle()
-    for j in range(held):
-        back.receive(refs.pieces.at[j], j if spread else 2 * core + j, line // 2)
-    back.drain()
     for copy in keep:
         copy.wait()
 
@@ -821,9 +884,8 @@
         d_att_out=S((length, WIDE), bf16),
         d_first_out=S((half, width), f32),
         w_out=S((3,) + plan.shape + (depth, WIDE), bf16),
-        pieces=S((held, places, width), bf16),
-    )
-    units = 2 * (KINDS - FIRST_UP) // 2
+        out_out=S((half, width), bf16),
+    )
     scratch = dict(
         source=((KINDS, plan.sides, depth, LANES), bf16),
         prefix=((held, plan.sides, 2, SLOTS, LANES), bf16),
@@ -844,7 +906,8 @@
         normal_one=((half, width), f32),
         rstd_one=((half, LANES), f32),
         normed=((half, width), bf16),
-        slope=((units, half, WIDE), bf16),
+        slope=((2 * GROUPS, half, WIDE), bf16),
+        acted=((2 * GROUPS, half, WIDE), bf16),
         acc=((half, width), f32),
         low=((half, width), bf16),
         out=((half, width), bf16),
@@ -859,15 +922,13 @@
         prefix_recv=semaphores(LINE, 2),
         grad_send=semaphores(held),
         grad_recv=semaphores(LINE, 2),
-        back_send=semaphores(4),
-        back_recv=semaphores(LINE, 2),
         share_send=semaphores(5),
         share_recv=semaphores(5),
         att_send=semaphores(pairs),
         att_recv=semaphores(pairs),
         d_send=semaphores(half // CHUNK),
         d_recv=semaphores(half // CHUNK),
-        publish=semaphores(10),
+        publish=semaphores(11),
     )
     smem = pl.BlockSpec(memory_space=pltpu.SMEM)
     vmem = pl.BlockSpec(memory_space=pltpu.VMEM)
@@ -1046,6 +1107,34 @@
         ),
     )(*vars(given).values())
     return results
+
+
+def hand_out(plan, part, held, places):
+    _, line, core = plan.here()
+    count = 2 * plan.cores
+    piece = lax.rem(line, 2) * plan.cores + (core if plan.core_in_tp else 0)
+    pieces = part.reshape(count, places, -1)
+    a, b, c = plan.shape
+    got = []
+    for k in range(count):
+        pairs = []
+        for place in itertools.product(range(a), range(b), range(c), range(LINE), range(2)):
+            coords, chip, side = place[:3], place[3], place[4]
+            if not plan.core_in_tp and coords[2] != side:
+                continue
+            which = (chip % count) ^ k
+            target = which % 2 if plan.core_in_tp else chip // 2
+            ends = plan.device(coords, chip, side), plan.device(coords, 2 * side + which // plan.cores, target)
+            pairs.append(tuple(r * plan.tp + t for r, t in ends))
+        mine = lax.dynamic_index_in_dim(pieces, lax.rem(line, count) ^ k, 0, keepdims=False)
+        got.append(lax.ppermute(mine, ("rows", "tp"), pairs))
+    slots = []
+    for j in range(held):
+        slot = got[0]
+        for k in range(1, count):
+            slot = jnp.where(piece ^ j == k, got[k], slot)
+        slots.append(slot)
+    return jnp.stack(slots)
 
 
 def shards(
@@ -1077,6 +1166,7 @@
             prefix_values=prefix_values,
         ),
     )
+    output = hand_out(plan, done.out_out, held, places)
     dq, dk, dv, d_pre = attend_backward(
         example_lengths.shape[1], done.q_out, done.k_out, done.v_out, done.d_att_out, done.att_out,
         done.pre_out, done.lse_out, done.meta_out,
@@ -1087,7 +1177,7 @@
             dq=dq, dk=dk, dv=dv, w=done.w_out, d_first=done.d_first_out, d_pre=d_pre, meta=done.meta_out
         ),
     )
-    return done.pieces, d_tokens.astype(jnp.float32), keys_grad, values_grad
+    return output, d_tokens.astype(jnp.float32), keys_grad, values_grad
 
 
 def solution(mesh):

time: 294 us -> 264 us (0.90)
  the two profiles are of different devices: /device:TPU:0 before, /device:TPU:9 now
where the time goes in v4:
time: 264 us
  Pallas kernels  245 us (93%)
  local copies, waits for them, and re-layouts  10.5 us (4%)
  other arithmetic  3.91 us (1%)
  starting transfers between devices  3.51 us (1%)
    pallas_call x1, Pallas kernels, forward_backward(): pl.pallas_call(functools.partial(forward_backward_kernel, plan, (*vars(gi...  160 us
    pallas_call x1, Pallas kernels, attend_backward(): pl.pallas_call(functools.partial(backward_kernel, examples), grid=(pairs,...  47.3 us
    pallas_call x1, Pallas kernels, finish(): pl.pallas_call(functools.partial(finish_kernel, plan, (*vars(given), *out...  37.1 us
    unnamed x18, local copies, waits for them, and re-layouts  8.15 us
  transfers between devices with their start and end apart: 2, of which 0 were waited for; matrix products, arithmetic and copies ran while one was open for 1% of the time, Pallas kernels for 32%

profile of v4, /device:TPU:9, one launch (start us, length us, event | category | flops | bytes accessed | tf_op | source)
XLA Modules:
  0.0 263.6 jit_solution(6235436835071944957)
XLA Ops:
  0.6 1.6 copy.22.args_16_
  2.3 1.6 copy.23.args_17_
  3.9 160.5 %shard_map.201 = (bf16[1024,512]{1,0:T(8,128)(2,1)}, bf16[1024,512]{1,0:T(8,128)(2,1)}, bf16[1024,512]{1,0:T(8,128)(2,1)}, bf16[1024,512]{1,0:T(8,128)(2,1)}, f3...) custom-call(s32[2]{0:T(128)} %args_0_.4, ...), custom_call_target="tpu_custom_call" | custom-call | tf_op jit(solution)/shard_map/pallas_call | solution.py:936
  164.4 0.0 copy-start.2
  164.4 0.0 copy-start.3
  164.4 0.0 copy-start.5
  164.4 0.0 copy-start.6
  164.4 2.4 dynamic-slice_bitcast_fusion
  166.8 3.4 %collective-permute-start.1 = (bf16[256,1024]{1,0:T(8,128)(2,1)}, bf16[256,1024]{1,0:T(8,128)(2,1)}, u32[]{:S(2)}, u32[]{:S(2)}) collective-permute-start(bf16[256,1024]{1,0:T(8,128)(2,1)} %get-tuple-element.46), channel_id=1, source_target_pairs={{0,0},{1,1},{2,4},{3,5},{4,2},{5,3},{6,6},{7,7},{8,8},{9,9},{10,12... | collective-permute-start | bytes 1572872 | tf_op jit(solution)/shard_map/ppermute | solution.py:1130
  170.3 0.1 collective-permute-start
  170.3 0.0 copy-done.2
  170.4 0.0 copy-done.3
  170.4 0.0 copy-done.5
  170.4 0.0 copy-done.6
  170.4 0.0 copy-start.4
  170.4 1.2 copy-done.4
  171.6 47.3 %shard_map.202 = (bf16[1024,512]{1,0:T(8,128)(2,1)S(1)}, bf16[1024,512]{1,0:T(8,128)(2,1)S(1)}, bf16[1024,512]{1,0:T(8,128)(2,1)S(1)}, f32[2,128,512]{2,1,0:T(8,128)S(1)}) custom-call(f32[8,1152]{1,0:T(8,128)S(1)} %copy-done.2, bf16[1024,512]{1,0:T(8,128)(2,1)S(1)} %copy-done.3, bf16[1024,512]{1,0:T(8,128)(2,1)S(1)} %copy-done.4, ...), custom_call_target="tpu_custom_call" | custom-call | flops 21474836480 | bytes 8388608 | tf_op jit(solution)/shard_map/pallas_call | solution.py:163
  218.9 0.0 copy-start
  218.9 0.8 copy-done
  219.7 0.0 copy-start.1
  219.7 1.0 copy-done.1
  220.7 37.1 %shard_map.203 = (bf16[2,256,1024]{2,1,0:T(8,128)(2,1)S(1)}, f32[4,100,256]{2,1,0:T(8,128)S(1)}, f32[4,100,256]{2,1,0:T(8,128)S(1)}) custom-call(bf16[1024,512]{1,0:T(8,128)(2,1)S(1)} %get-tuple-element.31.args_0_, bf16[1024,512]{1,0:T(8,128)(2,1)S(1)} %get-tuple-element.32.args_1_, bf16[1024,512]{1,0:T(8,128)(2,1)S(1)} %get-tuple-element.33.args_2_, ...), custom_call_target="tpu_custom_call" | custom-call | tf_op jit(solution)/shard_map/pallas_call | solution.py:1099
  257.8 0.9 copy.24
  258.7 0.9 copy.25
  259.7 1.6 convert_element_type.3
  261.2 0.0 collective-permute-done.1
  261.2 0.0 collective-permute-done
  261.2 1.3 select_bitcast_fusion.1
  262.5 1.1 pad_maximum_fusion
Async XLA Ops:
  164.4 5.9 %copy-start.2 = (f32[8,1152]{1,0:T(8,128)S(1)}, f32[8,1152]{1,0:T(8,128)}, u32[]{:S(2)}) copy-start(f32[8,1152]{1,0:T(8,128)} %get-tuple-element.23.ends_ref.meta_ref.args_6_) | copy-start | bytes 110596
  164.4 5.9 %copy-start.3 = (bf16[1024,512]{1,0:T(8,128)(2,1)S(1)}, bf16[1024,512]{1,0:T(8,128)(2,1)}, u32[]{:S(2)}) copy-start(bf16[1024,512]{1,0:T(8,128)(2,1)} %get-tuple-element.24.q_ref) | copy-start | bytes 3145732
  164.4 5.9 %copy-start.5 = (bf16[2,128,512]{2,1,0:T(8,128)(2,1)S(1)}, bf16[2,128,512]{2,1,0:T(8,128)(2,1)}, u32[]{:S(2)}) copy-start(bf16[2,128,512]{2,1,0:T(8,128)(2,1)} %get-tuple-element.29.pre_ref) | copy-start | bytes 786436
  164.4 5.9 %copy-start.6 = (f32[4,8,1024]{2,1,0:T(8,128)S(1)}, f32[4,8,1024]{2,1,0:T(8,128)}, u32[]{:S(2)}) copy-start(f32[4,8,1024]{2,1,0:T(8,128)} %get-tuple-element.30.lse_ref) | copy-start | bytes 393220
  166.8 94.4 %collective-permute-start.1 = (bf16[256,1024]{1,0:T(8,128)(2,1)}, bf16[256,1024]{1,0:T(8,128)(2,1)}, u32[]{:S(2)}, u32[]{:S(2)}) collective-permute-start(bf16[256,1024]{1,0:T(8,128)(2,1)} %get-tuple-element.46), channel_id=1, source_target_pairs={{0,0},{1,1},{2,4},{3,5},{4,2},{5,3},{6,6},{7,7},{8,8},{9,9},{10,12... | collective-permute-start | bytes 1572872 | tf_op jit(solution)/shard_map/ppermute | solution.py:1130
  170.3 91.0 %collective-permute-start = (bf16[256,1024]{1,0:T(8,128)(2,1)}, bf16[256,1024]{1,0:T(8,128)(2,1)}, u32[]{:S(2)}, u32[]{:S(2)}) collective-permute-start(bf16[256,1024]{1,0:T(8,128)(2,1)} %get-tuple-element.47), channel_id=1, source_target_pairs={{0,1},{1,0},{2,5},{3,4},{4,3},{5,2},{6,7},{7,6},{8,9},{9,8},{10,13... | collective-permute-start | bytes 1572872 | tf_op jit(solution)/shard_map/ppermute | solution.py:1130
  170.4 1.2 copy-start.4
  218.9 0.8 copy-start
  219.7 1.0 copy-start.1

commit v5 on v4

--- a/solution.py
+++ b/solution.py
@@ -1,5 +1,4 @@
 import functools
-import itertools
 import math
 from types import SimpleNamespace
 
@@ -15,6 +14,7 @@
 SLOTS = 128
 QB = 256
 KB = 256
+REACH = 512
 NEG = -1e30
 NT = (((1,), (1,)), ((), ()))
 
@@ -59,132 +59,30 @@
     return mixed.astype(jnp.bfloat16), totals
 
 
-def backward_kernel(
-    examples, ends_ref, q_ref, k_ref, v_ref, do_ref, att_ref, pre_ref, lse_ref, meta_ref,
-    dq_ref, dk_ref, dv_ref, dpre_ref,
-    dk_acc, dv_acc, dpk_acc, dpv_acc, k_t, pk_t, columns,
-):
-    length = q_ref.shape[0]
-    pk_ref, pv_ref = pre_ref.at[0], pre_ref.at[1]
-    live_ref, seg_ref = columns.at[0:SLOTS], columns.at[SLOTS:]
-
-    @pl.when(pl.program_id(0) == 0)
-    def _():
-        columns[...] = jnp.transpose(meta_ref[...])
-
-    dk_acc[...] = jnp.zeros_like(dk_acc)
-    dv_acc[...] = jnp.zeros_like(dv_acc)
-    dpk_acc[...] = jnp.zeros_like(dpk_acc)
-    dpv_acc[...] = jnp.zeros_like(dpv_acc)
-    k_t[...] = jnp.transpose(k_ref[...])
-    pk_t[...] = jnp.transpose(pk_ref[...])
+def inner_rows(do, att):
     picks = lax.broadcasted_iota(jnp.int32, (8, PAIR), 0)
     lanes = lax.broadcasted_iota(jnp.int32, (8, PAIR), 1) // HD
-    picker = jnp.where(picks == lanes, 1.0, 0.0)
-
-    def bounds(start):
-        low, high = jnp.int32(0), jnp.int32(length)
-        for j in range(examples):
-            end = ends_ref[2, j].astype(jnp.int32)
-            low = jnp.where(end <= start, jnp.maximum(low, end), low)
-            high = jnp.where(end >= start + QB, jnp.minimum(high, end), high)
-        return low // KB, (high + KB - 1) // KB
-
-    def block(b, carry):
-        start = pl.multiple_of(b * QB, QB)
-        rows = pl.ds(start, QB)
-        q = q_ref[rows, :]
-        do = do_ref[rows, :]
-        prod = do.astype(jnp.float32) * att_ref[rows, :].astype(jnp.float32)
-        inner = lax.dot_general(
-            picker, prod, NT, preferred_element_type=jnp.float32, precision=lax.Precision.HIGHEST
-        )
-        seg_q = meta_ref[0:1, pl.ds(SLOTS + start, QB)]
-        heads = []
-        for half in range(2):
-            qh = only_head(q, half) * jnp.asarray(0.125, jnp.bfloat16)
-            dh = only_head(do, half)
-            lse = lse_ref[0, half : half + 1, rows]
-            delta = inner[half : half + 1, :]
-            heads.append((qh, dh, lse, delta))
-
-        def tile(kk, vv, kt, allowed, half):
-            qh, dh, lse, delta = heads[half]
-            s = mm_nt(kk, qh)
-            p = jnp.exp(jnp.where(allowed, s, NEG) - lse)
-            dp = mm_nt(vv, dh)
-            ds = (p * (dp - delta)).astype(jnp.bfloat16)
-            return mm(ds, qh), mm(p.astype(jnp.bfloat16), dh), mm(kt, ds)
-
-        dqs = []
-        for half in range(2):
-            a, g, dq = tile(
-                pk_ref[...], pv_ref[...], pk_t[half * HD : (half + 1) * HD, :], live_ref[:, 0:1] > 0.5, half
-            )
-            dpk_acc[...] += a
-            dpv_acc[...] += g
-            dqs.append(dq)
-
-        def step(j, dqs):
-            at = pl.multiple_of(j * KB, KB)
-            krows = pl.ds(at, KB)
-            allowed = seg_ref[krows, 0:1] == seg_q
-            dk = dk_acc[krows, :]
-            dv = dv_acc[krows, :]
-            outs = []
-            for half in range(2):
-                a, g, dq = tile(
-                    k_ref[krows, :], v_ref[krows, :], k_t[half * HD : (half + 1) * HD, krows], allowed, half
-                )
-                dk = dk + a
-                dv = dv + g
-                outs.append(dqs[half] + dq)
-            dk_acc[krows, :] = dk
-            dv_acc[krows, :] = dv
-            return tuple(outs)
-
-        dqs = lax.fori_loop(*bounds(start), step, tuple(dqs))
-        dq_ref[rows, :] = (jnp.transpose(jnp.concatenate(dqs, axis=0)) * 0.125).astype(jnp.bfloat16)
-        return carry
-
-    lax.fori_loop(0, length // QB, block, 0)
-    dk_ref[...] = dk_acc[...].astype(jnp.bfloat16)
-    dv_ref[...] = dv_acc[...].astype(jnp.bfloat16)
-    dpre_ref[0] = dpk_acc[...]
-    dpre_ref[1] = dpv_acc[...]
-
-
-def attend_backward(examples, q, k, v, do, att, pre, lse, meta):
-    length, width = q.shape
-    pairs = width // PAIR
-    block = pl.BlockSpec((length, PAIR), lambda p: (0, p))
-    pre_block = pl.BlockSpec((2, SLOTS, PAIR), lambda p: (0, 0, p))
-    low = jax.ShapeDtypeStruct((length, width), jnp.bfloat16)
-    return pl.pallas_call(
-        functools.partial(backward_kernel, examples),
-        grid=(pairs,),
-        in_specs=[
-            pl.BlockSpec((8, SLOTS), lambda p: (0, 0), memory_space=pltpu.SMEM),
-            block, block, block, block, block, pre_block,
-            pl.BlockSpec((1, 8, length), lambda p: (p, 0, 0)),
-            pl.BlockSpec(meta.shape, lambda p: (0, 0)),
-        ],
-        out_specs=[block, block, block, pre_block],
-        out_shape=[low, low, low, jax.ShapeDtypeStruct((2, SLOTS, width), jnp.float32)],
-        scratch_shapes=[
-            pltpu.VMEM((length, PAIR), jnp.float32),
-            pltpu.VMEM((length, PAIR), jnp.float32),
-            pltpu.VMEM((SLOTS, PAIR), jnp.float32),
-            pltpu.VMEM((SLOTS, PAIR), jnp.float32),
-            pltpu.VMEM((PAIR, length), jnp.bfloat16),
-            pltpu.VMEM((PAIR, SLOTS), jnp.bfloat16),
-            pltpu.VMEM((meta.shape[1], 8), jnp.float32),
-        ],
-        compiler_params=pltpu.CompilerParams(vmem_limit_bytes=48 * 2**20),
-        cost_estimate=pl.CostEstimate(
-            flops=40 * length * length * width, bytes_accessed=16 * length * width, transcendentals=0
-        ),
-    )(meta, q, k, v, do, att, pre, lse, meta)
+    picker = jnp.where(picks == lanes, 1.0, 0.0).astype(jnp.bfloat16)
+    prod = do.astype(jnp.float32) * att.astype(jnp.float32)
+    high = prod.astype(jnp.bfloat16)
+    return mm_nt(picker, high) + mm_nt(picker, (prod - high.astype(jnp.float32)).astype(jnp.bfloat16))
+
+
+def gradient_tile(keys, values, q, do, rows, allowed):
+    back = jnp.transpose(keys)
+    d_keys = jnp.zeros(keys.shape, jnp.float32)
+    d_values = jnp.zeros(keys.shape, jnp.float32)
+    d_query = []
+    scaled = q * jnp.asarray(0.125, jnp.bfloat16)
+    for half in range(2):
+        qh, dh = only_head(scaled, half), only_head(do, half)
+        scores = jnp.where(allowed, mm_nt(keys, qh), NEG)
+        probs = jnp.exp(scores - rows[half : half + 1, :])
+        d_scores = (probs * (mm_nt(values, dh) - rows[2 + half : 3 + half, :])).astype(jnp.bfloat16)
+        d_keys = d_keys + mm(d_scores, qh)
+        d_values = d_values + mm(probs.astype(jnp.bfloat16), dh)
+        d_query.append(mm(back[half * HD : (half + 1) * HD, :], d_scores))
+    return d_keys, d_values, jnp.concatenate(d_query, axis=0)
 
 
 MESH = pl.DeviceIdType.MESH
@@ -482,6 +380,105 @@
 
     def copy(self, src, dst, at):
         return remote(src, dst, self.send_sems.at[at], self.recv_sems.at[at], self.device)
+
+
+class PrefixSum:
+    def __init__(self, plan, place, refs):
+        self.plan = plan
+        self.place = place
+        self.refs = refs
+        self.coords, self.line, self.core = place
+        self.terms = Line(plan, place, refs.terms_send, refs.terms_recv)
+        self.last = Sibling(plan, place, refs.total_send, refs.total_recv)
+
+    def start(self):
+        refs = self.refs
+        for chip in range(LINE):
+            lanes = slice(chip * LANES, (chip + 1) * LANES)
+            for which in range(2):
+                refs.terms[chip, which] = refs.d_pre[which, :, lanes].astype(jnp.bfloat16)
+            refs.terms[chip, 0, SLOTS - 16 :, :] = jnp.broadcast_to(refs.meta[1:2, 0:SLOTS], (16, SLOTS)).astype(
+                jnp.bfloat16
+            )
+        for chip in range(LINE):
+            self.terms.send(refs.terms.at[chip], refs.row_terms.at[self.line], chip, self.core)
+
+    def copies(self, step):
+        refs = self.refs
+        axis = self.plan.axes[step]
+        size = self.plan.shape[axis]
+        return [
+            remote(
+                refs.gone.at[step], refs.come.at[step, by - 1], refs.sum_send.at[step, by - 1],
+                refs.sum_recv.at[step, by - 1],
+                self.plan.device(shifted(self.coords, axis, by, size), self.line, self.core),
+            )
+            for by in range(1, size)
+        ]
+
+    def send(self, step):
+        self.refs.gone[step] = self.refs.total[...].astype(jnp.bfloat16)
+        for copy in self.copies(step):
+            copy.start()
+
+    def line_sum(self):
+        refs = self.refs
+        total = refs.total
+        tasks, _, kept = total.shape[:3]
+        self.terms.settle()
+        for chip in range(LINE):
+            self.terms.receive(refs.row_terms.at[chip], chip, self.core)
+            marks = refs.row_terms[chip, 0, SLOTS - 16 :, :].astype(jnp.float32)
+            for task in range(tasks):
+                for which in range(2):
+                    more = refs.row_terms[chip, which, 0:kept, :].astype(jnp.float32) * marks[0:1, task : task + 1]
+                    total[task, which] = more if chip == 0 else total[task, which] + more
+
+    def receive(self, step):
+        for by, copy in enumerate(self.copies(step)):
+            copy.wait_recv()
+            self.refs.total[...] += self.refs.come[step, by].astype(jnp.float32)
+
+    def go_on(self, beat):
+        steps = len(self.plan.axes)
+        if beat == 0:
+            self.line_sum()
+        elif beat <= steps:
+            self.receive(beat - 1)
+        if beat < steps:
+            self.send(beat)
+        elif beat == steps and not self.plan.core_in_tp:
+            self.last.copy(self.refs.total, self.refs.total_other, 0).start()
+
+    def put(self, block, lanes):
+        refs = self.refs
+        tasks, slots = refs.keys_grad.shape[:2]
+        for task in range(tasks):
+            refs.keys_grad[task, :, lanes] = block[task, 0, 0:slots, :]
+            refs.values_grad[task, :, lanes] = block[task, 1, 0:slots, :]
+
+    def finish(self, beats):
+        refs = self.refs
+        steps = len(self.plan.axes)
+        for beat in range(beats, steps + 1):
+            self.go_on(beat)
+        if self.plan.core_in_tp:
+            self.put(refs.total, slice(None))
+        else:
+            self.last.copy(refs.total, refs.total_other, 0).wait_recv()
+            sides = slice(0, LANES), slice(LANES, 2 * LANES)
+            for side in range(2):
+
+                @pl.when(self.core == side)
+                def _(side=side):
+                    self.put(refs.total, sides[side])
+                    self.put(refs.total_other, sides[1 - side])
+
+            self.last.copy(refs.total, refs.total_other, 0).wait_send()
+        self.terms.drain()
+        for step in range(steps):
+            for copy in self.copies(step):
+                copy.wait_send()
 
 
 def normalise(z):
@@ -656,9 +653,6 @@
         prefix_line.receive(pre.at[:, :, pl.ds(chip * LANES, LANES)], chip, core if spread else line // 2)
     refs.meta_cols[...] = jnp.transpose(meta[...])
 
-    def publish(ref, out, at):
-        return pltpu.make_async_copy(ref, out, sems.publish.at[at])
-
     def ready(first, amount, done):
         until = min(last, first + amount - 1 + steps)
         if until > done:
@@ -681,21 +675,17 @@
         lax.fori_loop(0, LINE, project, 0)
         beat(done)
         done = done + 1
-    kept = ((q, refs.q_out), (k, refs.k_out), (v, refs.v_out), (pre, refs.pre_out), (meta, refs.meta_out))
-    keep = [publish(ref, out, at) for at, (ref, out) in enumerate(kept)]
-    keep.append(pltpu.make_async_copy(whole.at[pl.ds(0, 3), core], refs.w_out, sems.publish.at[5]))
-    for copy in keep:
-        copy.start()
-
-
     att_share = Sibling(plan, place, sems.att_send, sems.att_recv)
     here = pl.ds(pl.multiple_of(core * half, half), half)
     there = pl.ds(pl.multiple_of((1 - core) * half, half), half)
     keys, values = refs.keys, refs.values
     blocks = length // QB
 
+    def pair_lanes(p):
+        return pl.ds(pl.multiple_of(p * PAIR, PAIR), PAIR)
+
     def att_copy(p):
-        lanes = pl.ds(pl.multiple_of(p * PAIR, PAIR), PAIR)
+        lanes = pair_lanes(p)
         return att_share.copy(att.at[there, lanes], refs.att_other.at[:, lanes], p)
 
     def pair(p, x):
@@ -727,9 +717,6 @@
     pairs = WIDE // PAIR
     lax.fori_loop(0, pairs, pair, 0)
     done = done + ATT_BEATS * pairs
-    keep += [publish(att, refs.att_out, 6), publish(lse, refs.lse_out, 7)]
-    for copy in keep[-2:]:
-        copy.start()
     for p in range(pairs):
         att_copy(p).wait_recv()
 
@@ -807,8 +794,15 @@
         return x
 
     lax.fori_loop(0, parts, close, 0)
-    keep.append(publish(out, refs.out_out, 10))
-    keep[-1].start()
+    places = tokens.shape[1]
+    out_back = Line(plan, place, sems.out_send, sems.out_recv)
+    for b in range(2):
+        for side in range(plan.cores):
+            spot, target = (line, side) if spread else (lax.rem(line, 2), line // 2)
+            out_back.send(
+                out.at[pl.ds((b * plan.cores + side) * places, places)], refs.pieces.at[spot],
+                2 * core + b, target,
+            )
 
     def feed_back(n, x):
         j, side = n // 2, lax.rem(n, 2)
@@ -839,30 +833,139 @@
         return x
 
     lax.fori_loop(0, parts, open_, 0)
-    keep.append(publish(acc, refs.d_first_out, 8))
-    keep[-1].start()
     for b in range(parts):
         d_copy(b).wait_recv()
-    keep.append(publish(d_att, refs.d_att_out, 9))
-    keep[-1].start()
-
-    lax.fori_loop(0, gather.count, lambda i, x: (gather.drain(i), x)[1], 0)
-    token_line.drain()
-    prefix_line.drain()
-    grad_line.drain()
+
+    def pair_inner(p, x):
+        lanes = pair_lanes(p)
+        lse[p, 2:4, :] = inner_rows(d_att[:, lanes], att[:, lanes])[0:2]
+        return x
+
+    lax.fori_loop(0, pairs, pair_inner, 0)
+    columns, dq_acc = refs.meta_cols, normal_one
+    d_queries, d_keys, d_values = (
+        acted.at[pl.ds(n * length // half, length // half)] for n in range(3)
+    )
+    d_pre = refs.d_pre
+
+    def prefix_pair(p, x):
+        lanes = pair_lanes(p)
+        live = columns[0:SLOTS, 0:1] > 0.5
+        a, g, dq = gradient_tile(pre[0, :, lanes], pre[1, :, lanes], q[:, lanes], d_att[:, lanes], lse[p], live)
+        d_pre[0, :, lanes] = a
+        d_pre[1, :, lanes] = g
+        dq_acc[lanes, :] = dq
+        return x
+
+    lax.fori_loop(0, pairs, prefix_pair, 0)
+    prefix_sum = PrefixSum(plan, place, refs)
+    prefix_sum.start()
+
+    def key_block(kb, first, count):
+        rows = pl.ds(pl.multiple_of(kb * KB, KB), KB)
+        span = pl.ds(pl.multiple_of(first * KB, KB), count * KB)
+        seg_k = columns[pl.ds(pl.multiple_of(SLOTS + kb * KB, SLOTS), KB), 0:1]
+        part, at = kb * KB // half, pl.ds(pl.multiple_of(lax.rem(kb * KB, half), KB), KB)
+
+        def one(p, x):
+            lanes = pair_lanes(p)
+            allowed = seg_k == meta[0:1, pl.ds(pl.multiple_of(SLOTS + first * KB, SLOTS), count * KB)]
+            a, g, dq = gradient_tile(
+                k[rows, lanes], v[rows, lanes], q[span, lanes], d_att[span, lanes], lse[p, :, span], allowed
+            )
+            d_keys[part, at, lanes] = a.astype(bf16)
+            d_values[part, at, lanes] = g.astype(bf16)
+            dq_acc[lanes, span] += dq
+            return x
+
+        lax.fori_loop(0, pairs, one, 0)
+
+    swap = Sibling(plan, place, sems.swap_send, sems.swap_recv)
+    spare = row
+    own_blocks = half // KB
     for chip in range(LINE):
         if spread:
             share.copy(row.at[chip, core], row.at[chip, core], chip).wait_send()
         else:
             pl.when(holds)(share.copy(row.at[chip, 0], row.at[chip, 0], chip).wait_send)
+
+    def swap_copy(i):
+        return swap.copy(spare.at[i], spare.at[own_blocks + i], i)
+
+    def grad_pieces(i):
+        for side in range(plan.cores):
+            spot, target = (line, side) if spread else (lax.rem(line, 2), line // 2)
+            chip = own_blocks * core + i
+            src = low.at[pl.ds(pl.multiple_of(i * KB + side * places, places), places)]
+            dst = refs.grad_pieces.at[spot]
+            stays = (chip == line) & (target == core)
+            sem = sems.back_send.at[i, side]
+            yield stays, remote(
+                src, dst, sem, sems.back_recv.at[line, core], plan.device(coords, chip, target)
+            ), pltpu.make_async_copy(src, dst, sem)
+
+    def give(b):
+        rows = pl.ds(pl.multiple_of(lax.rem(b * KB, half), KB), KB)
+        part = b * KB // half
+        span = pl.ds(pl.multiple_of(b * KB, KB), KB)
+        i = lax.rem(b, own_blocks)
+        d_queries[part, rows, :] = (jnp.transpose(dq_acc[:, span]) * 0.125).astype(bf16)
+        term = mm_nt(d_queries[part, rows, :], weight(0, core))
+        term = term + mm_nt(d_keys[part, rows, :], weight(1, core))
+        term = term + mm_nt(d_values[part, rows, :], weight(2, core))
+        owner = b // own_blocks
+
+        @pl.when(core != owner)
+        def _():
+            spare[i] = term.astype(bf16).reshape(spare.shape[1:])
+            swap_copy(i).start()
+
+        @pl.when(core == owner)
+        def _():
+            own = term + acc[rows, :]
+            swap_copy(i).wait_recv()
+            low[rows, :] = (own + spare[own_blocks + i].reshape(KB, width).astype(f32)).astype(bf16)
+            for stays, far, near in grad_pieces(i):
+                pl.when(jnp.logical_not(stays))(far.start)
+                pl.when(stays)(near.start)
+
+    blocks = length // KB
+    near_blocks = -(-(REACH - 1) // KB)
+    turned = line < LINE // 2
+    given = 0
+    for o in range(blocks):
+        first, final = max(0, o - near_blocks), min(blocks - 1, o + near_blocks)
+        key_block(
+            jnp.where(turned, blocks - 1 - o, o), jnp.where(turned, blocks - 1 - final, first), final - first + 1
+        )
+        prefix_sum.go_on(o)
+        while given < blocks and min(blocks - 1, given + near_blocks) <= o:
+            give(jnp.where(turned, blocks - 1 - given, given))
+            given = given + 1
+    prefix_sum.finish(blocks)
+
+    lax.fori_loop(0, gather.count, lambda i, x: (gather.drain(i), x)[1], 0)
+    token_line.drain()
+    prefix_line.drain()
+    grad_line.drain()
     if not spread:
         pl.when(holds)(meta_copy.wait_send)
     for p in range(pairs):
         att_copy(p).wait_send()
     for b in range(parts):
         d_copy(b).wait_send()
-    for copy in keep:
-        copy.wait()
+    for i in range(own_blocks):
+        swap_copy(i).wait_send()
+        for stays, far, near in grad_pieces(i):
+            pl.when(jnp.logical_not(stays))(far.wait_send)
+            pl.when(stays)(near.wait)
+    out_back.settle()
+    arrivals = Line(plan, place, sems.back_send, sems.back_recv)
+    for j in range(held):
+        chip = j if spread else 2 * core + j
+        out_back.receive(refs.pieces.at[j], chip, line // 2)
+        arrivals.receive(refs.grad_pieces.at[j], chip, line // 2)
+    out_back.drain()
 
 
 def forward_backward(plan, given):
@@ -873,18 +976,15 @@
     pairs = WIDE // PAIR
     bf16, f32 = jnp.bfloat16, jnp.float32
     S = jax.ShapeDtypeStruct
+    tasks, slots, part = given.prefix_keys.shape
+    kept = -(-slots // 16) * 16
+    steps = len(plan.axes)
+    reach = max(plan.shape[a] for a in plan.axes) - 1
     outs = dict(
-        q_out=S((length, WIDE), bf16),
-        k_out=S((length, WIDE), bf16),
-        v_out=S((length, WIDE), bf16),
-        att_out=S((length, WIDE), bf16),
-        lse_out=S((pairs, 8, length), f32),
-        pre_out=S((2, SLOTS, WIDE), bf16),
-        meta_out=S((8, SLOTS + length), f32),
-        d_att_out=S((length, WIDE), bf16),
-        d_first_out=S((half, width), f32),
-        w_out=S((3,) + plan.shape + (depth, WIDE), bf16),
-        out_out=S((half, width), bf16),
+        pieces=S((held, places, width), bf16),
+        grad_pieces=S((held, places, width), bf16),
+        keys_grad=S((tasks, slots, part), f32),
+        values_grad=S((tasks, slots, part), f32),
     )
     scratch = dict(
         source=((KINDS, plan.sides, depth, LANES), bf16),
@@ -913,6 +1013,13 @@
         out=((half, width), bf16),
         d_att=((length, WIDE), bf16),
         d_att_away=((half, WIDE), bf16),
+        d_pre=((2, SLOTS, WIDE), f32),
+        terms=((LINE, 2, SLOTS, LANES), bf16),
+        row_terms=((LINE, 2, SLOTS, LANES), bf16),
+        total=((tasks, 2, kept, LANES), f32),
+        total_other=((tasks, 2, kept, LANES), f32),
+        gone=((steps, tasks, 2, kept, LANES), bf16),
+        come=((steps, reach, tasks, 2, kept, LANES), bf16),
     )
     sems = gather_semaphores(plan)
     sems.update(
@@ -928,7 +1035,18 @@
         att_recv=semaphores(pairs),
         d_send=semaphores(half // CHUNK),
         d_recv=semaphores(half // CHUNK),
-        publish=semaphores(11),
+        out_send=semaphores(4),
+        out_recv=semaphores(LINE, 2),
+        back_send=semaphores(half // KB, 2),
+        back_recv=semaphores(LINE, 2),
+        swap_send=semaphores(half // KB),
+        swap_recv=semaphores(half // KB),
+        terms_send=semaphores(LINE),
+        terms_recv=semaphores(LINE, 2),
+        total_send=semaphores(1),
+        total_recv=semaphores(1),
+        sum_send=semaphores(steps, reach),
+        sum_recv=semaphores(steps, reach),
     )
     smem = pl.BlockSpec(memory_space=pltpu.SMEM)
     vmem = pl.BlockSpec(memory_space=pltpu.VMEM)
@@ -937,204 +1055,13 @@
         functools.partial(forward_backward_kernel, plan, (*vars(given), *outs, *scratch, *sems)),
         out_shape=list(outs.values()),
         in_specs=[smem, smem, smem, vmem, hbm, hbm] + [vmem] * 12,
-        out_specs=[hbm] * len(outs),
+        out_specs=[hbm, hbm, vmem, vmem],
         scratch_shapes=[pltpu.VMEM(*spec) for spec in scratch.values()] + list(sems.values()),
         compiler_params=pltpu.CompilerParams(
-            collective_id=0, has_side_effects=True, vmem_limit_bytes=62 * 2**20
+            collective_id=0, has_side_effects=True, vmem_limit_bytes=63 * 2**20
         ),
     )(*vars(given).values())
     return SimpleNamespace(**dict(zip(outs, results)))
-
-
-def finish_kernel(plan, names, *args):
-    refs = SimpleNamespace(**dict(zip(names, args)))
-    place = plan.here()
-    coords, line, core = place
-    bf16, f32 = jnp.bfloat16, jnp.float32
-    spread = plan.core_in_tp
-    width = refs.d_first.shape[1]
-    half = refs.d_first.shape[0]
-    held, places = refs.pieces.shape[:2]
-    tasks, slots = refs.keys_grad.shape[:2]
-    parts = half // CHUNK
-    kept = refs.total.shape[2]
-
-    for chip in range(LINE):
-        lanes = slice(chip * LANES, (chip + 1) * LANES)
-        for which in range(2):
-            refs.terms[chip, which] = refs.d_pre[which, :, lanes].astype(bf16)
-        refs.terms[chip, 0, SLOTS - 16 :, :] = jnp.broadcast_to(refs.meta[1:2, 0:SLOTS], (16, SLOTS)).astype(bf16)
-    greet(plan, place)
-    terms = Line(plan, place, refs.terms_send, refs.terms_recv)
-    for chip in range(LINE):
-        terms.send(refs.terms.at[chip], refs.row_terms.at[line], chip, core)
-
-    swap = Sibling(plan, place, refs.swap_send, refs.swap_recv)
-    back = Line(plan, place, refs.back_send, refs.back_recv)
-
-    def share(which, b):
-        rows = pl.ds(pl.multiple_of(which * half + b * CHUNK, CHUNK), CHUNK)
-        total = mm_nt(refs.dq[rows, :], refs.w[0].reshape(width, WIDE))
-        total = total + mm_nt(refs.dk[rows, :], refs.w[1].reshape(width, WIDE))
-        return total + mm_nt(refs.dv[rows, :], refs.w[2].reshape(width, WIDE))
-
-    def swap_copy(b):
-        rows = pl.ds(b * CHUNK, CHUNK)
-        return swap.copy(refs.away.at[rows], refs.other.at[rows], b)
-
-    for b in range(parts):
-        rows = pl.ds(b * CHUNK, CHUNK)
-        refs.away[rows, :] = share(1 - core, b).astype(bf16)
-        swap_copy(b).start()
-        own = share(core, b) + refs.d_first[rows, :]
-        swap_copy(b).wait_recv()
-        refs.sums[rows, :] = (own + refs.other[rows, :].astype(f32)).astype(bf16)
-        for side in range(plan.cores):
-            spot, target = (line, side) if spread else (lax.rem(line, 2), line // 2)
-            back.send(
-                refs.sums.at[pl.ds(b * CHUNK + side * places, places)], refs.pieces.at[spot], 2 * core + b, target
-            )
-
-    terms.settle()
-    total = refs.total
-    total[...] = jnp.zeros_like(total)
-    for chip in range(LINE):
-        terms.receive(refs.row_terms.at[chip], chip, core)
-        marks = refs.row_terms[chip, 0, SLOTS - 16 :, :].astype(f32)
-        for task in range(tasks):
-            for which in range(2):
-                total[task, which] += refs.row_terms[chip, which, 0:kept, :].astype(f32) * marks[0:1, task : task + 1]
-    for step, axis in enumerate(plan.axes):
-        size = plan.shape[axis]
-        refs.gone[step] = total[...].astype(bf16)
-        copies = [
-            remote(
-                refs.gone.at[step], refs.come.at[step, by - 1], refs.axis_send.at[step, by - 1],
-                refs.axis_recv.at[step, by - 1],
-                plan.device(shifted(coords, axis, by, size), line, core),
-            )
-            for by in range(1, size)
-        ]
-        for copy in copies:
-            copy.start()
-        for by, copy in enumerate(copies):
-            copy.wait_recv()
-            total[...] += refs.come[step, by].astype(f32)
-        for copy in copies:
-            copy.wait_send()
-
-    def put(block, lanes):
-        for task in range(tasks):
-            refs.keys_grad[task, :, lanes] = block[task, 0, 0:slots, :]
-            refs.values_grad[task, :, lanes] = block[task, 1, 0:slots, :]
-
-    if spread:
-        put(total, slice(None))
-    else:
-        last = swap.copy(total, refs.total_other, parts)
-        last.start()
-
-        @pl.when(core == 0)
-        def _():
-            put(total, slice(0, LANES))
-
-        @pl.when(core == 1)
-        def _():
-            put(total, slice(LANES, 2 * LANES))
-
-        last.wait_recv()
-
-        @pl.when(core == 0)
-        def _():
-            put(refs.total_other, slice(LANES, 2 * LANES))
-
-        @pl.when(core == 1)
-        def _():
-            put(refs.total_other, slice(0, LANES))
-
-        last.wait_send()
-
-    back.settle()
-    for j in range(held):
-        back.receive(refs.pieces.at[j], j if spread else 2 * core + j, line // 2)
-    back.drain()
-    terms.drain()
-    for b in range(parts):
-        swap_copy(b).wait_send()
-
-
-def finish(plan, held, places, tasks, slots, part, given):
-    half, width = given.d_first.shape
-    steps = len(plan.axes)
-    reach = max(plan.shape[a] for a in plan.axes) - 1
-    kept = -(-slots // 16) * 16
-    bf16, f32 = jnp.bfloat16, jnp.float32
-    outs = dict(
-        pieces=jax.ShapeDtypeStruct((held, places, width), bf16),
-        keys_grad=jax.ShapeDtypeStruct((tasks, slots, part), f32),
-        values_grad=jax.ShapeDtypeStruct((tasks, slots, part), f32),
-    )
-    scratch = dict(
-        terms=((LINE, 2, SLOTS, LANES), bf16),
-        row_terms=((LINE, 2, SLOTS, LANES), bf16),
-        away=((half, width), bf16),
-        other=((half, width), bf16),
-        sums=((half, width), bf16),
-        total=((tasks, 2, kept, LANES), f32),
-        total_other=((tasks, 2, kept, LANES), f32),
-        gone=((steps, tasks, 2, kept, LANES), bf16),
-        come=((steps, reach, tasks, 2, kept, LANES), bf16),
-    )
-    sems = dict(
-        terms_send=semaphores(LINE),
-        terms_recv=semaphores(LINE, 2),
-        swap_send=semaphores(half // CHUNK + 1),
-        swap_recv=semaphores(half // CHUNK + 1),
-        back_send=semaphores(4),
-        back_recv=semaphores(LINE, 2),
-        axis_send=semaphores(steps, reach),
-        axis_recv=semaphores(steps, reach),
-    )
-    vmem = pl.BlockSpec(memory_space=pltpu.VMEM)
-    results = pl.pallas_call(
-        functools.partial(finish_kernel, plan, (*vars(given), *outs, *scratch, *sems)),
-        out_shape=list(outs.values()),
-        in_specs=[vmem] * len(vars(given)),
-        out_specs=[pl.BlockSpec(memory_space=pl.ANY), vmem, vmem],
-        scratch_shapes=[pltpu.VMEM(*spec) for spec in scratch.values()] + list(sems.values()),
-        compiler_params=pltpu.CompilerParams(
-            collective_id=1, has_side_effects=True, vmem_limit_bytes=48 * 2**20
-        ),
-    )(*vars(given).values())
-    return results
-
-
-def hand_out(plan, part, held, places):
-    _, line, core = plan.here()
-    count = 2 * plan.cores
-    piece = lax.rem(line, 2) * plan.cores + (core if plan.core_in_tp else 0)
-    pieces = part.reshape(count, places, -1)
-    a, b, c = plan.shape
-    got = []
-    for k in range(count):
-        pairs = []
-        for place in itertools.product(range(a), range(b), range(c), range(LINE), range(2)):
-            coords, chip, side = place[:3], place[3], place[4]
-            if not plan.core_in_tp and coords[2] != side:
-                continue
-            which = (chip % count) ^ k
-            target = which % 2 if plan.core_in_tp else chip // 2
-            ends = plan.device(coords, chip, side), plan.device(coords, 2 * side + which // plan.cores, target)
-            pairs.append(tuple(r * plan.tp + t for r, t in ends))
-        mine = lax.dynamic_index_in_dim(pieces, lax.rem(line, count) ^ k, 0, keepdims=False)
-        got.append(lax.ppermute(mine, ("rows", "tp"), pairs))
-    slots = []
-    for j in range(held):
-        slot = got[0]
-        for k in range(1, count):
-            slot = jnp.where(piece ^ j == k, got[k], slot)
-        slots.append(slot)
-    return jnp.stack(slots)
 
 
 def shards(
@@ -1142,7 +1069,6 @@
     second_gain, second_shift, prefix_keys, prefix_values, example_lengths, task_ids, prefix_lens,
     slot_masks, out_grad,
 ):
-    held, places, _ = tokens.shape
     done = forward_backward(
         plan,
         SimpleNamespace(
@@ -1166,18 +1092,7 @@
             prefix_values=prefix_values,
         ),
     )
-    output = hand_out(plan, done.out_out, held, places)
-    dq, dk, dv, d_pre = attend_backward(
-        example_lengths.shape[1], done.q_out, done.k_out, done.v_out, done.d_att_out, done.att_out,
-        done.pre_out, done.lse_out, done.meta_out,
-    )
-    d_tokens, keys_grad, values_grad = finish(
-        plan, held, places, *prefix_keys.shape,
-        SimpleNamespace(
-            dq=dq, dk=dk, dv=dv, w=done.w_out, d_first=done.d_first_out, d_pre=d_pre, meta=done.meta_out
-        ),
-    )
-    return output, d_tokens.astype(jnp.float32), keys_grad, values_grad
+    return done.pieces, done.grad_pieces.astype(jnp.float32), done.keys_grad, done.values_grad
 
 
 def solution(mesh):

time: 264 us -> 226 us (0.86)
  the two profiles are of different devices: /device:TPU:9 before, /device:TPU:0 now
where the time goes in v5:
time: 226 us; the launch traced here: 225 us
  Pallas kernels  215 us (95%)
  local copies, waits for them, and re-layouts  8.26 us (4%)
    pallas_call x1, Pallas kernels, forward_backward(): pl.pallas_call(functools.partial(forward_backward_kernel, plan, (*vars(gi...  215 us
    unnamed x9, local copies, waits for them, and re-layouts  8.26 us

profile of v5, /device:TPU:0, one launch (start us, length us, event | category | flops | bytes accessed | tf_op | source)
XLA Modules:
  0.0 225.4 jit_solution(2980609906977509592)
XLA Ops:
  0.6 1.6 copy.22.args_16_
  2.3 1.6 copy.23.args_17_
  3.9 215.0 %shard_map.201 = (bf16[2,256,1024]{2,1,0:T(8,128)(2,1)}, bf16[2,256,1024]{2,1,0:T(8,128)(2,1)}, f32[4,100,256]{2,1,0:T(8,128)}, f32[4,100,256]{2,1,0:T(8,128)}) custom-call(s32[2]{0:T(128)} %args_0_.4, s32[2,8]{1,0:T(2,128)} %args_1_.4, s32[4]{0:T(128)} %args_2_.4, s32[4,100]{1,0:T(4,128)} %args_3_.4, bf16[2,256,1024]{2,1,0:T(8,128)(2,1)} %args_4_.4, ...), custom_call_target="tpu_custom_call" | custom-call | tf_op jit(solution)/shard_map/pallas_call | solution.py:1054
  218.9 0.0 copy-start
  218.9 2.0 copy.24
  220.9 0.0 copy-start.1
  220.9 2.0 copy.25
  222.9 0.0 copy-done
  222.9 1.6 convert_element_type.3
  224.5 0.0 copy-done.1
  224.5 1.0 copy.27
Async XLA Ops:
  218.9 4.0 %copy-start = (bf16[2,256,1024]{2,1,0:T(8,128)(2,1)S(1)}, bf16[2,256,1024]{2,1,0:T(8,128)(2,1)}, u32[]{:S(2)}) copy-start(bf16[2,256,1024]{2,1,0:T(8,128)(2,1)} %get-tuple-element.9) | copy-start | bytes 3145732
  220.9 3.6 %copy-start.1 = (bf16[2,256,1024]{2,1,0:T(8,128)(2,1)S(1)}, bf16[2,256,1024]{2,1,0:T(8,128)(2,1)}, u32[]{:S(2)}) copy-start(bf16[2,256,1024]{2,1,0:T(8,128)(2,1)} %get-tuple-element.20) | copy-start | bytes 3145732

commit v6 on v5

--- a/solution.py
+++ b/solution.py
@@ -16,6 +16,7 @@
 KB = 256
 REACH = 512
 NEG = -1e30
+MARKS = 16
 NT = (((1,), (1,)), ((), ()))
 
 
@@ -36,27 +37,43 @@
     return jnp.where(head_lanes(half), a, jnp.zeros_like(a))
 
 
-def attend_block(q, keys, values, seg_col, seg_row, live_row):
-    mixed = jnp.zeros((q.shape[0], PAIR), jnp.float32)
-    totals = jnp.zeros((q.shape[0], PAIR), jnp.float32)
-    lane = lax.broadcasted_iota(jnp.int32, (1, PAIR), 1)
+def key_marks(meta):
+    length = meta.shape[1]
+    row = lax.broadcasted_iota(jnp.int32, (PAIR, length), 0)
+    place = lax.broadcasted_iota(jnp.int32, (PAIR, length), 1)
+    seg = meta[0:1, :]
+    other = (place >= SLOTS) & (row < 8) & (row.astype(jnp.float32) != seg)
+    dead = (place < SLOTS) & (row == 8) & (seg < 0.5)
+    ones = (row >= 9) & (row < 12)
+    marks = jnp.where(other | dead, NEG, jnp.where(ones, 1.0, 0.0))
+    return jnp.transpose(marks).astype(jnp.bfloat16)
+
+
+def query_marks(meta):
+    length = meta.shape[1] - SLOTS
+    row = lax.broadcasted_iota(jnp.int32, (MARKS, length), 0)
+    seg = meta[0:1, SLOTS:]
+    return jnp.where(((row < 8) & (row.astype(jnp.float32) == seg)) | (row == 8), 1.0, 0.0)
+
+
+def attend_tile(q_t, marks, keys, values):
+    scaled = q_t * jnp.asarray(0.125, jnp.bfloat16)
+    blank = jnp.zeros((PAIR - MARKS, marks.shape[1]), jnp.bfloat16)
+    low_marks = jnp.concatenate([marks.astype(jnp.bfloat16), blank], axis=0)
+    mixed, totals = [], []
+    zero = jnp.zeros((HD, q_t.shape[1]), jnp.bfloat16)
+    ones = jnp.ones((16, keys.shape[0]), jnp.bfloat16)
     for half in range(2):
-        qh = only_head(q, half) * jnp.asarray(0.125, jnp.bfloat16)
-        scores = mm_nt(qh, keys)
-        seq = jnp.where(seg_col == seg_row, scores[:, SLOTS:], NEG)
-        pre = jnp.where(live_row > 0.5, scores[:, :SLOTS], NEG)
-        top = jnp.maximum(
-            jnp.max(seq, axis=1, keepdims=True), jnp.max(pre, axis=1, keepdims=True)
-        )
-        seq = jnp.exp(seq - top)
-        pre = jnp.exp(pre - top)
-        total = jnp.sum(seq, axis=1, keepdims=True) + jnp.sum(pre, axis=1, keepdims=True)
-        scale = 1.0 / total
-        low = jnp.concatenate([(pre * scale).astype(jnp.bfloat16), (seq * scale).astype(jnp.bfloat16)], axis=1)
-        out = mm(low, values)
-        mixed = jnp.where(head_lanes(half), out, mixed)
-        totals = jnp.where(lane == half, top + jnp.log(total), totals)
-    return mixed.astype(jnp.bfloat16), totals
+        rows = slice(half * HD, (half + 1) * HD)
+        own = [scaled[rows, :], zero] if half == 0 else [zero, scaled[rows, :]]
+        scores = mm(keys, jnp.concatenate([*own, low_marks], axis=0))
+        top = jnp.max(scores, axis=0, keepdims=True)
+        probs = jnp.exp(scores - top).astype(jnp.bfloat16)
+        out = mm(jnp.concatenate([values[rows, :], ones], axis=0), probs)
+        total = out[HD : HD + 1, :]
+        mixed.append(out[:HD, :] * (1.0 / total))
+        totals.append(top + jnp.log(total))
+    return jnp.concatenate(mixed, axis=0), totals
 
 
 def inner_rows(do, att):
@@ -561,7 +578,11 @@
 LAG = 2
 CUTS = 8
 TOKENS = 4
-ATT_BEATS = 2
+ATT_BEATS = 1
+QKV_BEATS = 3
+MIX_BEATS = 2
+ACT_BEATS = 1
+SPAN = 1024
 GRADS = 14
 
 
@@ -673,13 +694,14 @@
             return x
 
         lax.fori_loop(0, LINE, project, 0)
-        beat(done)
-        done = done + 1
+        if kind < QKV_BEATS:
+            beat(done)
+            done = done + 1
     att_share = Sibling(plan, place, sems.att_send, sems.att_recv)
     here = pl.ds(pl.multiple_of(core * half, half), half)
     there = pl.ds(pl.multiple_of((1 - core) * half, half), half)
-    keys, values = refs.keys, refs.values
-    blocks = length // QB
+    keys, values, queries = refs.keys, refs.values, refs.queries
+    keys[:, PAIR:] = key_marks(meta)
 
     def pair_lanes(p):
         return pl.ds(pl.multiple_of(p * PAIR, PAIR), PAIR)
@@ -689,26 +711,20 @@
         return att_share.copy(att.at[there, lanes], refs.att_other.at[:, lanes], p)
 
     def pair(p, x):
-        lanes = pl.ds(pl.multiple_of(p * PAIR, PAIR), PAIR)
-        keys[0:SLOTS, :] = pre[0, :, lanes]
-        keys[SLOTS:, :] = k[:, lanes]
-        values[0:SLOTS, :] = pre[1, :, lanes]
-        values[SLOTS:, :] = v[:, lanes]
-
-        def block(b, x):
-            rows = pl.ds(pl.multiple_of(b * QB, QB), QB)
-            mixed, totals = attend_block(
-                q[rows, lanes], keys[...], values[...],
-                refs.meta_cols[pl.ds(pl.multiple_of(SLOTS + b * QB, SLOTS), QB), 0:1],
-                meta[0:1, SLOTS:], meta[0:1, :SLOTS],
-            )
-            att[rows, lanes] = mixed
-            lse[p, :, rows] = jnp.transpose(totals)[0:8, :]
-            return x
-
-        lax.fori_loop(0, blocks // 2, block, 0)
-        beat(done + ATT_BEATS * p)
-        lax.fori_loop(blocks // 2, blocks, block, 0)
+        lanes = pair_lanes(p)
+        queries[...] = jnp.transpose(q[:, lanes])
+        keys[0:SLOTS, 0:PAIR] = pre[0, :, lanes]
+        keys[SLOTS:, 0:PAIR] = k[:, lanes]
+        values[:, 0:SLOTS] = jnp.transpose(pre[1, :, lanes])
+        values[:, SLOTS:] = jnp.transpose(v[:, lanes])
+        if ATT_BEATS > 0:
+            beat(done + ATT_BEATS * p)
+        for first in range(0, length, SPAN):
+            rows = slice(first, first + SPAN)
+            mixed, totals = attend_tile(queries[:, rows], query_marks(meta)[:, rows], keys[...], values[...])
+            att[rows, lanes] = jnp.transpose(mixed).astype(bf16)
+            lse[p, 0:1, rows] = totals[0]
+            lse[p, 1:2, rows] = totals[1]
         if ATT_BEATS > 1:
             beat(done + ATT_BEATS * p + 1)
         att_copy(p).start()
@@ -722,13 +738,13 @@
 
     done = ready(3 * plan.sides, plan.sides, done)
     normal_one, rstd_one, normed, acc = refs.normal_one, refs.rstd_one, refs.normed, refs.acc
-    low, slope, out = refs.low, refs.slope, refs.out
+    low, slope, out = refs.normed, refs.slope, refs.out
     parts = half // CHUNK
 
     def weight(kind, side):
         return whole[kind, side].reshape(width, WIDE)
 
-    def mix(b, x):
+    def mix(b):
         rows = pl.ds(pl.multiple_of(b * CHUNK, CHUNK), CHUNK)
         own = att[pl.ds(pl.multiple_of(core * half + b * CHUNK, CHUNK), CHUNK), :]
         total = row[2 * core + b].reshape(CHUNK, width).astype(f32)
@@ -739,11 +755,12 @@
         low_normed = (normal * refs.gain_one[...] + refs.shift_one[...]).astype(bf16)
         normed[rows, :] = low_normed
         acc[rows, :] = low_normed.astype(f32)
-        beat(done + b)
-        return x
-
-    lax.fori_loop(0, parts, mix, 0)
-    done = done + parts
+        if b < MIX_BEATS:
+            beat(done + b)
+
+    for b in range(parts):
+        mix(b)
+    done = done + min(parts, MIX_BEATS)
 
     acted = refs.acted
     chunks = [slice(b * CHUNK, (b + 1) * CHUNK) for b in range(parts)]
@@ -757,25 +774,23 @@
                 slope[2 * j + side, rows, :] = (
                     bell + upper * jnp.exp(upper * upper * -0.5) * (1.0 / (2.0 * math.pi) ** 0.5)
                 ).astype(bf16)
-            if done < last:
+            if ACT_BEATS > 0:
                 beat(done + side)
             return x
 
         lax.fori_loop(0, 2, unit, 0)
 
     def add(j, done):
-        def unit(side, x):
-            for rows in chunks:
-                acc[rows, :] += mm_nt(acted[2 * j + side, rows, :], weight(down_kind(j), side))
-            return x
-
-        lax.fori_loop(0, 2, unit, 0)
+        for rows in chunks:
+            acc[rows, :] += mm_nt(acted[2 * j, rows, :], weight(down_kind(j), 0)) + mm_nt(
+                acted[2 * j + 1, rows, :], weight(down_kind(j), 1)
+            )
 
     steps_of = sorted([(up_kind(j), act, j) for j in range(GROUPS)] + [(down_kind(j), add, j) for j in range(GROUPS)], key=lambda s: s[0])
     for kind, body, j in steps_of:
         done = ready(kind * plan.sides, plan.sides, done)
         body(j, done)
-        done = done + 2 if body is act else done
+        done = done + 2 if body is act and ACT_BEATS > 0 else done
 
     grad_line.settle()
     for part in range(2):
@@ -804,15 +819,15 @@
                 2 * core + b, target,
             )
 
-    def feed_back(n, x):
-        j, side = n // 2, lax.rem(n, 2)
-        for rows in chunks:
-            d_acted = mm(low[rows, :], weight(down_kind(j), side))
-            d_upper = (d_acted * slope[n, rows, :].astype(f32)).astype(bf16)
-            acc[rows, :] += mm_nt(d_upper, weight(up_kind(j), side))
+    def feed_back(j, x):
+        d_upper = [
+            (mm(low[...], weight(down_kind(j), side)) * slope[2 * j + side].astype(f32)).astype(bf16)
+            for side in range(2)
+        ]
+        acc[...] += mm_nt(d_upper[0], weight(up_kind(j), 0)) + mm_nt(d_upper[1], weight(up_kind(j), 1))
         return x
 
-    lax.fori_loop(0, 2 * GROUPS, feed_back, 0)
+    lax.fori_loop(0, GROUPS, feed_back, 0)
 
     d_att, away = refs.d_att, refs.d_att_away
     d_share = Sibling(plan, place, sems.d_send, sems.d_recv)
@@ -1000,8 +1015,9 @@
         att=((length, WIDE), bf16),
         lse=((pairs, 8, length), f32),
         att_other=((half, WIDE), bf16),
-        keys=((SLOTS + length, PAIR), bf16),
-        values=((SLOTS + length, PAIR), bf16),
+        keys=((SLOTS + length, 2 * PAIR), bf16),
+        values=((PAIR, SLOTS + length), bf16),
+        queries=((PAIR, length), bf16),
         meta_cols=((SLOTS + length, 8), f32),
         normal_one=((half, width), f32),
         rstd_one=((half, LANES), f32),
@@ -1009,7 +1025,6 @@
         slope=((2 * GROUPS, half, WIDE), bf16),
         acted=((2 * GROUPS, half, WIDE), bf16),
         acc=((half, width), f32),
-        low=((half, width), bf16),
         out=((half, width), bf16),
         d_att=((length, WIDE), bf16),
         d_att_away=((half, WIDE), bf16),

time: 226 us -> 219 us (0.969)
  Pallas kernels: 215 us -> 208 us
    pallas_call x1, Pallas kernels: 215 us -> 208 us  [forward_backward(): pl.pallas_call(functools.partial(forward_backward_kernel, plan, (*vars(gi...]
where the time goes in v6:
time: 219 us; the launch traced here: 218 us
  Pallas kernels  208 us (95%)
  local copies, waits for them, and re-layouts  8.26 us (4%)
    pallas_call x1, Pallas kernels, forward_backward(): pl.pallas_call(functools.partial(forward_backward_kernel, plan, (*vars(gi...  208 us
    unnamed x9, local copies, waits for them, and re-layouts  8.26 us

profile of v6, /device:TPU:0, one launch (start us, length us, event | category | flops | bytes accessed | tf_op | source)
XLA Modules:
  0.0 218.1 jit_solution(3218625940400919451)
XLA Ops:
  0.6 1.6 copy.22.args_16_
  2.3 1.6 copy.23.args_17_
  3.9 207.6 %shard_map.201 = (bf16[2,256,1024]{2,1,0:T(8,128)(2,1)}, bf16[2,256,1024]{2,1,0:T(8,128)(2,1)}, f32[4,100,256]{2,1,0:T(8,128)}, f32[4,100,256]{2,1,0:T(8,128)}) custom-call(s32[2]{0:T(128)} %args_0_.4, s32[2,8]{1,0:T(2,128)} %args_1_.4, s32[4]{0:T(128)} %args_2_.4, s32[4,100]{1,0:T(4,128)} %args_3_.4, bf16[2,256,1024]{2,1,0:T(8,128)(2,1)} %args_4_.4, ...), custom_call_target="tpu_custom_call" | custom-call | tf_op jit(solution)/shard_map/pallas_call | solution.py:1069
  211.5 0.0 copy-start
  211.6 2.0 copy.24
  213.6 0.0 copy-start.1
  213.6 2.0 copy.25
  215.6 0.0 copy-done
  215.6 1.6 convert_element_type.3
  217.1 0.0 copy-done.1
  217.1 1.0 copy.27
Async XLA Ops:
  211.5 4.0 %copy-start = (bf16[2,256,1024]{2,1,0:T(8,128)(2,1)S(1)}, bf16[2,256,1024]{2,1,0:T(8,128)(2,1)}, u32[]{:S(2)}) copy-start(bf16[2,256,1024]{2,1,0:T(8,128)(2,1)} %get-tuple-element.9) | copy-start | bytes 3145732
  213.6 3.6 %copy-start.1 = (bf16[2,256,1024]{2,1,0:T(8,128)(2,1)S(1)}, bf16[2,256,1024]{2,1,0:T(8,128)(2,1)}, u32[]{:S(2)}) copy-start(bf16[2,256,1024]{2,1,0:T(8,128)(2,1)} %get-tuple-element.20) | copy-start | bytes 3145732
